TPU v7x, 128 devices: a whole 4x4x4 slice. The times are simulated.
128 devices in a mesh: dom: 32 (over y, x, core), mode: 4 (over z).
Axes of the slice: x: 4, y: 4, z: 4, core: 2. Of those that a mesh axis runs over, the one named last changes fastest.
Arguments:
- mode_shapes: bfloat16 [128, 6, 32768], P('mode', None, 'dom'), may hold values from -0.29882812 to 0.29882812
- eigenvalues: float32 [128], replicated, may hold values from 0.7 to 192, as said below
- mode_weights: float32 [128], P('mode'), may hold values from 0.1 to 1
- stiff_deriv: bfloat16 [24, 24, 49152], P(None, None, 'dom'), as said below
- mass_ref: bfloat16 [24, 24], replicated, as said below
- mass_scale: float32 [49152], P('dom'), may hold values from 0.5 to 2
- connectivity: int32 [4, 49152], P(None, 'dom'), may hold values from 0 to 1087, as said below
- design_owner: int32 [49152], P('dom'), may hold values from 0 to 20479, as said below
- direction: float32 [20480], P('dom'), may hold values from -0.12 to 0.12
Outputs:
- hess_vec: float32 [20480], P('dom')
- eig_deriv: float32 [128], P('mode')
Inputs may be any that keep to these rules, and one draw needn't show every extreme that they name: Distinct eigenvalues, increasing with the mode index, neighbours at least 0.4 apart. `stiff_deriv`: symmetric 24 by 24 matrices with a positive diagonal. `mass_ref`: Symmetric, with a positive diagonal. `connectivity`: index into the extended node list of the element's device: the 32 upper rim nodes of the lower neighbour, the device's own 1024 nodes, then the 32 lower rim nodes of the upper neighbour. The corners of one element lie within 64 positions of one another. Elements of the first device never name the lower rim; those of the last never name the upper rim. `design_owner`: an element of index r of dom has its design variable in the blocks of 640 design variables of indices r - 1, r or r + 1 of dom.
All inputs are finite; a program needn't handle non-finite values.
Results may differ from a plain program's by a relative error of at most 0.01.
Values may be sent and summed in bfloat16 or wider, within the bound.
No kernel may reach another device: no remote copies, remote signals or barrier semaphores. Data moves between devices by JAX's collectives and lax.ppermute only.
A program may use at most 64 MiB of HBM per device.

v0:
```python
import jax
import jax.numpy as jnp
from jax import lax
from jax.sharding import PartitionSpec as P

EBLK = 256
H = 32


def with_halo(block, sides, width):
    for axis, dim in sides:
        count = lax.axis_size(axis)
        forward = [(i, i + 1) for i in range(count - 1)]
        backward = [(target, source) for source, target in forward]
        low = lax.ppermute(
            lax.slice_in_dim(block, block.shape[dim] - width, None, axis=dim), axis, forward
        )
        high = lax.ppermute(lax.slice_in_dim(block, 0, width, axis=dim), axis, backward)
        block = jnp.concatenate([low, block, high], axis=dim)
    return block


def shifted(value, axis, steps):
    count = lax.axis_size(axis)
    leading, last = (max(0, -steps), min(count, count - steps))
    return lax.ppermute(value, axis, [(source, source + steps) for source in range(leading, last)])


def element_dofs(field, element_nodes):
    picked = field[:, :, element_nodes]
    return picked.reshape(field.shape[0], 24, element_nodes.shape[1])


def on_device(
    mode_shapes,
    eigenvalues,
    mode_weights,
    stiff_deriv,
    mass_ref,
    mass_scale,
    connectivity,
    design_owner,
    direction,
):
    mode_dev = mode_shapes.shape[0]
    elem_dev = connectivity.shape[1]
    des_dev = direction.shape[0]
    mode_start = lax.axis_index("mode") * mode_dev
    dom_rank = lax.axis_index("dom")
    all_modes = lax.all_gather(mode_shapes, "mode", axis=0, tiled=True)
    extended = with_halo(all_modes, (("dom", 2),), H)
    ext_mine = lax.dynamic_slice_in_dim(extended, mode_start, mode_dev, 0)
    eig_mine = lax.dynamic_slice_in_dim(eigenvalues, mode_start, mode_dev, 0)
    dir_table = with_halo(direction, (("dom", 0),), des_dev)
    local_owner = design_owner - (dom_rank - 1) * des_dev
    table_len = 3 * des_dev
    elem_dir = dir_table[local_owner]
    elem_dirmass = elem_dir * mass_scale
    num_blocks = elem_dev // EBLK

    def gram_block(block, totals):
        start = block * EBLK
        element_nodes = lax.dynamic_slice_in_dim(connectivity, start, EBLK, 1)
        matrices = lax.dynamic_slice_in_dim(stiff_deriv, start, EBLK, 2)
        dir_block = lax.dynamic_slice_in_dim(elem_dir, start, EBLK, 0)
        dirmass_block = lax.dynamic_slice_in_dim(elem_dirmass, start, EBLK, 0)
        all_dofs = element_dofs(extended, element_nodes)
        mine_dofs = lax.dynamic_slice_in_dim(all_dofs, mode_start, mode_dev, 0)
        stiff_part = jnp.einsum(
            "abe,mbe->mae", matrices, mine_dofs, preferred_element_type=jnp.float32
        )
        force_k = (dir_block * stiff_part).astype(jnp.bfloat16)
        mass_shapes = jnp.einsum(
            "ab,mbe->mae", mass_ref, mine_dofs, preferred_element_type=jnp.float32
        )
        force_m = (dirmass_block * mass_shapes).astype(jnp.bfloat16)
        dims = (((1, 2), (1, 2)), ((), ()))
        stiff_gram = lax.dot_general(all_dofs, force_k, dims, preferred_element_type=jnp.float32)
        mass_gram = lax.dot_general(all_dofs, force_m, dims, preferred_element_type=jnp.float32)
        return (totals[0] + stiff_gram, totals[1] + mass_gram)

    empty = jnp.zeros((extended.shape[0], mode_dev), jnp.float32)
    stiff_gram, mass_gram = lax.fori_loop(0, num_blocks, gram_block, (empty, empty))
    stiff_gram, mass_gram = lax.psum((stiff_gram, mass_gram), "dom")
    resid = stiff_gram - eig_mine[None, :] * mass_gram
    mass_diag = jnp.diagonal(lax.dynamic_slice_in_dim(mass_gram, mode_start, mode_dev, 0))
    eig_deriv = jnp.diagonal(lax.dynamic_slice_in_dim(resid, mode_start, mode_dev, 0))
    row_index = jnp.arange(extended.shape[0], dtype=jnp.int32)[:, None]
    col_index = mode_start + jnp.arange(mode_dev, dtype=jnp.int32)[None, :]
    diagonal_mask = row_index == col_index
    spacing = eig_mine[None, :] - eigenvalues[:, None]
    combiner = jnp.where(
        diagonal_mask, -0.5 * mass_diag[None, :], resid / jnp.where(diagonal_mask, 1.0, spacing)
    ).astype(jnp.bfloat16)
    deriv_ext = jnp.einsum(
        "ji,jcn->icn", combiner, extended, preferred_element_type=jnp.float32
    ).astype(jnp.bfloat16)

    def energy_block(block, energy):
        start = block * EBLK
        element_nodes = lax.dynamic_slice_in_dim(connectivity, start, EBLK, 1)
        matrices = lax.dynamic_slice_in_dim(stiff_deriv, start, EBLK, 2)
        mass_block = lax.dynamic_slice_in_dim(mass_scale, start, EBLK, 0)
        shapes = element_dofs(ext_mine, element_nodes)
        deriv_dofs = element_dofs(deriv_ext, element_nodes)
        stiff_q = jnp.einsum(
            "abe,mbe->mae", matrices, deriv_dofs, preferred_element_type=jnp.float32
        )
        mass_q = jnp.einsum("ab,mbe->mae", mass_ref, deriv_dofs, preferred_element_type=jnp.float32)
        mass_shapes = jnp.einsum(
            "ab,mbe->mae", mass_ref, shapes, preferred_element_type=jnp.float32
        )
        term_k = jnp.sum(shapes * stiff_q, axis=1)
        term_m = jnp.sum(shapes * mass_q, axis=1)
        term_p = jnp.sum(shapes * mass_shapes, axis=1)
        inner = 2.0 * term_k - mass_block[None, :] * (
            2.0 * eig_mine[:, None] * term_m + eig_deriv[:, None] * term_p
        )
        values = jnp.sum(mode_weights[:, None] * inner, axis=0)
        return lax.dynamic_update_slice_in_dim(energy, values, start, 0)

    energy = lax.fori_loop(0, num_blocks, energy_block, jnp.zeros((elem_dev,), jnp.float32))
    local_sums = jax.ops.segment_sum(energy, local_owner, num_segments=table_len)
    from_upper = shifted(local_sums[:des_dev], "dom", -1)
    from_lower = shifted(local_sums[2 * des_dev :], "dom", 1)
    owned = local_sums[des_dev : 2 * des_dev] + from_upper + from_lower
    hess_vec = lax.psum(owned, "mode")
    return (hess_vec, eig_deriv)


def solution(mesh):
    return jax.shard_map(
        on_device,
        mesh=mesh,
        in_specs=(
            P("mode", None, "dom"),
            P(),
            P("mode"),
            P(None, None, "dom"),
            P(),
            P("dom"),
            P(None, "dom"),
            P("dom"),
            P("dom"),
        ),
        out_specs=(P("dom"), P("mode")),
        check_vma=False,
    )
```

profile of v0, /device:TPU:2, one launch (start us, length us, event | category | flops | bytes accessed | tf_op | source)
XLA Modules:
  0.0 602.0 jit_solution(8886556330250387583)
XLA Ops:
  13.5 10.5 %copy.100 = bf16[24,24,1536]{1,0,2:T(8,128)(2,1)} copy(bf16[24,24,1536]{2,1,0:T(8,128)(2,1)} %param.16) | data formatting | bytes 3538944
  25.8 13.0 %all-gather.2.cloned.1.call-done = bf16[128,6,1024]{2,0,1:T(8,128)(2,1)} async-done(((bf16[32,6,1024]{2,0,1:T(8,128)(2,1)}), bf16[128,6,1024]{2,0,1:T(8,128)(2,1)}) %all-gather.2.cloned.1.call-update) | async-done | bytes 1572880 | tf_op jit(solution)/shard_map/all_gather | solution.py:50
  46.4 11.8 %gather_fusion.3 = f32[1536]{0:T(1024)} fusion(f32[1920]{0:T(1024)S(1)} %pad_maximum_fusion.1, s32[2048]{0:T(1024)S(1)} %pad_clamp_fusion), kind=kCustom, calls=%fused_computation.3 | custom fusion | bytes 18432 | tf_op jit(solution)/shard_map/gather | solution.py:57
  60.6 7.4 %copy.99 = bf16[128,6,1088]{0,1,2:T(8,128)(2,1)} copy(bf16[128,6,1088]{0,2,1:T(8,128)(2,1)S(1)} %pad_maximum_fusion) | data formatting | bytes 3342336
  68.0 7.3 %copy.101 = bf16[32,6,1088]{0,1,2:T(8,128)(2,1)} copy(bf16[32,6,1088]{0,2,1:T(8,128)(2,1)S(1)} %constant_dynamic-slice_fusion.3) | data formatting | bytes 835584 | tf_op jit(solution)/shard_map/while | solution.py:122
  75.3 145.4 %while.32 = (s32[]{:T(128)}, f32[128,32]{0,1:T(8,128)}, f32[128,32]{0,1:T(8,128)}, s32[4,1536]{1,0:T(4,128)}, bf16[128,6,1088]{0,1,2:T(8,128)(2,1)}, /*index=5*/...) while((s32[]{:T(128)}, f32[128,32]{0,1:T(8,128)}, ...), condition=%wide.region_1.0_spmd.clone, body=%wide.region_0.0_spmd.clone.sunk | while | flops 120344584 | bytes 15175058 | solution.py:83
  77.5 9.3 %gather_fusion.2 = bf16[1024,128,6]{1,2,0:T(8,128)(2,1)} fusion(bf16[128,6,1088]{0,1,2:T(8,128)(2,1)} %get-tuple-element.781, s32[1024]{0:T(1024)S(1)} %broadcast_clamp_fusion.5), kind=kCustom, calls=%fused_computation.clone.clone.1 | custom fusion | bytes 3149824 | tf_op jit(solution)/shard_map/while/body/eval_jaxpr/gather | solution.py:30
  101.8 9.3 %gather_fusion.2 = bf16[1024,128,6]{1,2,0:T(8,128)(2,1)} fusion(bf16[128,6,1088]{0,1,2:T(8,128)(2,1)} %get-tuple-element.781, s32[1024]{0:T(1024)S(1)} %broadcast_clamp_fusion.5), kind=kCustom, calls=%fused_computation.clone.clone.1 | custom fusion | bytes 3149824 | tf_op jit(solution)/shard_map/while/body/eval_jaxpr/gather | solution.py:30
  126.0 9.3 %gather_fusion.2 = bf16[1024,128,6]{1,2,0:T(8,128)(2,1)} fusion(bf16[128,6,1088]{0,1,2:T(8,128)(2,1)} %get-tuple-element.781, s32[1024]{0:T(1024)S(1)} %broadcast_clamp_fusion.5), kind=kCustom, calls=%fused_computation.clone.clone.1 | custom fusion | bytes 3149824 | tf_op jit(solution)/shard_map/while/body/eval_jaxpr/gather | solution.py:30
  150.2 9.3 %gather_fusion.2 = bf16[1024,128,6]{1,2,0:T(8,128)(2,1)} fusion(bf16[128,6,1088]{0,1,2:T(8,128)(2,1)} %get-tuple-element.781, s32[1024]{0:T(1024)S(1)} %broadcast_clamp_fusion.5), kind=kCustom, calls=%fused_computation.clone.clone.1 | custom fusion | bytes 3149824 | tf_op jit(solution)/shard_map/while/body/eval_jaxpr/gather | solution.py:30
  174.5 9.3 %gather_fusion.2 = bf16[1024,128,6]{1,2,0:T(8,128)(2,1)} fusion(bf16[128,6,1088]{0,1,2:T(8,128)(2,1)} %get-tuple-element.781, s32[1024]{0:T(1024)S(1)} %broadcast_clamp_fusion.5), kind=kCustom, calls=%fused_computation.clone.clone.1 | custom fusion | bytes 3149824 | tf_op jit(solution)/shard_map/while/body/eval_jaxpr/gather | solution.py:30
  198.7 9.3 %gather_fusion.2 = bf16[1024,128,6]{1,2,0:T(8,128)(2,1)} fusion(bf16[128,6,1088]{0,1,2:T(8,128)(2,1)} %get-tuple-element.781, s32[1024]{0:T(1024)S(1)} %broadcast_clamp_fusion.5), kind=kCustom, calls=%fused_computation.clone.clone.1 | custom fusion | bytes 3149824 | tf_op jit(solution)/shard_map/while/body/eval_jaxpr/gather | solution.py:30
  220.7 122.2 %all-reduce = (f32[128,32]{0,1:T(8,128)S(1)}, f32[128,32]{0,1:T(8,128)S(1)}) all-reduce(f32[128,32]{0,1:T(8,128)} %get-tuple-element.423, f32[128,32]{0,1:T(8,128)} %get-tuple-element.422), channel_id=1, replica_groups=mesh['dom'=32,'mode'=4] {'dom'}, use_global_device_ids=true, to_apply=%region_3.0 | all-reduce | flops 8192 | bytes 65536 | tf_op jit(solution)/shard_map/psum | solution.py:84
  350.0 215.5 %while.31 = (s32[]{:T(128)}, f32[1536]{0:T(1024)S(1)}, f32[32]{0:T(128)S(1)}, s32[4,1536]{1,0:T(4,128)}, bf16[32,6,1088]{0,1,2:T(8,128)(2,1)}, /*index=5*/bf16[3...) while((s32[]{:T(128)}, f32[1536]{0:T(1024)S(1)}, ...), condition=%wide.region_9.10_spmd, body=%wide.region_4.9_spmd.sunk | while | flops 29929252 | bytes 18916456 | solution.py:122
  351.5 5.0 gather_fusion.1
  360.1 9.3 %gather_fusion = bf16[1024,32,6]{1,2,0:T(8,128)(2,1)} fusion(bf16[32,6,1088]{0,1,2:T(8,128)(2,1)} %get-tuple-element.825, s32[1024]{0:T(1024)S(1)} %broadcast_clamp_fusion.4), kind=kCustom, calls=%fused_computation.1.clone.1 | custom fusion | bytes 790528 | tf_op jit(solution)/shard_map/while/body/eval_jaxpr/gather | solution.py:30
  381.1 4.3 fusion.85
  387.4 5.0 gather_fusion.1
  396.0 9.3 %gather_fusion = bf16[1024,32,6]{1,2,0:T(8,128)(2,1)} fusion(bf16[32,6,1088]{0,1,2:T(8,128)(2,1)} %get-tuple-element.825, s32[1024]{0:T(1024)S(1)} %broadcast_clamp_fusion.4), kind=kCustom, calls=%fused_computation.1.clone.1 | custom fusion | bytes 790528 | tf_op jit(solution)/shard_map/while/body/eval_jaxpr/gather | solution.py:30
  417.1 4.3 fusion.85
  423.3 5.0 gather_fusion.1
  431.9 9.3 %gather_fusion = bf16[1024,32,6]{1,2,0:T(8,128)(2,1)} fusion(bf16[32,6,1088]{0,1,2:T(8,128)(2,1)} %get-tuple-element.825, s32[1024]{0:T(1024)S(1)} %broadcast_clamp_fusion.4), kind=kCustom, calls=%fused_computation.1.clone.1 | custom fusion | bytes 790528 | tf_op jit(solution)/shard_map/while/body/eval_jaxpr/gather | solution.py:30
  453.0 4.3 fusion.85
  459.3 5.0 gather_fusion.1
  467.9 9.3 %gather_fusion = bf16[1024,32,6]{1,2,0:T(8,128)(2,1)} fusion(bf16[32,6,1088]{0,1,2:T(8,128)(2,1)} %get-tuple-element.825, s32[1024]{0:T(1024)S(1)} %broadcast_clamp_fusion.4), kind=kCustom, calls=%fused_computation.1.clone.1 | custom fusion | bytes 790528 | tf_op jit(solution)/shard_map/while/body/eval_jaxpr/gather | solution.py:30
  495.2 5.0 gather_fusion.1
  503.8 9.3 %gather_fusion = bf16[1024,32,6]{1,2,0:T(8,128)(2,1)} fusion(bf16[32,6,1088]{0,1,2:T(8,128)(2,1)} %get-tuple-element.825, s32[1024]{0:T(1024)S(1)} %broadcast_clamp_fusion.4), kind=kCustom, calls=%fused_computation.1.clone.1 | custom fusion | bytes 790528 | tf_op jit(solution)/shard_map/while/body/eval_jaxpr/gather | solution.py:30
  531.1 5.0 gather_fusion.1
  539.7 9.3 %gather_fusion = bf16[1024,32,6]{1,2,0:T(8,128)(2,1)} fusion(bf16[32,6,1088]{0,1,2:T(8,128)(2,1)} %get-tuple-element.825, s32[1024]{0:T(1024)S(1)} %broadcast_clamp_fusion.4), kind=kCustom, calls=%fused_computation.1.clone.1 | custom fusion | bytes 790528 | tf_op jit(solution)/shard_map/while/body/eval_jaxpr/gather | solution.py:30
  565.5 8.8 %scatter_custom_fusion = f32[1920]{0:T(1024)S(1)} fusion(s32[1536]{0:T(1024)} %get-tuple-element.610, f32[1536]{0:T(1024)S(1)} %get-tuple-element.424, f32[]{:T(128)} %constant.130.clone.1), kind=kCustom, calls=%fused_computation.58 | custom fusion | flops 1536 | bytes 8192 | tf_op jit(solution)/shard_map/scatter-add | solution.py:123
  578.7 6.5 %collective-permute-done.5 = f32[640]{0:T(1024)S(1)} collective-permute-done((f32[640]{0:T(1024)S(1)}, f32[640]{0:T(1024)S(1)}, u32[]{:S(2)}, u32[]{:S(2)}) %collective-permute-start.5) | collective-permute-done | bytes 2592 | tf_op jit(solution)/shard_map/ppermute | solution.py:26
  585.2 9.9 %psum.23 = f32[640]{0:T(1024)} all-reduce(f32[640]{0:T(1024)S(1)} %fusion.40), channel_id=1, replica_groups=mesh['dom'=32,'mode'=4] {'mode'}, use_global_device_ids=true, to_apply=%region_11.12 | all-reduce | flops 640 | bytes 5120 | tf_op jit(solution)/shard_map/psum | solution.py:127
  (289 shorter events, 236.0 us)
Async XLA Ops:
  7.2 31.6 %all-gather.2.cloned.1.call-start = ((), (), s32[]{:S(2)}) async-start(), calls=%async_computation | async-start | bytes 1966080 | tf_op jit(solution)/shard_map/all_gather | solution.py:50
  7.9 38.4 %collective-permute-start.2 = (f32[640]{0:T(1024)}, f32[640]{0:T(1024)S(1)}, u32[]{:S(2)}, u32[]{:S(2)}) collective-permute-start(f32[640]{0:T(1024)} %param.21), channel_id=1, source_target_pairs={{0,4},{4,8},{8,12},{12,16},{16,20},{20,24},{24,28},{28,32},{32,36}... | collective-permute-start | bytes 7688 | tf_op jit(solution)/shard_map/ppermute | solution.py:15
  9.8 36.5 %collective-permute-start.3 = (f32[640]{0:T(1024)}, f32[640]{0:T(1024)S(1)}, u32[]{:S(2)}, u32[]{:S(2)}) collective-permute-start(f32[640]{0:T(1024)} %param.21), channel_id=1, source_target_pairs={{4,0},{8,4},{12,8},{16,12},{20,16},{24,20},{28,24},{32,28},{36,32}... | collective-permute-start | bytes 7688 | tf_op jit(solution)/shard_map/ppermute | solution.py:18
  13.5 10.5 %copy-start.13 = (f32[128]{0:T(128)S(1)}, f32[128]{0:T(128)}, u32[]{:S(2)}) copy-start(f32[128]{0:T(128)} %param.14) | copy-start | bytes 1540
  13.5 11.7 %copy-start.10 = (s32[1536]{0:T(1024)S(1)}, s32[1536]{0:T(1024)}, u32[]{:S(2)}) copy-start(s32[1536]{0:T(1024)} %param.20) | copy-start | bytes 18436
  25.8 20.5 %copy-start.11 = (f32[640]{0:T(1024)S(1)}, f32[640]{0:T(1024)}, u32[]{:S(2)}) copy-start(f32[640]{0:T(1024)} %param.21) | copy-start | bytes 7684
  40.7 18.7 %copy-start.1 = (bf16[128,6,1024]{0,2,1:T(8,128)(2,1)}, bf16[128,6,1024]{0,2,1:T(8,128)(2,1)S(1)}, u32[]{:S(2)}) copy-start(bf16[128,6,1024]{0,2,1:T(8,128)(2,1)S(1)} %copy.96) | copy-start | bytes 4718596
  40.7 18.7 %collective-permute-start = (bf16[128,6,32]{0,2,1:T(8,128)(2,1)S(1)}, bf16[128,6,32]{0,2,1:T(8,128)(2,1)S(1)}, u32[]{:S(2)}, u32[]{:S(2)}) collective-permute-start(bf16[128,6,32]{0,2,1:T(8,128)(2,1)S(1)} %get-tuple-element.611), channel_id=1, source_target_pairs={{0,4},{4,8},{8,12},{12,16},{16,20},{20,24},{24,28},{28,32},{32,36}... | collective-permute-start | bytes 147464 | tf_op jit(solution)/shard_map/ppermute | solution.py:15
  42.7 16.8 %collective-permute-start.1 = (bf16[128,6,32]{0,2,1:T(8,128)(2,1)S(1)}, bf16[128,6,32]{0,2,1:T(8,128)(2,1)S(1)}, u32[]{:S(2)}, u32[]{:S(2)}) collective-permute-start(bf16[128,6,32]{0,2,1:T(8,128)(2,1)S(1)} %get-tuple-element.612), channel_id=1, source_target_pairs={{4,0},{8,4},{12,8},{16,12},{20,16},{24,20},{28,24},{32,28},{36,32}... | collective-permute-start | bytes 147464 | tf_op jit(solution)/shard_map/ppermute | solution.py:18
  46.4 11.8 %copy-start.7 = (f32[1536]{0:T(1024)S(1)}, f32[1536]{0:T(1024)}, u32[]{:S(2)}) copy-start(f32[1536]{0:T(1024)} %param.18) | copy-start | bytes 18436
  59.4 0.6 copy-start.5
  59.5 0.6 copy-start.6
  68.0 7.3 %copy-start.2 = (bf16[24,24]{1,0:T(8,128)(2,1)S(1)}, bf16[24,24]{1,0:T(8,128)(2,1)}, u32[]{:S(2)}) copy-start(bf16[24,24]{1,0:T(8,128)(2,1)} %param.17) | copy-start | bytes 3460
  96.2 2.1 copy-start.3
  120.4 2.1 copy-start.3
  123.2 0.6 copy-start.4
  144.6 2.1 copy-start.3
  168.9 2.1 copy-start.3
  171.6 0.6 copy-start.4
  193.1 2.1 copy-start.3
  217.3 2.1 copy-start.3
  347.3 2.6 copy-start.9
  347.4 2.6 copy-start.12
  376.7 2.2 copy-start
  412.7 2.2 copy-start
  448.6 2.2 copy-start
  484.5 2.2 copy-start
  520.5 2.2 copy-start
  556.4 2.2 copy-start
  565.5 29.6 %copy-start.8 = (f32[32]{0:T(128)}, f32[32]{0:T(128)S(1)}, u32[]{:S(2)}) copy-start(f32[32]{0:T(128)S(1)} %get-tuple-element.846) | copy-start | bytes 388
  574.3 4.3 collective-permute-start.4
  576.3 8.9 %collective-permute-start.5 = (f32[640]{0:T(1024)S(1)}, f32[640]{0:T(1024)S(1)}, u32[]{:S(2)}, u32[]{:S(2)}) collective-permute-start(f32[640]{0:T(1024)S(1)} %get-tuple-element.614), channel_id=1, source_target_pairs={{0,4},{4,8},{8,12},{12,16},{16,20},{20,24},{24,28},{28,32},{32,36}... | collective-permute-start | bytes 7688 | tf_op jit(solution)/shard_map/ppermute | solution.py:26
  (4 other events, 2.4 us)
Sparse Core Ops, SparseCore 0:
  9.7 29.0 all-gather.1
where the time goes:
time: 605 us; the launch traced here: 602 us
  local copies, waits for them, and re-layouts  318 us (53%)
  blocking collectives  132 us (22%)
  matrix products  54.7 us (9%)
  other arithmetic  46.7 us (8%)
  waiting for transfers between devices  20.2 us (3%)
  starting transfers between devices  15.5 us (3%)
  between operations  14.3 us (2%)
    gather x42, local copies, waits for them, and re-layouts, element_dofs(): picked = field[:, :, element_nodes]  193 us
    psum x1, blocking collectives, on_device(): stiff_gram, mass_gram = lax.psum((stiff_gram, mass_gram), 'dom')  122 us
    reduce_sum x6, other arithmetic, energy_block(): term_m = jnp.sum(shapes * mass_q, axis=1)  25.5 us
    dot_general x6, matrix products, gram_block(): lax.dot_general(all_dofs, force_k, dims, preferred_element_type=jnp.float32)  19.3 us
    unnamed x24, local copies, waits for them, and re-layouts  18.4 us
    dot_general x6, matrix products, energy_block(): jnp.einsum('abe,mbe->mae', matrices, deriv_dofs, preferred_element_type=j...  14.3 us
    dot_general x6, local copies, waits for them, and re-layouts, energy_block(): jnp.einsum('ab,mbe->mae', mass_ref, shapes, preferred_element_type=jnp.fl...  13.3 us
    dot_general x6, local copies, waits for them, and re-layouts, energy_block(): jnp.einsum('ab,mbe->mae', mass_ref, deriv_dofs, preferred_element_type=jn...  13 us
  transfers between devices with their start and end apart: 7, of which 2 were waited for; matrix products, arithmetic and copies ran while one was open for 5% of the time, Pallas kernels for 0%

commit v1 on v0

v1 whole, which is shorter than its diff:
```python
import functools

import jax
import jax.numpy as jnp
from jax import lax
from jax.experimental import pallas as pl
from jax.experimental.pallas import tpu as pltpu
from jax.sharding import PartitionSpec as P

H = 32
COMPS = 6
CORNERS = 4
DOFS = 24
TILE = 256
LANES = 128
MIB = 1 << 20
f32, bf16 = jnp.float32, jnp.bfloat16


def dot(a, b):
    return lax.dot_general(a, b, (((1,), (0,)), ((), ())), preferred_element_type=f32)


def dot_nt(a, b):
    return lax.dot_general(a, b, (((1,), (1,)), ((), ())), preferred_element_type=f32)


def iota(shape, dim):
    return lax.broadcasted_iota(jnp.int32, shape, dim)


def one_hot(rows, index):
    hit = iota((rows, index.shape[1]), 0) == index
    return jnp.where(hit, 1.0, 0.0).astype(bf16)


def three_pieces(x):
    first = x.astype(bf16)
    rest = x - first.astype(f32)
    second = rest.astype(bf16)
    third = (rest - second.astype(f32)).astype(bf16)
    return first, second, third


def column_of(row, offset, count):
    n = row.shape[1]
    mask = iota((count, n), 1) == iota((count, n), 0) + offset
    return jnp.sum(jnp.where(mask, row, 0.0), axis=1, keepdims=True)


def fill_one_hot(conn_ref, own_hot, rim_hot, nodes):
    for k in range(CORNERS):
        index = conn_ref[k : k + 1, :]
        cols = pl.ds(k * TILE, TILE)
        own_hot[:, cols] = one_hot(nodes, index - H)
        rim = jnp.where(index < H, index, jnp.where(index < nodes + H, -1, index - nodes))
        rim_hot[:, cols] = one_hot(2 * H, rim)


def forces_kernel(
    modes,
    nodes,
    des,
    conn_ref,
    owner_ref,
    mass_ref_,
    stiff_ref,
    field_ref,
    rim_ref,
    dir_low_ref,
    dir_own_ref,
    dir_high_ref,
    ref_ref,
    eig_ref,
    weight_ref,
    resid_ref,
    power_ref,
    node_ref,
    node_rim_ref,
    diag_ref,
    mass_big,
    table,
    own_hot,
    rim_hot,
    shapes,
    stacked,
    mass_q,
    stiff_wide,
    force,
):
    step = pl.program_id(0)
    rows = COMPS * modes
    big = CORNERS * rows
    rank = lax.axis_index("dom")
    mode_start = lax.axis_index("mode") * modes

    @pl.when(step == 0)
    def _():
        row = iota((big, DOFS), 0)
        dof = CORNERS * ((row % rows) // modes) + row // rows
        spread = jnp.where(dof == iota((big, DOFS), 1), 1.0, 0.0).astype(bf16)
        half = dot(spread, ref_ref[...]).astype(bf16)
        for part in range(CORNERS):
            span = pl.ds(part * rows, rows)
            wide = dot_nt(half, spread[part * rows : (part + 1) * rows])
            same = iota((big, rows), 0) % modes == iota((big, rows), 1) % modes
            mass_big[:, span] = jnp.where(same, wide, 0.0).astype(bf16)
        per = des // LANES
        table[...] = jnp.zeros_like(table)
        for side, ref in enumerate((dir_low_ref, dir_own_ref, dir_high_ref)):
            for i in range(per):
                at = side * per + i
                table[at : at + 1, :] = ref[:, i * LANES : (i + 1) * LANES]
        node_ref[...] = jnp.zeros_like(node_ref)
        node_rim_ref[...] = jnp.zeros_like(node_rim_ref)
        diag_ref[...] = jnp.zeros_like(diag_ref)

    eig = column_of(eig_ref[...], mode_start, modes)
    weight = 2.0 * column_of(weight_ref[...], 0, modes)

    local = owner_ref[...] - (rank - 1) * des
    entries = table.shape[0]
    pieces = jnp.concatenate(three_pieces(table[...]), axis=0)
    looked = dot(pieces, one_hot(LANES, local % LANES))
    looked = looked[:entries] + looked[entries : 2 * entries] + looked[2 * entries :]
    here = iota((entries, TILE), 0) == local // LANES
    elem_dir = jnp.sum(jnp.where(here, looked, 0.0), axis=0, keepdims=True)
    elem_mass = mass_ref_[...]

    fill_one_hot(conn_ref, own_hot, rim_hot, nodes)
    shapes[...] = dot(field_ref[...], own_hot[...]) + dot(rim_ref[...], rim_hot[...])
    for k in range(CORNERS):
        stacked[k * rows : (k + 1) * rows, :] = shapes[:, k * TILE : (k + 1) * TILE].astype(bf16)
    mass_q[...] = dot(mass_big[...], stacked[...])
    stiff_wide[...] = stiff_ref[...].astype(f32)

    for lane in range(TILE // LANES):
        cols = slice(lane * LANES, (lane + 1) * LANES)
        direction = elem_dir[:, cols]
        mass = elem_mass[:, cols]
        scaled = eig * mass
        power = jnp.zeros((modes, LANES), f32)
        for first in range(0, DOFS, 4):
            sums = [jnp.zeros((modes, LANES), f32) for _ in range(4)]
            for b in range(DOFS):
                c, k = b // CORNERS, b % CORNERS
                at = k * TILE + lane * LANES
                s = shapes[c * modes : (c + 1) * modes, at : at + LANES]
                for q in range(4):
                    sums[q] = sums[q] + stiff_wide[first + q, b : b + 1, cols] * s
            for q in range(4):
                c, k = (first + q) // CORNERS, (first + q) % CORNERS
                at = k * TILE + lane * LANES
                s = shapes[c * modes : (c + 1) * modes, at : at + LANES]
                base = k * rows + c * modes
                mq = mass_q[base : base + modes, cols]
                power = power + s * mq
                resid = sums[q] - scaled * mq
                force[c * modes : (c + 1) * modes, at : at + LANES] = (direction * resid).astype(bf16)
                resid_ref[base : base + modes, cols] = weight * resid
        power = power * mass
        power_ref[:, cols] = power
        diag_ref[...] += direction * power

    node_ref[...] += dot_nt(force[...], own_hot[...])
    node_rim_ref[...] += dot_nt(force[...], rim_hot[...])


def gather_modes(refs, c, modes):
    return jnp.concatenate([r[c * modes : (c + 1) * modes, :] for r in refs], axis=0)


def gram_kernel(modes, groups, node_ref, node_rim_ref, diag_ref, *rest):
    fields, rims, out_ref = rest[:groups], rest[groups : 2 * groups], rest[2 * groups]
    total = jnp.zeros((modes, groups * modes), f32)
    for c in range(COMPS):
        span = slice(c * modes, (c + 1) * modes)
        for part, parts in ((node_ref, fields), (node_rim_ref, rims)):
            exact = part[span, :]
            high = exact.astype(bf16)
            low = (exact - high.astype(f32)).astype(bf16)
            both = dot_nt(jnp.concatenate([high, low], axis=0), gather_modes(parts, c, modes))
            total = total + both[:modes] + both[modes:]
    out_ref[0:modes, :] = total
    diag = jnp.sum(diag_ref[...], axis=1, keepdims=True)
    mask = iota((modes, LANES), 0) == iota((modes, LANES), 1)
    out_ref[modes : modes + 8, :] = jnp.broadcast_to(
        jnp.sum(jnp.where(mask, diag, 0.0), axis=0, keepdims=True), (8, LANES)
    )


def energy_kernel(modes, groups, nodes, des, parts, *refs):
    gram_refs, refs = refs[:parts], refs[parts:]
    eig_ref, weight_ref = refs[:2]
    fields, rims, refs = refs[2 : 2 + groups], refs[2 + groups : 2 + 2 * groups], refs[2 + 2 * groups :]
    conn_ref, owner_ref, resid_ref, power_ref = refs[:4]
    low_ref, own_ref, high_ref, deriv_ref = refs[4:8]
    deriv, deriv_rim, factor, own_hot, rim_hot, totals = refs[8:]
    step = pl.program_id(0)
    rows = COMPS * modes
    rank = lax.axis_index("dom")
    mode_start = lax.axis_index("mode") * modes

    @pl.when(step == 0)
    def _():
        total = gram_refs[0][...]
        for ref in gram_refs[1:]:
            total = total + ref[...]
        gram = total[:modes]
        mass_diag = total[modes : modes + 1]
        shape = (modes, groups * modes)
        mask = iota(shape, 0) == iota(shape, 1)
        eig_rows = jnp.broadcast_to(eig_ref[...], (8, LANES))
        turned = pltpu.roll(eig_rows, lax.rem(LANES - mode_start, LANES), 1)[0:1]
        spacing = column_of(turned, 0, modes) - turned
        combiner = jnp.where(
            mask, -0.5 * mass_diag, gram / jnp.where(mask, 1.0, spacing)
        ).astype(bf16)
        diagonal = jnp.where(mask, gram, 0.0)
        deriv_ref[...] = jnp.sum(diagonal, axis=0, keepdims=True)[:, :modes]
        eig_deriv = jnp.sum(diagonal, axis=1, keepdims=True)
        factor[...] = jnp.broadcast_to(
            eig_deriv * column_of(weight_ref[...], 0, modes), factor.shape
        )
        for c in range(COMPS):
            span = slice(c * modes, (c + 1) * modes)
            deriv[span, :] = dot(combiner, gather_modes(fields, c, modes)).astype(bf16)
            deriv_rim[span, :] = dot(combiner, gather_modes(rims, c, modes)).astype(bf16)
        totals[...] = jnp.zeros_like(totals)

    fill_one_hot(conn_ref, own_hot, rim_hot, nodes)
    moved = dot(deriv[...], own_hot[...]) + dot(deriv_rim[...], rim_hot[...])
    energies = []
    for lane in range(TILE // LANES):
        cols = slice(lane * LANES, (lane + 1) * LANES)
        total = -factor[...] * power_ref[:, cols]
        for k in range(CORNERS):
            at = k * TILE + lane * LANES
            for c in range(COMPS):
                base = k * rows + c * modes
                total = total + moved[c * modes : (c + 1) * modes, at : at + LANES] * resid_ref[
                    base : base + modes, cols
                ]
        energies.append(jnp.sum(total, axis=0, keepdims=True))
    energy = jnp.concatenate(energies, axis=1)
    local = owner_ref[...] - (rank - 1) * des
    entries = totals.shape[0]
    here = iota((entries, TILE), 0) == local // LANES
    spread = jnp.concatenate(
        [jnp.where(here, p.astype(f32), 0.0).astype(bf16) for p in three_pieces(energy)], axis=0
    )
    sums = dot_nt(spread, one_hot(LANES, local % LANES))
    totals[...] += sums[:entries] + sums[entries : 2 * entries] + sums[2 * entries :]

    @pl.when(step == pl.num_programs(0) - 1)
    def _():
        per = des // LANES
        for side, ref in enumerate((low_ref, own_ref, high_ref)):
            for i in range(per):
                at = side * per + i
                ref[:, i * LANES : (i + 1) * LANES] = totals[at : at + 1, :]


def shift_in(value, axis, step):
    count = lax.axis_size(axis)
    return lax.ppermute(value, axis, [(i, (i - step) % count) for i in range(count)])


def neighbour(value, step):
    count = lax.axis_size("dom")
    pairs = [(i, i + step) for i in range(count) if 0 <= i + step < count]
    return lax.ppermute(value, "dom", pairs)


def others(value, groups):
    size = len(groups[0])
    return [
        lax.ppermute(value, "dom", [(g[i], g[(i + s) % size]) for g in groups for i in range(size)])
        for s in range(1, size)
    ]


def whole(shape):
    return pl.BlockSpec(shape, lambda t: (0,) * len(shape))


def on_device(
    mode_shapes,
    eigenvalues,
    mode_weights,
    stiff_deriv,
    mass_ref,
    mass_scale,
    connectivity,
    design_owner,
    direction,
):
    modes, _, nodes = mode_shapes.shape
    elems = connectivity.shape[1]
    des = direction.shape[0]
    groups = lax.axis_size("mode")
    total_modes = groups * modes
    rows = COMPS * modes
    big = CORNERS * rows
    tiles = elems // TILE
    entries = 16

    dir_own = direction.reshape(1, des)
    dir_low, dir_high = neighbour(dir_own, 1), neighbour(dir_own, -1)
    field = jnp.transpose(mode_shapes, (1, 0, 2)).reshape(rows, nodes)
    rim = jnp.concatenate(
        [neighbour(field[:, nodes - H :], 1), neighbour(field[:, :H], -1)], axis=1
    )
    fields = [field] + [shift_in(field, "mode", s) for s in range(1, groups)]
    rims = [rim] + [shift_in(rim, "mode", s) for s in range(1, groups)]
    eig_row = eigenvalues.reshape(1, total_modes)
    weight_row = mode_weights.reshape(1, modes)
    mass_row = mass_scale.reshape(1, elems)
    owner_row = design_owner.reshape(1, elems)

    def tiled(rows_):
        return pl.BlockSpec((rows_, TILE), lambda t: (0, t))

    resid, power, node, node_rim, diag = pl.pallas_call(
        functools.partial(forces_kernel, modes, nodes, des),
        grid=(tiles,),
        in_specs=[
            tiled(CORNERS),
            tiled(1),
            tiled(1),
            pl.BlockSpec((DOFS, DOFS, TILE), lambda t: (0, 0, t)),
            whole((rows, nodes)),
            whole((rows, 2 * H)),
            whole((1, des)),
            whole((1, des)),
            whole((1, des)),
            whole((DOFS, DOFS)),
            whole((1, total_modes)),
            whole((1, modes)),
        ],
        out_specs=[
            tiled(big),
            tiled(modes),
            whole((rows, nodes)),
            whole((rows, 2 * H)),
            whole((modes, LANES)),
        ],
        out_shape=[
            jax.ShapeDtypeStruct((big, elems), f32),
            jax.ShapeDtypeStruct((modes, elems), f32),
            jax.ShapeDtypeStruct((rows, nodes), f32),
            jax.ShapeDtypeStruct((rows, 2 * H), f32),
            jax.ShapeDtypeStruct((modes, LANES), f32),
        ],
        scratch_shapes=[
            pltpu.VMEM((big, big), bf16),
            pltpu.VMEM((entries, LANES), f32),
            pltpu.VMEM((nodes, CORNERS * TILE), bf16),
            pltpu.VMEM((2 * H, CORNERS * TILE), bf16),
            pltpu.VMEM((rows, CORNERS * TILE), f32),
            pltpu.VMEM((big, TILE), bf16),
            pltpu.VMEM((big, TILE), f32),
            pltpu.VMEM((DOFS, DOFS, TILE), f32),
            pltpu.VMEM((rows, CORNERS * TILE), bf16),
        ],
        compiler_params=pltpu.CompilerParams(vmem_limit_bytes=40 * MIB),
        cost_estimate=pl.CostEstimate(
            flops=8_000_000_000, bytes_accessed=8_000_000, transcendentals=0
        ),
        name="forces",
    )(
        connectivity,
        owner_row,
        mass_row,
        stiff_deriv,
        field,
        rim,
        dir_low,
        dir_own,
        dir_high,
        mass_ref,
        eig_row,
        weight_row,
    )

    gram = pl.pallas_call(
        functools.partial(gram_kernel, modes, groups),
        out_shape=jax.ShapeDtypeStruct((modes + 8, total_modes), f32),
        compiler_params=pltpu.CompilerParams(vmem_limit_bytes=40 * MIB),
        name="gram",
    )(node, node_rim, diag, *fields, *rims)

    count = lax.axis_size("dom")
    cores = [[i, i + 1] for i in range(0, count, 2)]
    along_x = [[y * 8 + x * 2 + c for x in range(4)] for y in range(count // 8) for c in range(2)]
    along_y = [[y * 8 + k for y in range(count // 8)] for k in range(8)]
    for part in (cores, along_x):
        gram = sum(others(gram, part), gram)
    grams = [gram] + others(gram, along_y)

    low, own, high, eig_deriv = pl.pallas_call(
        functools.partial(energy_kernel, modes, groups, nodes, des, len(grams)),
        grid=(tiles,),
        in_specs=[whole(gram.shape)] * len(grams)
        + [whole((1, total_modes)), whole((1, modes))]
        + [whole((rows, nodes))] * groups
        + [whole((rows, 2 * H))] * groups
        + [tiled(CORNERS), tiled(1), tiled(big), tiled(modes)],
        out_specs=[whole((1, des))] * 3 + [whole((1, modes))],
        out_shape=[jax.ShapeDtypeStruct((1, des), f32)] * 3 + [jax.ShapeDtypeStruct((1, modes), f32)],
        scratch_shapes=[
            pltpu.VMEM((rows, nodes), bf16),
            pltpu.VMEM((rows, 2 * H), bf16),
            pltpu.VMEM((modes, LANES), f32),
            pltpu.VMEM((nodes, CORNERS * TILE), bf16),
            pltpu.VMEM((2 * H, CORNERS * TILE), bf16),
            pltpu.VMEM((entries, LANES), f32),
        ],
        compiler_params=pltpu.CompilerParams(vmem_limit_bytes=40 * MIB),
        name="energy",
    )(*grams, eig_row, weight_row, *fields, *rims, connectivity, owner_row, resid, power)

    owned = own + neighbour(low, -1) + neighbour(high, 1)
    for_all = owned
    for s in range(1, groups):
        for_all = for_all + shift_in(owned, "mode", s)
    return (for_all.reshape(des), eig_deriv.reshape(modes))


def solution(mesh):
    return jax.shard_map(
        on_device,
        mesh=mesh,
        in_specs=(
            P("mode", None, "dom"),
            P(),
            P("mode"),
            P(None, None, "dom"),
            P(),
            P("dom"),
            P(None, "dom"),
            P("dom"),
            P("dom"),
        ),
        out_specs=(P("dom"), P("mode")),
        check_vma=False,
    )
```

time: 605 us -> 101 us (0.17)
  the two profiles are of different devices: /device:TPU:2 before, /device:TPU:8 now
where the time goes in v1:
time: 101 us; the launch traced here: 99.9 us
  starting transfers between devices  41.2 us (41%)
  Pallas kernels  31.3 us (31%)
  waiting for transfers between devices  17.7 us (18%)
  local copies, waits for them, and re-layouts  8.22 us (8%)
    pallas_call x1, Pallas kernels, on_device(): pl.pallas_call(functools.partial(forces_kernel, modes, nodes, des), grid=...  23.9 us
    ppermute x6, starting transfers between devices, neighbour(): return lax.ppermute(value, 'dom', pairs)  19.4 us
    ppermute x9, starting transfers between devices, shift_in(): lax.ppermute(value, axis, [(i, (i - step) % count) for i in range(count)])  14.6 us
    ppermute x7, waiting for transfers between devices, others(): lax.ppermute(value, 'dom', [(g[i], g[(i + s) % size]) for g in groups for...  8.66 us
    ppermute x7, starting transfers between devices, others(): lax.ppermute(value, 'dom', [(g[i], g[(i + s) % size]) for g in groups for...  7.17 us
    pallas_call x1, Pallas kernels, on_device(): pl.pallas_call(functools.partial(energy_kernel, modes, groups, nodes, des...  6.63 us
    ppermute x6, waiting for transfers between devices, neighbour(): return lax.ppermute(value, 'dom', pairs)  6.32 us
    unnamed x16, local copies, waits for them, and re-layouts  5.22 us
  transfers between devices with their start and end apart: 22, of which 11 were waited for; matrix products, arithmetic and copies ran while one was open for 2% of the time, Pallas kernels for 24%

profile of v1, /device:TPU:8, one launch (start us, length us, event | category | flops | bytes accessed | tf_op | source)
XLA Modules:
  0.0 99.9 jit_solution(7153435901952768021)
XLA Ops:
  0.6 0.9 fusion
  1.5 1.9 %collective-permute-start = (bf16[192,32]{1,0:T(8,128)(2,1)S(1)}, bf16[192,32]{1,0:T(8,128)(2,1)S(1)}, u32[]{:S(2)}, u32[]{:S(2)}) collective-permute-start(bf16[192,32]{1,0:T(8,128)(2,1)S(1)} %get-tuple-element.20), channel_id=1, source_target_pairs={{0,4},{4,8},{8,12},{12,16},{16,20},{20,24},{24,28},{28,32},{32,36}... | collective-permute-start | bytes 36872 | tf_op jit(solution)/shard_map/ppermute | solution.py:272
  3.5 5.8 %collective-permute-start.1 = (bf16[192,32]{1,0:T(8,128)(2,1)S(1)}, bf16[192,32]{1,0:T(8,128)(2,1)S(1)}, u32[]{:S(2)}, u32[]{:S(2)}) collective-permute-start(bf16[192,32]{1,0:T(8,128)(2,1)S(1)} %get-tuple-element.21), channel_id=1, source_target_pairs={{4,0},{8,4},{12,8},{16,12},{20,16},{24,20},{28,24},{32,28},{36,32}... | collective-permute-start | bytes 36872 | tf_op jit(solution)/shard_map/ppermute | solution.py:272
  9.2 1.7 %collective-permute-done.1 = bf16[192,32]{1,0:T(8,128)(2,1)S(1)} collective-permute-done((bf16[192,32]{1,0:T(8,128)(2,1)S(1)}, bf16[192,32]{1,0:T(8,128)(2,1)S(1)}, u32[]{:S(2)}, u32[]{:S(2)}) %collective-permute-start.1) | collective-permute-done | bytes 12320 | tf_op jit(solution)/shard_map/ppermute | solution.py:272
  11.1 2.0 %collective-permute-start.9 = (bf16[192,64]{1,0:T(8,128)(2,1)S(1)}, bf16[192,64]{1,0:T(8,128)(2,1)S(1)}, u32[]{:S(2)}, u32[]{:S(2)}) collective-permute-start(bf16[192,64]{1,0:T(8,128)(2,1)S(1)} %pad_maximum_fusion.rim_ref.rest_4_.refs_10_), channel_id=1, source_target_pairs={{0,1},{1,2},{2,3},{3,0},{4,5},{5,6},{6,7},{7,4},{8,9},{9,10},{10,1... | collective-permute-start | bytes 73736 | tf_op jit(solution)/shard_map/ppermute | solution.py:266
  13.7 5.5 %collective-permute-start.3 = (f32[1,640]{1,0:T(1,128)S(1)}, f32[1,640]{1,0:T(1,128)S(1)}, u32[]{:S(2)}, u32[]{:S(2)}) collective-permute-start(f32[1,640]{1,0:T(1,128)S(1)} %reshape.31.dir_own_ref), channel_id=1, source_target_pairs={{4,0},{8,4},{12,8},{16,12},{20,16},{24,20},{28,24},{32,28},{36,32}... | collective-permute-start | bytes 7688 | tf_op jit(solution)/shard_map/ppermute | solution.py:272
  19.2 1.9 %collective-permute-start.2 = (f32[1,640]{1,0:T(1,128)S(1)}, f32[1,640]{1,0:T(1,128)S(1)}, u32[]{:S(2)}, u32[]{:S(2)}) collective-permute-start(f32[1,640]{1,0:T(1,128)S(1)} %reshape.31.dir_own_ref), channel_id=1, source_target_pairs={{0,4},{4,8},{8,12},{12,16},{16,20},{20,24},{24,28},{28,32},{32,36}... | collective-permute-start | bytes 7688 | tf_op jit(solution)/shard_map/ppermute | solution.py:272
  21.2 2.0 %collective-permute-start.6 = (bf16[192,1024]{1,0:T(8,128)(2,1)}, bf16[192,1024]{1,0:T(8,128)(2,1)S(1)}, u32[]{:S(2)}, u32[]{:S(2)}) collective-permute-start(bf16[192,1024]{1,0:T(8,128)(2,1)} %bitcast.7), channel_id=1, source_target_pairs={{0,1},{1,2},{2,3},{3,0},{4,5},{5,6},{6,7},{7,4},{8,9},{9,10},{10,1... | collective-permute-start | bytes 1179656 | tf_op jit(solution)/shard_map/ppermute | solution.py:266
  23.1 2.0 %collective-permute-start.5 = (bf16[192,1024]{1,0:T(8,128)(2,1)}, bf16[192,1024]{1,0:T(8,128)(2,1)S(1)}, u32[]{:S(2)}, u32[]{:S(2)}) collective-permute-start(bf16[192,1024]{1,0:T(8,128)(2,1)} %bitcast.8), channel_id=1, source_target_pairs={{0,2},{1,3},{2,0},{3,1},{4,6},{5,7},{6,4},{7,5},{8,10},{9,11},{10,... | collective-permute-start | bytes 1179656 | tf_op jit(solution)/shard_map/ppermute | solution.py:266
  26.5 2.4 %collective-permute-start.4 = (bf16[192,1024]{1,0:T(8,128)(2,1)}, bf16[192,1024]{1,0:T(8,128)(2,1)S(1)}, u32[]{:S(2)}, u32[]{:S(2)}) collective-permute-start(bf16[192,1024]{1,0:T(8,128)(2,1)} %bitcast.9), channel_id=1, source_target_pairs={{0,3},{1,0},{2,1},{3,2},{4,7},{5,4},{6,5},{7,6},{8,11},{9,8},{10,9... | collective-permute-start | bytes 1179656 | tf_op jit(solution)/shard_map/ppermute | solution.py:266
  28.9 1.0 collective-permute-start.8
  29.8 1.4 %collective-permute-start.7 = (bf16[192,64]{1,0:T(8,128)(2,1)S(1)}, bf16[192,64]{1,0:T(8,128)(2,1)S(1)}, u32[]{:S(2)}, u32[]{:S(2)}) collective-permute-start(bf16[192,64]{1,0:T(8,128)(2,1)S(1)} %pad_maximum_fusion.rim_ref.rest_4_.refs_10_), channel_id=1, source_target_pairs={{0,3},{1,0},{2,1},{3,2},{4,7},{5,4},{6,5},{7,6},{8,11},{9,8},{10,9... | collective-permute-start | bytes 73736 | tf_op jit(solution)/shard_map/ppermute | solution.py:266
  31.2 1.0 copy-done
  32.2 0.7 copy-done.2
  34.3 1.5 %copy-done.6 = bf16[24,24,1536]{2,1,0:T(8,128)(2,1)S(1)} copy-done((bf16[24,24,1536]{2,1,0:T(8,128)(2,1)S(1)}, bf16[24,24,1536]{2,1,0:T(8,128)(2,1)}, u32[]{:S(2)}) %copy-start.6) | copy-done | bytes 1769496
  36.4 23.9 %forces.1 = (f32[768,1536]{1,0:T(8,128)S(1)}, f32[32,1536]{1,0:T(8,128)S(1)}, f32[192,1024]{1,0:T(8,128)S(1)}, f32[192,64]{1,0:T(8,128)S(1)}, f32[32,128]{1,0:T(8,128)S(1)}) custom-call(s32[4,1536]{1,0:T(4,128)S(1)} %copy-done.2, s32[1,1536]{1,0:T(1,128)S(1)} %reshape.28.owner_ref.refs_15_, f32[1,1536]{1,0:T(1,128)S(1)} %reshape.29.mass_ref_, ...), custom_call_target="tpu_custom_call" | custom-call | flops 8000000000 | bytes 8000000 | tf_op jit(solution)/shard_map/forces/pallas_call | solution.py:324
  60.4 0.8 gram.1
  61.3 1.2 %collective-permute-done.10 = f32[40,128]{1,0:T(8,128)S(1)} collective-permute-done((f32[40,128]{1,0:T(8,128)S(1)}, f32[40,128]{1,0:T(8,128)S(1)}, u32[]{:S(2)}, u32[]{:S(2)}) %collective-permute-start.10) | collective-permute-done | bytes 20512 | tf_op jit(solution)/shard_map/ppermute | solution.py:278
  62.5 2.7 %collective-permute-start.13 = (f32[40,128]{1,0:T(8,128)S(1)}, f32[40,128]{1,0:T(8,128)S(1)}, u32[]{:S(2)}, u32[]{:S(2)}) collective-permute-start(f32[40,128]{1,0:T(8,128)S(1)} %add.27), channel_id=1, source_target_pairs={{0,24},{8,0},{16,8},{24,16},{4,28},{12,4},{20,12},{28,20},{32,56},... | collective-permute-start | bytes 61448 | tf_op jit(solution)/shard_map/ppermute | solution.py:278
  65.2 0.9 collective-permute-start.11
  66.6 3.8 %collective-permute-done.12 = f32[40,128]{1,0:T(8,128)S(1)} collective-permute-done((f32[40,128]{1,0:T(8,128)S(1)}, f32[40,128]{1,0:T(8,128)S(1)}, u32[]{:S(2)}, u32[]{:S(2)}) %collective-permute-start.12) | collective-permute-done | bytes 20512 | tf_op jit(solution)/shard_map/ppermute | solution.py:278
  71.0 2.3 %collective-permute-start.15 = (f32[40,128]{1,0:T(8,128)S(1)}, f32[40,128]{1,0:T(8,128)S(1)}, u32[]{:S(2)}, u32[]{:S(2)}) collective-permute-start(f32[40,128]{1,0:T(8,128)S(1)} %add_add_fusion.refs_0_), channel_id=1, source_target_pairs={{0,64},{32,96},{64,0},{96,32},{4,68},{36,100},{68,4},{100,36},{8,7... | collective-permute-start | bytes 61448 | tf_op jit(solution)/shard_map/ppermute | solution.py:278
  74.3 2.0 %collective-permute-done.15.refs_2_ = f32[40,128]{1,0:T(8,128)S(1)} collective-permute-done((f32[40,128]{1,0:T(8,128)S(1)}, f32[40,128]{1,0:T(8,128)S(1)}, u32[]{:S(2)}, u32[]{:S(2)}) %collective-permute-start.15) | collective-permute-done | bytes 20512 | tf_op jit(solution)/shard_map/ppermute | solution.py:278
  76.3 0.8 collective-permute-done.14.refs_1_
  77.1 6.6 %energy.1 = (f32[1,640]{1,0:T(1,128)S(1)}, f32[1,640]{1,0:T(1,128)S(1)}, f32[1,640]{1,0:T(1,128)S(1)}, f32[1,32]{1,0:T(1,128)}) custom-call(f32[40,128]{1,0:T(8,128)S(1)} %add_add_fusion.refs_0_, f32[40,128]{1,0:T(8,128)S(1)} %collective-permute-done.14.refs_1_, f32[40,128]{1,0:T(8,128)S(1)} %collective-permute-done.15.refs_2_, ...), custom_call_target="tpu_custom_call" | custom-call | tf_op jit(solution)/shard_map/energy/pallas_call | solution.py:401
  83.7 1.9 %collective-permute-start.17 = (f32[1,640]{1,0:T(1,128)S(1)}, f32[1,640]{1,0:T(1,128)S(1)}, u32[]{:S(2)}, u32[]{:S(2)}) collective-permute-start(f32[1,640]{1,0:T(1,128)S(1)} %get-tuple-element.17), channel_id=1, source_target_pairs={{4,0},{8,4},{12,8},{16,12},{20,16},{24,20},{28,24},{32,28},{36,32}... | collective-permute-start | bytes 7688 | tf_op jit(solution)/shard_map/ppermute | solution.py:272
  85.6 2.4 %collective-permute-start.18 = (f32[1,640]{1,0:T(1,128)S(1)}, f32[1,640]{1,0:T(1,128)S(1)}, u32[]{:S(2)}, u32[]{:S(2)}) collective-permute-start(f32[1,640]{1,0:T(1,128)S(1)} %get-tuple-element.18), channel_id=1, source_target_pairs={{0,4},{4,8},{8,12},{12,16},{16,20},{20,24},{24,28},{28,32},{32,36}... | collective-permute-start | bytes 7688 | tf_op jit(solution)/shard_map/ppermute | solution.py:272
  88.0 4.6 %collective-permute-done.18 = f32[1,640]{1,0:T(1,128)S(1)} collective-permute-done((f32[1,640]{1,0:T(1,128)S(1)}, f32[1,640]{1,0:T(1,128)S(1)}, u32[]{:S(2)}, u32[]{:S(2)}) %collective-permute-start.18) | collective-permute-done | bytes 2592 | tf_op jit(solution)/shard_map/ppermute | solution.py:272
  92.6 3.1 %collective-permute-start.20 = (f32[1,640]{1,0:T(1,128)S(1)}, f32[1,640]{1,0:T(1,128)S(1)}, u32[]{:S(2)}, u32[]{:S(2)}) collective-permute-start(f32[1,640]{1,0:T(1,128)S(1)} %add_add_fusion.1), channel_id=1, source_target_pairs={{0,2},{1,3},{2,0},{3,1},{4,6},{5,7},{6,4},{7,5},{8,10},{9,11},{10,... | collective-permute-start | bytes 7688 | tf_op jit(solution)/shard_map/ppermute | solution.py:266
  95.7 0.9 collective-permute-start.19
  96.6 0.8 collective-permute-done.21
  97.8 1.5 %collective-permute-done.19 = f32[1,640]{1,0:T(1,128)S(1)} collective-permute-done((f32[1,640]{1,0:T(1,128)S(1)}, f32[1,640]{1,0:T(1,128)S(1)}, u32[]{:S(2)}, u32[]{:S(2)}) %collective-permute-start.19) | collective-permute-done | bytes 2592 | tf_op jit(solution)/shard_map/ppermute | solution.py:266
  (40 shorter events, 7.4 us)
Async XLA Ops:
  1.5 7.7 %collective-permute-start = (bf16[192,32]{1,0:T(8,128)(2,1)S(1)}, bf16[192,32]{1,0:T(8,128)(2,1)S(1)}, u32[]{:S(2)}, u32[]{:S(2)}) collective-permute-start(bf16[192,32]{1,0:T(8,128)(2,1)S(1)} %get-tuple-element.20), channel_id=1, source_target_pairs={{0,4},{4,8},{8,12},{12,16},{16,20},{20,24},{24,28},{28,32},{32,36}... | collective-permute-start | bytes 36872 | tf_op jit(solution)/shard_map/ppermute | solution.py:272
  3.5 7.5 %collective-permute-start.1 = (bf16[192,32]{1,0:T(8,128)(2,1)S(1)}, bf16[192,32]{1,0:T(8,128)(2,1)S(1)}, u32[]{:S(2)}, u32[]{:S(2)}) collective-permute-start(bf16[192,32]{1,0:T(8,128)(2,1)S(1)} %get-tuple-element.21), channel_id=1, source_target_pairs={{4,0},{8,4},{12,8},{16,12},{20,16},{24,20},{28,24},{32,28},{36,32}... | collective-permute-start | bytes 36872 | tf_op jit(solution)/shard_map/ppermute | solution.py:272
  11.1 18.8 %collective-permute-start.9 = (bf16[192,64]{1,0:T(8,128)(2,1)S(1)}, bf16[192,64]{1,0:T(8,128)(2,1)S(1)}, u32[]{:S(2)}, u32[]{:S(2)}) collective-permute-start(bf16[192,64]{1,0:T(8,128)(2,1)S(1)} %pad_maximum_fusion.rim_ref.rest_4_.refs_10_), channel_id=1, source_target_pairs={{0,1},{1,2},{2,3},{3,0},{4,5},{5,6},{6,7},{7,4},{8,9},{9,10},{10,1... | collective-permute-start | bytes 73736 | tf_op jit(solution)/shard_map/ppermute | solution.py:266
  13.7 12.8 %collective-permute-start.3 = (f32[1,640]{1,0:T(1,128)S(1)}, f32[1,640]{1,0:T(1,128)S(1)}, u32[]{:S(2)}, u32[]{:S(2)}) collective-permute-start(f32[1,640]{1,0:T(1,128)S(1)} %reshape.31.dir_own_ref), channel_id=1, source_target_pairs={{4,0},{8,4},{12,8},{16,12},{20,16},{24,20},{28,24},{32,28},{36,32}... | collective-permute-start | bytes 7688 | tf_op jit(solution)/shard_map/ppermute | solution.py:272
  19.2 9.7 %collective-permute-start.2 = (f32[1,640]{1,0:T(1,128)S(1)}, f32[1,640]{1,0:T(1,128)S(1)}, u32[]{:S(2)}, u32[]{:S(2)}) collective-permute-start(f32[1,640]{1,0:T(1,128)S(1)} %reshape.31.dir_own_ref), channel_id=1, source_target_pairs={{0,4},{4,8},{8,12},{12,16},{16,20},{20,24},{24,28},{28,32},{32,36}... | collective-permute-start | bytes 7688 | tf_op jit(solution)/shard_map/ppermute | solution.py:272
  21.2 39.2 %collective-permute-start.6 = (bf16[192,1024]{1,0:T(8,128)(2,1)}, bf16[192,1024]{1,0:T(8,128)(2,1)S(1)}, u32[]{:S(2)}, u32[]{:S(2)}) collective-permute-start(bf16[192,1024]{1,0:T(8,128)(2,1)} %bitcast.7), channel_id=1, source_target_pairs={{0,1},{1,2},{2,3},{3,0},{4,5},{5,6},{6,7},{7,4},{8,9},{9,10},{10,1... | collective-permute-start | bytes 1179656 | tf_op jit(solution)/shard_map/ppermute | solution.py:266
  23.1 37.2 %collective-permute-start.5 = (bf16[192,1024]{1,0:T(8,128)(2,1)}, bf16[192,1024]{1,0:T(8,128)(2,1)S(1)}, u32[]{:S(2)}, u32[]{:S(2)}) collective-permute-start(bf16[192,1024]{1,0:T(8,128)(2,1)} %bitcast.8), channel_id=1, source_target_pairs={{0,2},{1,3},{2,0},{3,1},{4,6},{5,7},{6,4},{7,5},{8,10},{9,11},{10,... | collective-permute-start | bytes 1179656 | tf_op jit(solution)/shard_map/ppermute | solution.py:266
  26.5 33.9 %collective-permute-start.4 = (bf16[192,1024]{1,0:T(8,128)(2,1)}, bf16[192,1024]{1,0:T(8,128)(2,1)S(1)}, u32[]{:S(2)}, u32[]{:S(2)}) collective-permute-start(bf16[192,1024]{1,0:T(8,128)(2,1)} %bitcast.9), channel_id=1, source_target_pairs={{0,3},{1,0},{2,1},{3,2},{4,7},{5,4},{6,5},{7,6},{8,11},{9,8},{10,9... | collective-permute-start | bytes 1179656 | tf_op jit(solution)/shard_map/ppermute | solution.py:266
  28.9 31.5 %collective-permute-start.8 = (bf16[192,64]{1,0:T(8,128)(2,1)S(1)}, bf16[192,64]{1,0:T(8,128)(2,1)S(1)}, u32[]{:S(2)}, u32[]{:S(2)}) collective-permute-start(bf16[192,64]{1,0:T(8,128)(2,1)S(1)} %pad_maximum_fusion.rim_ref.rest_4_.refs_10_), channel_id=1, source_target_pairs={{0,2},{1,3},{2,0},{3,1},{4,6},{5,7},{6,4},{7,5},{8,10},{9,11},{10,... | collective-permute-start | bytes 73736 | tf_op jit(solution)/shard_map/ppermute | solution.py:266
  29.8 30.5 %collective-permute-start.7 = (bf16[192,64]{1,0:T(8,128)(2,1)S(1)}, bf16[192,64]{1,0:T(8,128)(2,1)S(1)}, u32[]{:S(2)}, u32[]{:S(2)}) collective-permute-start(bf16[192,64]{1,0:T(8,128)(2,1)S(1)} %pad_maximum_fusion.rim_ref.rest_4_.refs_10_), channel_id=1, source_target_pairs={{0,3},{1,0},{2,1},{3,2},{4,7},{5,4},{6,5},{7,6},{8,11},{9,8},{10,9... | collective-permute-start | bytes 73736 | tf_op jit(solution)/shard_map/ppermute | solution.py:266
  31.2 1.0 copy-start
  32.2 0.7 copy-start.2
  33.0 0.7 copy-start.3
  33.6 0.7 copy-start.4
  34.3 1.5 %copy-start.6 = (bf16[24,24,1536]{2,1,0:T(8,128)(2,1)S(1)}, bf16[24,24,1536]{2,1,0:T(8,128)(2,1)}, u32[]{:S(2)}) copy-start(bf16[24,24,1536]{2,1,0:T(8,128)(2,1)} %stiff_ref.1) | copy-start | bytes 5308420
  35.7 0.7 copy-start.7
  36.4 24.0 %copy-start.1 = (bf16[32,6,1024]{2,0,1:T(8,128)(2,1)S(1)}, bf16[32,6,1024]{2,0,1:T(8,128)(2,1)}, u32[]{:S(2)}) copy-start(bf16[32,6,1024]{2,0,1:T(8,128)(2,1)} %param.9) | copy-start | bytes 1179652
  36.4 40.6 %copy-start.5 = (f32[32]{0:T(128)S(1)}, f32[32]{0:T(128)}, u32[]{:S(2)}) copy-start(f32[32]{0:T(128)} %param.11) | copy-start | bytes 388
  61.2 1.3 %collective-permute-start.10 = (f32[40,128]{1,0:T(8,128)S(1)}, f32[40,128]{1,0:T(8,128)S(1)}, u32[]{:S(2)}, u32[]{:S(2)}) collective-permute-start(f32[40,128]{1,0:T(8,128)S(1)} %gram.1), channel_id=1, source_target_pairs={{0,4},{4,0},{8,12},{12,8},{16,20},{20,16},{24,28},{28,24},{32,36},... | collective-permute-start | bytes 61448 | tf_op jit(solution)/shard_map/ppermute | solution.py:278
  62.5 4.2 %collective-permute-start.13 = (f32[40,128]{1,0:T(8,128)S(1)}, f32[40,128]{1,0:T(8,128)S(1)}, u32[]{:S(2)}, u32[]{:S(2)}) collective-permute-start(f32[40,128]{1,0:T(8,128)S(1)} %add.27), channel_id=1, source_target_pairs={{0,24},{8,0},{16,8},{24,16},{4,28},{12,4},{20,12},{28,20},{32,56},... | collective-permute-start | bytes 61448 | tf_op jit(solution)/shard_map/ppermute | solution.py:278
  65.2 5.3 %collective-permute-start.12 = (f32[40,128]{1,0:T(8,128)S(1)}, f32[40,128]{1,0:T(8,128)S(1)}, u32[]{:S(2)}, u32[]{:S(2)}) collective-permute-start(f32[40,128]{1,0:T(8,128)S(1)} %add.27), channel_id=1, source_target_pairs={{0,16},{8,24},{16,0},{24,8},{4,20},{12,28},{20,4},{28,12},{32,48},... | collective-permute-start | bytes 61448 | tf_op jit(solution)/shard_map/ppermute | solution.py:278
  65.2 5.3 %collective-permute-start.11 = (f32[40,128]{1,0:T(8,128)S(1)}, f32[40,128]{1,0:T(8,128)S(1)}, u32[]{:S(2)}, u32[]{:S(2)}) collective-permute-start(f32[40,128]{1,0:T(8,128)S(1)} %add.27), channel_id=1, source_target_pairs={{0,8},{8,16},{16,24},{24,0},{4,12},{12,20},{20,28},{28,4},{32,40},... | collective-permute-start | bytes 61448 | tf_op jit(solution)/shard_map/ppermute | solution.py:278
  70.5 3.9 %collective-permute-start.16 = (f32[40,128]{1,0:T(8,128)S(1)}, f32[40,128]{1,0:T(8,128)S(1)}, u32[]{:S(2)}, u32[]{:S(2)}) collective-permute-start(f32[40,128]{1,0:T(8,128)S(1)} %add_add_fusion.refs_0_), channel_id=1, source_target_pairs={{0,96},{32,0},{64,32},{96,64},{4,100},{36,4},{68,36},{100,68},{8,1... | collective-permute-start | bytes 61448 | tf_op jit(solution)/shard_map/ppermute | solution.py:278
  71.0 5.3 %collective-permute-start.15 = (f32[40,128]{1,0:T(8,128)S(1)}, f32[40,128]{1,0:T(8,128)S(1)}, u32[]{:S(2)}, u32[]{:S(2)}) collective-permute-start(f32[40,128]{1,0:T(8,128)S(1)} %add_add_fusion.refs_0_), channel_id=1, source_target_pairs={{0,64},{32,96},{64,0},{96,32},{4,68},{36,100},{68,4},{100,36},{8,7... | collective-permute-start | bytes 61448 | tf_op jit(solution)/shard_map/ppermute | solution.py:278
  73.3 3.8 %collective-permute-start.14 = (f32[40,128]{1,0:T(8,128)S(1)}, f32[40,128]{1,0:T(8,128)S(1)}, u32[]{:S(2)}, u32[]{:S(2)}) collective-permute-start(f32[40,128]{1,0:T(8,128)S(1)} %add_add_fusion.refs_0_), channel_id=1, source_target_pairs={{0,32},{32,64},{64,96},{96,0},{4,36},{36,68},{68,100},{100,4},{8,4... | collective-permute-start | bytes 61448 | tf_op jit(solution)/shard_map/ppermute | solution.py:278
  83.7 4.3 %collective-permute-start.17 = (f32[1,640]{1,0:T(1,128)S(1)}, f32[1,640]{1,0:T(1,128)S(1)}, u32[]{:S(2)}, u32[]{:S(2)}) collective-permute-start(f32[1,640]{1,0:T(1,128)S(1)} %get-tuple-element.17), channel_id=1, source_target_pairs={{4,0},{8,4},{12,8},{16,12},{20,16},{24,20},{28,24},{32,28},{36,32}... | collective-permute-start | bytes 7688 | tf_op jit(solution)/shard_map/ppermute | solution.py:272
  85.6 7.0 %collective-permute-start.18 = (f32[1,640]{1,0:T(1,128)S(1)}, f32[1,640]{1,0:T(1,128)S(1)}, u32[]{:S(2)}, u32[]{:S(2)}) collective-permute-start(f32[1,640]{1,0:T(1,128)S(1)} %get-tuple-element.18), channel_id=1, source_target_pairs={{0,4},{4,8},{8,12},{12,16},{16,20},{20,24},{24,28},{28,32},{32,36}... | collective-permute-start | bytes 7688 | tf_op jit(solution)/shard_map/ppermute | solution.py:272
  92.6 4.8 %collective-permute-start.21 = (f32[1,640]{1,0:T(1,128)S(1)}, f32[1,640]{1,0:T(1,128)S(1)}, u32[]{:S(2)}, u32[]{:S(2)}) collective-permute-start(f32[1,640]{1,0:T(1,128)S(1)} %add_add_fusion.1), channel_id=1, source_target_pairs={{0,1},{1,2},{2,3},{3,0},{4,5},{5,6},{6,7},{7,4},{8,9},{9,10},{10,1... | collective-permute-start | bytes 7688 | tf_op jit(solution)/shard_map/ppermute | solution.py:266
  92.6 5.2 %collective-permute-start.20 = (f32[1,640]{1,0:T(1,128)S(1)}, f32[1,640]{1,0:T(1,128)S(1)}, u32[]{:S(2)}, u32[]{:S(2)}) collective-permute-start(f32[1,640]{1,0:T(1,128)S(1)} %add_add_fusion.1), channel_id=1, source_target_pairs={{0,2},{1,3},{2,0},{3,1},{4,6},{5,7},{6,4},{7,5},{8,10},{9,11},{10,... | collective-permute-start | bytes 7688 | tf_op jit(solution)/shard_map/ppermute | solution.py:266
  95.7 3.6 %collective-permute-start.19 = (f32[1,640]{1,0:T(1,128)S(1)}, f32[1,640]{1,0:T(1,128)S(1)}, u32[]{:S(2)}, u32[]{:S(2)}) collective-permute-start(f32[1,640]{1,0:T(1,128)S(1)} %add_add_fusion.1), channel_id=1, source_target_pairs={{0,3},{1,0},{2,1},{3,2},{4,7},{5,4},{6,5},{7,6},{8,11},{9,8},{10,9... | collective-permute-start | bytes 7688 | tf_op jit(solution)/shard_map/ppermute | solution.py:266

commit v2 on v1

v2 whole, which is shorter than its diff:
```python
import functools

import jax
import jax.numpy as jnp
from jax import lax
from jax.experimental import pallas as pl
from jax.experimental.pallas import tpu as pltpu
from jax.sharding import PartitionSpec as P

H = 32
COMPS = 6
CORNERS = 4
DOFS = 24
TILE = 256
LANES = 128
EXTRA = 16
MIB = 1 << 20
f32, bf16 = jnp.float32, jnp.bfloat16


def dot(a, b):
    return lax.dot_general(a, b, (((1,), (0,)), ((), ())), preferred_element_type=f32)


def dot_nt(a, b):
    return lax.dot_general(a, b, (((1,), (1,)), ((), ())), preferred_element_type=f32)


def iota(shape, dim):
    return lax.broadcasted_iota(jnp.int32, shape, dim)


def one_hot(rows, index):
    hit = iota((rows, index.shape[1]), 0) == index
    return jnp.where(hit, 1.0, 0.0).astype(bf16)


def three_pieces(x):
    first = x.astype(bf16)
    rest = x - first.astype(f32)
    second = rest.astype(bf16)
    third = (rest - second.astype(f32)).astype(bf16)
    return first, second, third


def column_of(row, offset, count):
    n = row.shape[1]
    mask = iota((count, n), 1) == iota((count, n), 0) + offset
    return jnp.sum(jnp.where(mask, row, 0.0), axis=1, keepdims=True)


def rim_one_hot(conn_ref, rim_hot, nodes):
    for k in range(CORNERS):
        index = conn_ref[k : k + 1, :]
        rim = jnp.where(
            index < H, index + (LANES - H), jnp.where(index < nodes + H, -1, index - (nodes + H))
        )
        rim_hot[:, k * TILE : (k + 1) * TILE] = one_hot(LANES, rim)


def pack_kernel(rows, des, first_ref, last_ref, dir_ref, owner_ref, mass_ref_, up_ref, down_ref, owner_row, mass_row):
    up_ref[0:rows, :] = last_ref[...]
    down_ref[0:rows, :] = first_ref[...]
    table = jnp.concatenate(
        [dir_ref[i * LANES : (i + 1) * LANES].reshape(1, LANES) for i in range(des // LANES)], axis=0
    )
    pieces = [p.astype(f32) for p in three_pieces(table)]
    pad = jnp.zeros((EXTRA - 3 * (des // LANES), LANES), f32)
    packed = jnp.concatenate(pieces + [pad], axis=0).astype(bf16)
    up_ref[rows : rows + EXTRA, :] = packed
    down_ref[rows : rows + EXTRA, :] = packed
    for i in range(owner_row.shape[1] // LANES):
        span = slice(i * LANES, (i + 1) * LANES)
        owner_row[:, span] = owner_ref[span].reshape(1, LANES)
        mass_row[:, span] = mass_ref_[span].reshape(1, LANES)


def prepare_kernel(modes, nodes, conn_ref, field_ref, ref_ref, own_hot, shapes, mass_big):
    rows = COMPS * modes
    big = CORNERS * rows

    @pl.when(pl.program_id(0) == 0)
    def _():
        row = iota((big, DOFS), 0)
        dof = CORNERS * ((row % rows) // modes) + row // rows
        spread = jnp.where(dof == iota((big, DOFS), 1), 1.0, 0.0).astype(bf16)
        half = dot(spread, ref_ref[...]).astype(bf16)
        same = iota((big, rows), 0) % modes == iota((big, rows), 1) % modes
        for part in range(CORNERS):
            wide = dot_nt(half, spread[part * rows : (part + 1) * rows])
            mass_big[:, part * rows : (part + 1) * rows] = jnp.where(same, wide, 0.0).astype(bf16)

    for k in range(CORNERS):
        own_hot[:, k * TILE : (k + 1) * TILE] = one_hot(nodes, conn_ref[k : k + 1, :] - H)
    shapes[...] = dot(field_ref[...], own_hot[...]).astype(bf16)


def forces_kernel(
    modes,
    nodes,
    des,
    conn_ref,
    owner_ref,
    mass_ref_,
    stiff_ref,
    own_hot,
    own_shapes,
    low_ref,
    own_ref,
    high_ref,
    mass_big,
    eig_ref,
    weight_ref,
    resid_ref,
    power_ref,
    node_ref,
    node_rim_ref,
    diag_ref,
    table,
    rim,
    rim_hot,
    shapes,
    stacked,
    mass_q,
    stiff_wide,
    force,
):
    step = pl.program_id(0)
    rows = COMPS * modes
    rank = lax.axis_index("dom")
    mode_start = lax.axis_index("mode") * modes
    entries = table.shape[0] // 3

    @pl.when(step == 0)
    def _():
        per = des // LANES
        sides = []
        for ref in (low_ref, own_ref, high_ref):
            packed = ref[rows : rows + EXTRA, :].astype(f32)
            sides.append(packed[:per] + packed[per : 2 * per] + packed[2 * per : 3 * per])
        sides.append(jnp.zeros((entries - 3 * per, LANES), f32))
        for i, piece in enumerate(three_pieces(jnp.concatenate(sides, axis=0))):
            table[i * entries : (i + 1) * entries, :] = piece
        lower = iota((rows, LANES), 1) >= LANES // 2
        rim[...] = jnp.where(lower, low_ref[0:rows, :].astype(f32), high_ref[0:rows, :].astype(f32)).astype(bf16)
        node_ref[...] = jnp.zeros_like(node_ref)
        node_rim_ref[...] = jnp.zeros_like(node_rim_ref)
        diag_ref[...] = jnp.zeros_like(diag_ref)

    eig = column_of(eig_ref[...], mode_start, modes)
    weight = 2.0 * column_of(weight_ref[...], 0, modes)

    local = owner_ref[...] - (rank - 1) * des
    looked = dot(table[...], one_hot(LANES, local % LANES))
    looked = looked[:entries] + looked[entries : 2 * entries] + looked[2 * entries :]
    here = iota((entries, TILE), 0) == local // LANES
    elem_dir = jnp.sum(jnp.where(here, looked, 0.0), axis=0, keepdims=True)
    elem_mass = mass_ref_[...]

    rim_one_hot(conn_ref, rim_hot, nodes)
    shapes[...] = own_shapes[...].astype(f32) + dot(rim[...], rim_hot[...])
    for k in range(CORNERS):
        stacked[k * rows : (k + 1) * rows, :] = shapes[:, k * TILE : (k + 1) * TILE].astype(bf16)
    mass_q[...] = dot(mass_big[...], stacked[...])
    stiff_wide[...] = stiff_ref[...].astype(f32)

    for lane in range(TILE // LANES):
        cols = slice(lane * LANES, (lane + 1) * LANES)
        direction = elem_dir[:, cols]
        mass = elem_mass[:, cols]
        scaled = eig * mass
        power = jnp.zeros((modes, LANES), f32)
        for first in range(0, DOFS, 4):
            sums = [jnp.zeros((modes, LANES), f32) for _ in range(4)]
            for b in range(DOFS):
                c, k = b // CORNERS, b % CORNERS
                at = k * TILE + lane * LANES
                s = shapes[c * modes : (c + 1) * modes, at : at + LANES]
                for q in range(4):
                    sums[q] = sums[q] + stiff_wide[first + q, b : b + 1, cols] * s
            for q in range(4):
                c, k = (first + q) // CORNERS, (first + q) % CORNERS
                at = k * TILE + lane * LANES
                s = shapes[c * modes : (c + 1) * modes, at : at + LANES]
                base = k * rows + c * modes
                mq = mass_q[base : base + modes, cols]
                power = power + s * mq
                resid = sums[q] - scaled * mq
                force[c * modes : (c + 1) * modes, at : at + LANES] = (direction * resid).astype(bf16)
                resid_ref[base : base + modes, cols] = weight * resid
        power = power * mass
        power_ref[:, cols] = power
        diag_ref[...] += direction * power

    node_ref[...] += dot_nt(force[...], own_hot[...])
    node_rim_ref[...] += dot_nt(force[...], rim_hot[...])


def gather_modes(ref, c, modes, groups):
    rows = COMPS * modes
    return jnp.concatenate(
        [ref[g * rows + c * modes : g * rows + (c + 1) * modes, :] for g in range(groups)], axis=0
    )


def gram_kernel(modes, groups, node_ref, node_rim_ref, diag_ref, fields, rims, out_ref):
    mode_start = lax.axis_index("mode") * modes
    total = jnp.zeros((modes, groups * modes), f32)
    for c in range(COMPS):
        span = slice(c * modes, (c + 1) * modes)
        for part, parts in ((node_ref, fields), (node_rim_ref, rims)):
            exact = part[span, :]
            high = exact.astype(bf16)
            low = (exact - high.astype(f32)).astype(bf16)
            both = dot_nt(
                jnp.concatenate([high, low], axis=0), gather_modes(parts, c, modes, groups)
            )
            total = total + both[:modes] + both[modes:]
    out_ref[0:modes, :] = total
    diag = jnp.sum(diag_ref[...], axis=1, keepdims=True)
    mask = iota((modes, LANES), 0) == iota((modes, LANES), 1)
    out_ref[modes : modes + 8, :] = jnp.broadcast_to(
        jnp.sum(jnp.where(mask, diag, 0.0), axis=0, keepdims=True), (8, LANES)
    )


def energy_kernel(
    modes,
    groups,
    nodes,
    des,
    gram_ref,
    eig_ref,
    weight_ref,
    fields,
    rims,
    conn_ref,
    owner_ref,
    own_hot,
    resid_ref,
    power_ref,
    low_ref,
    own_ref,
    high_ref,
    deriv_ref,
    deriv,
    deriv_rim,
    factor,
    rim_hot,
    totals,
):
    step = pl.program_id(0)
    rows = COMPS * modes
    rank = lax.axis_index("dom")
    mode_start = lax.axis_index("mode") * modes

    @pl.when(step == 0)
    def _():
        total = gram_ref[0]
        for i in range(1, gram_ref.shape[0]):
            total = total + gram_ref[i]
        gram = total[:modes]
        mass_diag = column_of(total[modes : modes + 1], 0, modes)
        shape = (modes, groups * modes)
        mask = iota(shape, 0) + mode_start == iota(shape, 1)
        eig_row = eig_ref[...]
        spacing = column_of(eig_row, mode_start, modes) - eig_row
        combiner = jnp.where(
            mask, -0.5 * mass_diag, gram / jnp.where(mask, 1.0, spacing)
        ).astype(bf16)
        eig_deriv = jnp.sum(jnp.where(mask, gram, 0.0), axis=1, keepdims=True)
        small = iota((modes, modes), 0) == iota((modes, modes), 1)
        deriv_ref[...] = jnp.sum(jnp.where(small, eig_deriv, 0.0), axis=0, keepdims=True)
        factor[...] = jnp.broadcast_to(
            eig_deriv * column_of(weight_ref[...], 0, modes), factor.shape
        )
        for c in range(COMPS):
            span = slice(c * modes, (c + 1) * modes)
            deriv[span, :] = dot(combiner, gather_modes(fields, c, modes, groups)).astype(bf16)
            deriv_rim[span, :] = dot(combiner, gather_modes(rims, c, modes, groups)).astype(bf16)
        totals[...] = jnp.zeros_like(totals)

    rim_one_hot(conn_ref, rim_hot, nodes)
    moved = dot(deriv[...], own_hot[...]) + dot(deriv_rim[...], rim_hot[...])
    energies = []
    for lane in range(TILE // LANES):
        cols = slice(lane * LANES, (lane + 1) * LANES)
        total = -factor[...] * power_ref[:, cols]
        for k in range(CORNERS):
            at = k * TILE + lane * LANES
            for c in range(COMPS):
                base = k * rows + c * modes
                total = total + moved[c * modes : (c + 1) * modes, at : at + LANES] * resid_ref[
                    base : base + modes, cols
                ]
        energies.append(jnp.sum(total, axis=0, keepdims=True))
    energy = jnp.concatenate(energies, axis=1)
    local = owner_ref[...] - (rank - 1) * des
    entries = totals.shape[0]
    here = iota((entries, TILE), 0) == local // LANES
    spread = jnp.concatenate(
        [jnp.where(here, p.astype(f32), 0.0).astype(bf16) for p in three_pieces(energy)], axis=0
    )
    sums = dot_nt(spread, one_hot(LANES, local % LANES))
    totals[...] += sums[:entries] + sums[entries : 2 * entries] + sums[2 * entries :]

    @pl.when(step == pl.num_programs(0) - 1)
    def _():
        per = des // LANES
        for side, ref in enumerate((low_ref, own_ref, high_ref)):
            for i in range(per):
                at = side * per + i
                ref[:, i * LANES : (i + 1) * LANES] = totals[at : at + 1, :]


def neighbour(value, step):
    count = lax.axis_size("dom")
    pairs = [(i, i + step) for i in range(count) if 0 <= i + step < count]
    return lax.ppermute(value, "dom", pairs)


def from_all(value, axis, groups):
    size = len(groups[0])
    copies = jnp.broadcast_to(value[None], (size,) + value.shape)
    return lax.all_to_all(copies, axis, 0, 0, axis_index_groups=groups)


def whole(shape):
    return pl.BlockSpec(shape, lambda t: (0,) * len(shape))


def tiled(rows):
    return pl.BlockSpec((rows, TILE), lambda t: (0, t))


def params(mib):
    return pltpu.CompilerParams(vmem_limit_bytes=mib * MIB)


def cost(flops, bytes_):
    return pl.CostEstimate(flops=flops, bytes_accessed=bytes_, transcendentals=0)


def on_device(
    mode_shapes,
    eigenvalues,
    mode_weights,
    stiff_deriv,
    mass_ref,
    mass_scale,
    connectivity,
    design_owner,
    direction,
):
    modes, _, nodes = mode_shapes.shape
    elems = connectivity.shape[1]
    des = direction.shape[0]
    groups = lax.axis_size("mode")
    count = lax.axis_size("dom")
    total_modes = groups * modes
    rows = COMPS * modes
    big = CORNERS * rows
    tiles = elems // TILE
    wide = CORNERS * TILE
    entries = 16
    shaped = jax.ShapeDtypeStruct
    wide_tile = pl.BlockSpec((nodes, wide), lambda t: (0, t))
    shape_tile = pl.BlockSpec((rows, wide), lambda t: (0, t))

    field = jnp.transpose(mode_shapes, (1, 0, 2)).reshape(rows, nodes)
    fields = lax.all_gather(field, "mode", axis=0, tiled=True)
    eig_row = eigenvalues.reshape(1, total_modes)
    weight_row = mode_weights.reshape(1, modes)

    up, down, owner_row, mass_row = pl.pallas_call(
        functools.partial(pack_kernel, rows, des),
        grid=(1,),
        in_specs=[
            pl.BlockSpec((rows, LANES), lambda t: (0, 0)),
            pl.BlockSpec((rows, LANES), lambda t: (0, nodes // LANES - 1)),
            whole((des,)),
            whole((elems,)),
            whole((elems,)),
        ],
        out_specs=[whole((rows + EXTRA, LANES))] * 2 + [whole((1, elems))] * 2,
        out_shape=[shaped((rows + EXTRA, LANES), bf16)] * 2
        + [shaped((1, elems), jnp.int32), shaped((1, elems), f32)],
        name="pack",
    )(field, field, direction, design_owner, mass_scale)
    low, high = neighbour(up, 1), neighbour(down, -1)

    own_hot, own_shapes, mass_big = pl.pallas_call(
        functools.partial(prepare_kernel, modes, nodes),
        grid=(tiles,),
        in_specs=[tiled(CORNERS), whole((rows, nodes)), whole((DOFS, DOFS))],
        out_specs=[wide_tile, shape_tile, whole((big, big))],
        out_shape=[
            shaped((nodes, CORNERS * elems), bf16),
            shaped((rows, CORNERS * elems), bf16),
            shaped((big, big), bf16),
        ],
        compiler_params=params(24),
        cost_estimate=cost(4_000_000_000, 8_000_000),
        name="prepare",
    )(connectivity, field, mass_ref)

    upper = lax.broadcasted_iota(jnp.int32, (rows, LANES), 1) < LANES // 2
    rims = lax.all_gather(jnp.where(upper, high[:rows], low[:rows]), "mode", axis=0, tiled=True)

    resid, power, node, node_rim, diag = pl.pallas_call(
        functools.partial(forces_kernel, modes, nodes, des),
        grid=(tiles,),
        in_specs=[
            tiled(CORNERS),
            tiled(1),
            tiled(1),
            pl.BlockSpec((DOFS, DOFS, TILE), lambda t: (0, 0, t)),
            wide_tile,
            shape_tile,
            whole((rows + EXTRA, LANES)),
            whole((rows + EXTRA, LANES)),
            whole((rows + EXTRA, LANES)),
            whole((big, big)),
            whole((1, total_modes)),
            whole((1, modes)),
        ],
        out_specs=[
            tiled(big),
            tiled(modes),
            whole((rows, nodes)),
            whole((rows, LANES)),
            whole((modes, LANES)),
        ],
        out_shape=[
            shaped((big, elems), f32),
            shaped((modes, elems), f32),
            shaped((rows, nodes), f32),
            shaped((rows, LANES), f32),
            shaped((modes, LANES), f32),
        ],
        scratch_shapes=[
            pltpu.VMEM((3 * entries, LANES), bf16),
            pltpu.VMEM((rows, LANES), bf16),
            pltpu.VMEM((LANES, wide), bf16),
            pltpu.VMEM((rows, wide), f32),
            pltpu.VMEM((big, TILE), bf16),
            pltpu.VMEM((big, TILE), f32),
            pltpu.VMEM((DOFS, DOFS, TILE), f32),
            pltpu.VMEM((rows, wide), bf16),
        ],
        compiler_params=params(24),
        cost_estimate=cost(8_000_000_000, 8_000_000),
        name="forces",
    )(
        connectivity,
        owner_row,
        mass_row,
        stiff_deriv,
        own_hot,
        own_shapes,
        low,
        up,
        high,
        mass_big,
        eig_row,
        weight_row,
    )

    gram = pl.pallas_call(
        functools.partial(gram_kernel, modes, groups),
        out_shape=shaped((modes + 8, total_modes), f32),
        compiler_params=params(24),
        name="gram",
    )(node, node_rim, diag, fields, rims)

    gram = gram + lax.ppermute(gram, "dom", [(i, i ^ 1) for i in range(count)])
    grams = from_all(gram, "dom", [list(range(core, count, 2)) for core in range(2)])

    low_sum, own_sum, high_sum, eig_deriv = pl.pallas_call(
        functools.partial(energy_kernel, modes, groups, nodes, des),
        grid=(tiles,),
        in_specs=[
            whole(grams.shape),
            whole((1, total_modes)),
            whole((1, modes)),
            whole((groups * rows, nodes)),
            whole((groups * rows, LANES)),
            tiled(CORNERS),
            tiled(1),
            wide_tile,
            tiled(big),
            tiled(modes),
        ],
        out_specs=[whole((1, des))] * 3 + [whole((1, modes))],
        out_shape=[shaped((1, des), f32)] * 3 + [shaped((1, modes), f32)],
        scratch_shapes=[
            pltpu.VMEM((rows, nodes), bf16),
            pltpu.VMEM((rows, LANES), bf16),
            pltpu.VMEM((modes, LANES), f32),
            pltpu.VMEM((LANES, wide), bf16),
            pltpu.VMEM((entries, LANES), f32),
        ],
        compiler_params=params(24),
        name="energy",
    )(grams, eig_row, weight_row, fields, rims, connectivity, owner_row, own_hot, resid, power)

    owned = own_sum + neighbour(low_sum, -1) + neighbour(high_sum, 1)
    hess_vec = jnp.sum(from_all(owned, "mode", [list(range(groups))]), axis=0)
    return (hess_vec.reshape(des), eig_deriv.reshape(modes))


def solution(mesh):
    return jax.shard_map(
        on_device,
        mesh=mesh,
        in_specs=(
            P("mode", None, "dom"),
            P(),
            P("mode"),
            P(None, None, "dom"),
            P(),
            P("dom"),
            P(None, "dom"),
            P("dom"),
            P("dom"),
        ),
        out_specs=(P("dom"), P("mode")),
        check_vma=False,
    )
```

time: 101 us -> 122 us (1.21)
  blocking collectives: 0 us -> 36 us
  starting transfers between devices: 41.2 us -> 12.1 us
  between operations: 0.81 us -> 14.2 us
  waiting for transfers between devices: 17.7 us -> 6.62 us
  local copies, waits for them, and re-layouts: 8.22 us -> 17.4 us
  Pallas kernels: 31.3 us -> 34.8 us
    all_to_all x0 -> x2, blocking collectives: none -> 21.8 us  [from_all(): return lax.all_to_all(copies, axis, 0, 0, axis_index_groups=groups)]
    ppermute x16 -> x1, starting transfers between devices: 21.8 us -> 0.09 us  [on_device(): gram = gram + lax.ppermute(gram, 'dom', [(i, i ^ 1) for i in range(count)])]
    all_gather x0 -> x1, blocking collectives: none -> 14.2 us  [on_device(): lax.all_gather(jnp.where(upper, high[:rows], low[:rows]), 'mode', axis=0,...]
    unnamed x16 -> x32, local copies, waits for them, and re-layouts: 5.22 us -> 17.4 us
    ppermute x16 -> x1, waiting for transfers between devices: 11.4 us -> 1.18 us  [on_device(): gram = gram + lax.ppermute(gram, 'dom', [(i, i ^ 1) for i in range(count)])]
    ppermute x6 -> x4, starting transfers between devices: 19.4 us -> 12 us  [neighbour(): return lax.ppermute(value, 'dom', pairs)]
    pallas_call x1 -> x3, Pallas kernels: 0.78 us -> 8.15 us  [the longest x1 5.86 us: on_device(): pl.pallas_call(functools.partial(prepare_kernel, modes, nodes), grid=(til...]
    pallas_call x1, Pallas kernels: 23.9 us -> 19.5 us  [on_device(): pl.pallas_call(functools.partial(forces_kernel, modes, nodes, des), grid=...]
  transfers between devices with their start and end apart: 22 -> 6, of which waited for: 11 -> 2; matrix products, arithmetic and copies ran while one was open for 2% -> 0% of each run, Pallas kernels for 24% -> 22%
where the time goes in v2:
time: 122 us
  blocking collectives  36 us (30%)
  Pallas kernels  34.8 us (29%)
  local copies, waits for them, and re-layouts  17.4 us (14%)
  between operations  14.2 us (12%)
  starting transfers between devices  12.1 us (10%)
  waiting for transfers between devices  6.62 us (5%)
    all_to_all x2, blocking collectives, from_all(): return lax.all_to_all(copies, axis, 0, 0, axis_index_groups=groups)  21.8 us
    pallas_call x1, Pallas kernels, on_device(): pl.pallas_call(functools.partial(forces_kernel, modes, nodes, des), grid=...  19.5 us
    unnamed x32, local copies, waits for them, and re-layouts  17.4 us
    all_gather x1, blocking collectives, on_device(): lax.all_gather(jnp.where(upper, high[:rows], low[:rows]), 'mode', axis=0,...  14.2 us
    ppermute x4, starting transfers between devices, neighbour(): return lax.ppermute(value, 'dom', pairs)  12 us
    pallas_call x1, Pallas kernels, on_device(): pl.pallas_call(functools.partial(energy_kernel, modes, groups, nodes, des...  7.1 us
    pallas_call x1, Pallas kernels, on_device(): pl.pallas_call(functools.partial(prepare_kernel, modes, nodes), grid=(til...  5.86 us
    ppermute x4, waiting for transfers between devices, neighbour(): return lax.ppermute(value, 'dom', pairs)  4.76 us
  transfers between devices with their start and end apart: 6, of which 2 were waited for; matrix products, arithmetic and copies ran while one was open for 0% of the time, Pallas kernels for 22%

profile of v2, /device:TPU:8, one launch (start us, length us, event | category | flops | bytes accessed | tf_op | source)
XLA Modules:
  0.0 121.8 jit_solution(16607426575023526946)
XLA Ops:
  7.2 0.0 all-gather.2.cloned.1.call-start
  7.2 0.7 all-gather.2.cloned.1.call-update
  7.9 1.5 %pack.1 = (bf16[208,128]{1,0:T(8,128)(2,1)}, bf16[208,128]{1,0:T(8,128)(2,1)}, s32[1,1536]{1,0:T(1,128)}, f32[1,1536]{1,0:T(1,128)}) custom-call(bf16[192,1024]{1,0:T(8,128)(2,1)} %bitcast.7, bf16[192,1024]{1,0:T(8,128)(2,1)} %bitcast.8, f32[640]{0:T(1024)} %dir_ref.1, s32[1536]{0:T(1024)} %owner_ref.1, f32[1536]{0:T(1024)} %mass_ref_.1), custom_call_target="tpu_custom_call" | custom-call | tf_op jit(solution)/shard_map/pack/pallas_call | solution.py:375
  9.4 1.9 %collective-permute-start = (bf16[208,128]{1,0:T(8,128)(2,1)}, bf16[208,128]{1,0:T(8,128)(2,1)S(1)}, u32[]{:S(2)}, u32[]{:S(2)}) collective-permute-start(bf16[208,128]{1,0:T(8,128)(2,1)} %get-tuple-element.22.own_ref), channel_id=1, source_target_pairs={{0,4},{4,8},{8,12},{12,16},{16,20},{20,24},{24,28},{28,32},{32,36}... | collective-permute-start | bytes 159752 | tf_op jit(solution)/shard_map/ppermute | solution.py:319
  11.3 5.8 %collective-permute-start.1 = (bf16[208,128]{1,0:T(8,128)(2,1)}, bf16[208,128]{1,0:T(8,128)(2,1)S(1)}, u32[]{:S(2)}, u32[]{:S(2)}) collective-permute-start(bf16[208,128]{1,0:T(8,128)(2,1)} %get-tuple-element.23), channel_id=1, source_target_pairs={{4,0},{8,4},{12,8},{16,12},{20,16},{24,20},{28,24},{32,28},{36,32}... | collective-permute-start | bytes 159752 | tf_op jit(solution)/shard_map/ppermute | solution.py:319
  17.1 0.0 copy-start.6
  17.1 1.0 copy-done.6
  18.1 0.7 copy-done.7
  18.8 0.7 copy-done.14
  19.5 0.0 copy-start.13
  19.5 5.9 %prepare.1 = (bf16[1024,6144]{1,0:T(8,128)(2,1)S(1)}, bf16[192,6144]{1,0:T(8,128)(2,1)S(1)}, bf16[768,768]{1,0:T(8,128)(2,1)S(1)}) custom-call(s32[4,1536]{1,0:T(4,128)S(1)} %copy-done.7, bf16[192,1024]{1,0:T(8,128)(2,1)S(1)} %bitcast.9, bf16[24,24]{1,0:T(8,128)(2,1)S(1)} %copy-done.14), custom_call_target="tpu_custom_call" | custom-call | flops 4000000000 | bytes 8000000 | tf_op jit(solution)/shard_map/prepare/pallas_call | solution.py:392
  25.4 0.0 collective-permute-done.low_ref
  25.4 0.0 collective-permute-done.1.high_ref
  25.5 14.2 %all_gather.7.rims = bf16[768,128]{1,0:T(8,128)(2,1)S(1)} all-gather(bf16[192,128]{1,0:T(8,128)(2,1)S(1)} %slice_select_fusion), channel_id=1, replica_groups=mesh['dom'=32,'mode'=4] {'mode'}, dimensions={0}, use_global_device_ids=true | all-gather | bytes 245760 | tf_op jit(solution)/shard_map/all_gather | solution.py:408
  39.7 0.0 copy-start.8
  39.8 19.5 %forces.1 = (f32[768,1536]{1,0:T(8,128)S(1)}, f32[32,1536]{1,0:T(8,128)S(1)}, f32[192,1024]{1,0:T(8,128)S(1)}, f32[192,128]{1,0:T(8,128)S(1)}, f32[32,128]{1,0:T(8,128)S(1)}) custom-call(s32[4,1536]{1,0:T(4,128)S(1)} %copy-done.7, s32[1,1536]{1,0:T(1,128)S(1)} %copy-done.9, f32[1,1536]{1,0:T(1,128)S(1)} %copy-done.15, bf16[24,24,1536]{2,1,0:T(8,128)(2,1)S(1)} %copy-done.12, ...), custom_call_target="tpu_custom_call" | custom-call | flops 8000000000 | bytes 8000000 | tf_op jit(solution)/shard_map/forces/pallas_call | solution.py:410
  59.3 4.5 %copy-done = bf16[1024,6144]{1,0:T(8,128)(2,1)} copy-done((bf16[1024,6144]{1,0:T(8,128)(2,1)}, bf16[1024,6144]{1,0:T(8,128)(2,1)S(1)}, u32[]{:S(2)}) %copy-start) | copy-done | bytes 12582936
  63.8 2.1 %copy-done.4 = f32[768,1536]{1,0:T(8,128)} copy-done((f32[768,1536]{1,0:T(8,128)}, f32[768,1536]{1,0:T(8,128)S(1)}, u32[]{:S(2)}) %copy-start.4) | copy-done | bytes 4718616
  65.9 1.4 %copy-done.2 = bf16[768,1024]{1,0:T(8,128)(2,1)S(1)} copy-done((bf16[768,1024]{1,0:T(8,128)(2,1)S(1)}, bf16[768,1024]{1,0:T(8,128)(2,1)}, u32[]{:S(2)}) %copy-start.2) | copy-done | bytes 1572888
  67.3 0.8 gram.1
  68.1 0.1 collective-permute-start.2
  68.2 1.2 collective-permute-done.2
  69.4 12.5 %all_to_all.10.gram_ref = f32[16,40,128]{2,1,0:T(8,128)S(1)} all-to-all(f32[16,40,128]{2,1,0:T(8,128)S(1)} %broadcast_in_dim.6), channel_id=1, replica_groups={{0,8,16,24,32,40,48,56,64,72,80,88,96,104,112,120},{4,12,20,28,36,44,52..., dimensions={0} | all-to-all | bytes 655360 | tf_op jit(solution)/shard_map/all_to_all | solution.py:325
  82.0 4.6 %copy-done.1 = bf16[1024,6144]{1,0:T(8,128)(2,1)S(1)} copy-done((bf16[1024,6144]{1,0:T(8,128)(2,1)S(1)}, bf16[1024,6144]{1,0:T(8,128)(2,1)}, u32[]{:S(2)}) %copy-start.1) | copy-done | bytes 12582936
  86.5 2.3 %copy-done.5 = f32[768,1536]{1,0:T(8,128)S(1)} copy-done((f32[768,1536]{1,0:T(8,128)S(1)}, f32[768,1536]{1,0:T(8,128)}, u32[]{:S(2)}) %copy-start.5) | copy-done | bytes 4718616
  88.9 7.1 %energy.1 = (f32[1,640]{1,0:T(1,128)S(1)}, f32[1,640]{1,0:T(1,128)S(1)}, f32[1,640]{1,0:T(1,128)S(1)}, f32[1,32]{1,0:T(1,128)}) custom-call(f32[16,40,128]{2,1,0:T(8,128)S(1)} %all_to_all.10.gram_ref, f32[1,128]{1,0:T(1,128)S(1)} %bitcast.11, f32[1,32]{1,0:T(1,128)S(1)} %bitcast.13, bf16[768,1024]{1,0:T(8,128)(2,1)S(1)} %copy-done.3, ...), custom_call_target="tpu_custom_call" | custom-call | tf_op jit(solution)/shard_map/energy/pallas_call | solution.py:479
  96.0 2.1 %collective-permute-start.3 = (f32[1,640]{1,0:T(1,128)S(1)}, f32[1,640]{1,0:T(1,128)S(1)}, u32[]{:S(2)}, u32[]{:S(2)}) collective-permute-start(f32[1,640]{1,0:T(1,128)S(1)} %get-tuple-element.31), channel_id=1, source_target_pairs={{4,0},{8,4},{12,8},{16,12},{20,16},{24,20},{28,24},{32,28},{36,32}... | collective-permute-start | bytes 7688 | tf_op jit(solution)/shard_map/ppermute | solution.py:319
  98.1 2.2 %collective-permute-start.4 = (f32[1,640]{1,0:T(1,128)S(1)}, f32[1,640]{1,0:T(1,128)S(1)}, u32[]{:S(2)}, u32[]{:S(2)}) collective-permute-start(f32[1,640]{1,0:T(1,128)S(1)} %get-tuple-element.32), channel_id=1, source_target_pairs={{0,4},{4,8},{8,12},{12,16},{16,20},{20,24},{24,28},{28,32},{32,36}... | collective-permute-start | bytes 7688 | tf_op jit(solution)/shard_map/ppermute | solution.py:319
  100.3 0.0 collective-permute-done.3
  100.3 4.8 %collective-permute-done.4 = f32[1,640]{1,0:T(1,128)S(1)} collective-permute-done((f32[1,640]{1,0:T(1,128)S(1)}, f32[1,640]{1,0:T(1,128)S(1)}, u32[]{:S(2)}, u32[]{:S(2)}) %collective-permute-start.4) | collective-permute-done | bytes 2592 | tf_op jit(solution)/shard_map/ppermute | solution.py:319
  105.1 9.2 %all_to_all.11 = f32[4,1,640]{2,1,0:T(1,128)S(1)} all-to-all(f32[4,1,640]{2,1,0:T(1,128)S(1)} %broadcast_in_dim.16), channel_id=1, replica_groups={{0,1,2,3},{4,5,6,7},{8,9,10,11},{12,13,14,15},{16,17,18,19},{20,21,22,2..., dimensions={0} | all-to-all | bytes 20480 | tf_op jit(solution)/shard_map/all_to_all | solution.py:325
  114.3 0.6 reduce_sum.9
  (28 shorter events, 0.1 us)
Async XLA Ops:
  7.2 58.7 %all-gather.2.cloned.1.call-start = ((), (), s32[]{:S(2)}) async-start(), calls=%async_computation.2 | async-start | bytes 1966080 | tf_op jit(solution)/shard_map/all_gather | solution.py:371
  9.4 16.0 %collective-permute-start = (bf16[208,128]{1,0:T(8,128)(2,1)}, bf16[208,128]{1,0:T(8,128)(2,1)S(1)}, u32[]{:S(2)}, u32[]{:S(2)}) collective-permute-start(bf16[208,128]{1,0:T(8,128)(2,1)} %get-tuple-element.22.own_ref), channel_id=1, source_target_pairs={{0,4},{4,8},{8,12},{12,16},{16,20},{20,24},{24,28},{28,32},{32,36}... | collective-permute-start | bytes 159752 | tf_op jit(solution)/shard_map/ppermute | solution.py:319
  11.3 14.1 %collective-permute-start.1 = (bf16[208,128]{1,0:T(8,128)(2,1)}, bf16[208,128]{1,0:T(8,128)(2,1)S(1)}, u32[]{:S(2)}, u32[]{:S(2)}) collective-permute-start(bf16[208,128]{1,0:T(8,128)(2,1)} %get-tuple-element.23), channel_id=1, source_target_pairs={{4,0},{8,4},{12,8},{16,12},{20,16},{24,20},{28,24},{32,28},{36,32}... | collective-permute-start | bytes 159752 | tf_op jit(solution)/shard_map/ppermute | solution.py:319
  17.1 1.0 copy-start.6
  18.1 0.7 copy-start.7
  18.8 0.7 copy-start.14
  19.5 20.2 %copy-start.9 = (s32[1,1536]{1,0:T(1,128)S(1)}, s32[1,1536]{1,0:T(1,128)}, u32[]{:S(2)}) copy-start(s32[1,1536]{1,0:T(1,128)} %get-tuple-element.18.owner_ref) | copy-start | bytes 18436
  19.5 20.2 %copy-start.10 = (f32[128]{0:T(128)S(1)}, f32[128]{0:T(128)}, u32[]{:S(2)}) copy-start(f32[128]{0:T(128)} %param.10) | copy-start | bytes 1540
  19.5 20.2 %copy-start.11 = (f32[32]{0:T(128)S(1)}, f32[32]{0:T(128)}, u32[]{:S(2)}) copy-start(f32[32]{0:T(128)} %param.11) | copy-start | bytes 388
  19.5 20.2 %copy-start.12 = (bf16[24,24,1536]{2,1,0:T(8,128)(2,1)S(1)}, bf16[24,24,1536]{2,1,0:T(8,128)(2,1)}, u32[]{:S(2)}) copy-start(bf16[24,24,1536]{2,1,0:T(8,128)(2,1)} %stiff_ref.1) | copy-start | bytes 5308420
  19.5 20.2 %copy-start.13 = (bf16[208,128]{1,0:T(8,128)(2,1)S(1)}, bf16[208,128]{1,0:T(8,128)(2,1)}, u32[]{:S(2)}) copy-start(bf16[208,128]{1,0:T(8,128)(2,1)} %get-tuple-element.22.own_ref) | copy-start | bytes 159748
  19.5 20.2 %copy-start.15 = (f32[1,1536]{1,0:T(1,128)S(1)}, f32[1,1536]{1,0:T(1,128)}, u32[]{:S(2)}) copy-start(f32[1,1536]{1,0:T(1,128)} %get-tuple-element.19.mass_ref_) | copy-start | bytes 18436
  39.7 42.2 %copy-start.8 = (s32[4,1536]{1,0:T(4,128)S(1)}, s32[4,1536]{1,0:T(4,128)}, u32[]{:S(2)}) copy-start(s32[4,1536]{1,0:T(4,128)} %conn_ref.5) | copy-start | bytes 73732
  59.3 4.5 %copy-start = (bf16[1024,6144]{1,0:T(8,128)(2,1)}, bf16[1024,6144]{1,0:T(8,128)(2,1)S(1)}, u32[]{:S(2)}) copy-start(bf16[1024,6144]{1,0:T(8,128)(2,1)S(1)} %get-tuple-element.20.own_hot) | copy-start | bytes 37748740
  63.8 2.1 %copy-start.4 = (f32[768,1536]{1,0:T(8,128)}, f32[768,1536]{1,0:T(8,128)S(1)}, u32[]{:S(2)}) copy-start(f32[768,1536]{1,0:T(8,128)S(1)} %get-tuple-element.28.resid_ref) | copy-start | bytes 14155780
  65.9 1.4 %copy-start.2 = (bf16[768,1024]{1,0:T(8,128)(2,1)S(1)}, bf16[768,1024]{1,0:T(8,128)(2,1)}, u32[]{:S(2)}) copy-start(bf16[768,1024]{1,0:T(8,128)(2,1)} %all-gather.2.cloned.1.call-done.fields) | copy-start | bytes 4718596
  67.3 14.6 %copy-start.3 = (bf16[768,1024]{1,0:T(8,128)(2,1)S(1)}, bf16[768,1024]{1,0:T(8,128)(2,1)}, u32[]{:S(2)}) copy-start(bf16[768,1024]{1,0:T(8,128)(2,1)} %all-gather.2.cloned.1.call-done.fields) | copy-start | bytes 4718596
  68.1 1.3 %collective-permute-start.2 = (f32[40,128]{1,0:T(8,128)S(1)}, f32[40,128]{1,0:T(8,128)S(1)}, u32[]{:S(2)}, u32[]{:S(2)}) collective-permute-start(f32[40,128]{1,0:T(8,128)S(1)} %gram.1), channel_id=1, source_target_pairs={{0,4},{4,0},{8,12},{12,8},{16,20},{20,16},{24,28},{28,24},{32,36},... | collective-permute-start | bytes 61448 | tf_op jit(solution)/shard_map/ppermute | solution.py:476
  82.0 4.6 %copy-start.1 = (bf16[1024,6144]{1,0:T(8,128)(2,1)S(1)}, bf16[1024,6144]{1,0:T(8,128)(2,1)}, u32[]{:S(2)}) copy-start(bf16[1024,6144]{1,0:T(8,128)(2,1)} %copy-done) | copy-start | bytes 37748740
  86.5 2.3 %copy-start.5 = (f32[768,1536]{1,0:T(8,128)S(1)}, f32[768,1536]{1,0:T(8,128)}, u32[]{:S(2)}) copy-start(f32[768,1536]{1,0:T(8,128)} %copy-done.4) | copy-start | bytes 14155780
  96.0 4.3 %collective-permute-start.3 = (f32[1,640]{1,0:T(1,128)S(1)}, f32[1,640]{1,0:T(1,128)S(1)}, u32[]{:S(2)}, u32[]{:S(2)}) collective-permute-start(f32[1,640]{1,0:T(1,128)S(1)} %get-tuple-element.31), channel_id=1, source_target_pairs={{4,0},{8,4},{12,8},{16,12},{20,16},{24,20},{28,24},{32,28},{36,32}... | collective-permute-start | bytes 7688 | tf_op jit(solution)/shard_map/ppermute | solution.py:319
  98.1 7.0 %collective-permute-start.4 = (f32[1,640]{1,0:T(1,128)S(1)}, f32[1,640]{1,0:T(1,128)S(1)}, u32[]{:S(2)}, u32[]{:S(2)}) collective-permute-start(f32[1,640]{1,0:T(1,128)S(1)} %get-tuple-element.32), channel_id=1, source_target_pairs={{0,4},{4,8},{8,12},{12,16},{16,20},{20,24},{24,28},{28,32},{32,36}... | collective-permute-start | bytes 7688 | tf_op jit(solution)/shard_map/ppermute | solution.py:319
Sparse Core Ops, SparseCore 0:
  9.7 30.6 all-gather.1

commit v3 on v0

v3 whole, which is shorter than its diff:
```python
import functools

import jax
import jax.numpy as jnp
from jax import lax
from jax.experimental import pallas as pl
from jax.experimental.pallas import tpu as pltpu
from jax.sharding import PartitionSpec as P

H = 32
COMPS = 6
CORNERS = 4
DOFS = 24
TILE = 256
LANES = 128
EXTRA = 16
SUBS = 8
MIB = 1 << 20
f32, bf16 = jnp.float32, jnp.bfloat16


def dot(a, b):
    return lax.dot_general(a, b, (((1,), (0,)), ((), ())), preferred_element_type=f32)


def dot_nt(a, b):
    return lax.dot_general(a, b, (((1,), (1,)), ((), ())), preferred_element_type=f32)


def iota(shape, dim):
    return lax.broadcasted_iota(jnp.int32, shape, dim)


def one_hot(rows, index):
    hit = iota((rows, index.shape[1]), 0) == index
    return jnp.where(hit, 1.0, 0.0).astype(bf16)


def three_pieces(x):
    first = x.astype(bf16)
    rest = x - first.astype(f32)
    second = rest.astype(bf16)
    third = (rest - second.astype(f32)).astype(bf16)
    return first, second, third


def column_of(row, offset, count):
    n = row.shape[1]
    mask = iota((count, n), 1) == iota((count, n), 0) + offset
    return jnp.sum(jnp.where(mask, row, 0.0), axis=1, keepdims=True)


def pack_kernel(rows, des, first_ref, last_ref, dir_ref, up_ref, down_ref):
    up_ref[0:rows, :] = last_ref[...]
    down_ref[0:rows, :] = first_ref[...]
    table = jnp.concatenate(
        [dir_ref[i * LANES : (i + 1) * LANES].reshape(1, LANES) for i in range(des // LANES)], axis=0
    )
    pieces = [p.astype(f32) for p in three_pieces(table)]
    pad = jnp.zeros((EXTRA - 3 * (des // LANES), LANES), f32)
    packed = jnp.concatenate(pieces + [pad], axis=0).astype(bf16)
    up_ref[rows : rows + EXTRA, :] = packed
    down_ref[rows : rows + EXTRA, :] = packed


def fill_one_hot(conn_ref, at, hot, nodes):
    for k in range(CORNERS):
        index = conn_ref[k : k + 1, pl.ds(at, TILE)]
        index = jnp.where(index < H, index + (nodes + LANES - H), index - H)
        hot[:, k * TILE : (k + 1) * TILE] = one_hot(nodes + LANES, index)


def rows_of(flat_ref, row_ref):
    for i in range(row_ref.shape[1] // LANES):
        span = slice(i * LANES, (i + 1) * LANES)
        row_ref[:, span] = flat_ref[span].reshape(1, LANES)


def expand_mass(ref):
    size = DOFS * SUBS
    spread = jnp.where(iota((size, DOFS), 0) // SUBS == iota((size, DOFS), 1), 1.0, 0.0).astype(bf16)
    full = dot_nt(dot(spread, ref).astype(bf16), spread)
    same = iota((size, size), 0) % SUBS == iota((size, size), 1) % SUBS
    return jnp.where(same, full, 0.0).astype(bf16)


def forces_kernel(
    modes,
    nodes,
    des,
    elems,
    conn_hbm,
    owner_hbm,
    mass_hbm,
    stiff_hbm,
    field_hbm,
    ref_hbm,
    eig_hbm,
    weight_hbm,
    low_ref,
    own_ref,
    high_ref,
    resid_ref,
    power_ref,
    node_ref,
    conn,
    owner_row,
    eig_row,
    weight_row,
    owner_flat,
    mass_flat,
    stiff,
    field,
    ref,
    sems,
    stiff_sems,
    mass_row,
    dir_row,
    mass_big,
    hot,
    shapes,
    mass_q,
    stiff_wide,
    force,
    sums_t,
):
    rows = COMPS * modes
    tiles = elems // TILE
    rank = lax.axis_index("dom")
    mode_start = lax.axis_index("mode") * modes
    entries = 16
    small = [
        pltpu.make_async_copy(source, target, sems.at[i])
        for i, (source, target) in enumerate(
            (
                (ref_hbm, ref),
                (conn_hbm, conn),
                (field_hbm, field.at[:, pl.ds(0, nodes)]),
                (owner_hbm, owner_flat),
                (mass_hbm, mass_flat),
                (eig_hbm, eig_row),
                (weight_hbm, weight_row),
            )
        )
    ]

    def stiff_copy(t):
        cols = pl.ds(pl.multiple_of(t * TILE, TILE), TILE)
        return pltpu.make_async_copy(stiff_hbm.at[:, :, cols], stiff.at[t], stiff_sems.at[t])

    for copy in small:
        copy.start()
    for t in range(tiles):
        stiff_copy(t).start()

    per = des // LANES
    sides = []
    for ref_ in (low_ref, own_ref, high_ref):
        packed = ref_[rows : rows + EXTRA, :].astype(f32)
        sides.append(packed[:per] + packed[per : 2 * per] + packed[2 * per : 3 * per])
    sides.append(jnp.zeros((entries - 3 * per, LANES), f32))
    table = jnp.concatenate(three_pieces(jnp.concatenate(sides, axis=0)), axis=0)
    lower = iota((rows, LANES), 1) >= LANES // 2
    field[:, nodes : nodes + LANES] = jnp.where(
        lower, low_ref[0:rows, :].astype(f32), high_ref[0:rows, :].astype(f32)
    ).astype(bf16)
    sums_t[...] = jnp.zeros_like(sums_t)
    for copy in small:
        copy.wait()
    mass_big[...] = expand_mass(ref[...])
    rows_of(owner_flat, owner_row)
    rows_of(mass_flat, mass_row)
    eig = column_of(eig_row[...], mode_start, modes)
    weight = 2.0 * column_of(weight_row[...], 0, modes)
    local = owner_row[...] - (rank - 1) * des
    looked = dot(table, one_hot(LANES, local % LANES))
    looked = looked[:entries] + looked[entries : 2 * entries] + looked[2 * entries :]
    here = iota((entries, elems), 0) == local // LANES
    dir_row[...] = jnp.sum(jnp.where(here, looked, 0.0), axis=0, keepdims=True)

    @pl.loop(0, tiles)
    def _(t):
        at = pl.multiple_of(t * TILE, TILE)
        elem_dir = dir_row[:, pl.ds(at, TILE)]
        elem_mass = mass_row[:, pl.ds(at, TILE)]
        fill_one_hot(conn, at, hot, nodes)
        shapes[...] = dot(field[...], hot[...])
        for g in range(modes // SUBS):
            stacked = [
                shapes[
                    (b // CORNERS) * modes + g * SUBS : (b // CORNERS) * modes + (g + 1) * SUBS,
                    (b % CORNERS) * TILE : (b % CORNERS + 1) * TILE,
                ]
                for b in range(DOFS)
            ]
            mass_q[g] = dot(mass_big[...], jnp.concatenate(stacked, axis=0).astype(bf16))
        stiff_copy(t).wait()
        stiff_wide[...] = stiff[t].astype(f32)

        for lane in range(TILE // LANES):
            cols = slice(lane * LANES, (lane + 1) * LANES)
            at_lane = pl.multiple_of(at + lane * LANES, LANES)
            direction = elem_dir[:, cols]
            mass = elem_mass[:, cols]
            scaled = eig * mass
            dir_mass = direction * mass
            power = jnp.zeros((modes, LANES), f32)
            for first in range(0, DOFS, 4):
                sums = [jnp.zeros((modes, LANES), f32) for _ in range(4)]
                for b in range(DOFS):
                    c, k = b // CORNERS, b % CORNERS
                    col = k * TILE + lane * LANES
                    s = shapes[c * modes : (c + 1) * modes, col : col + LANES]
                    for q in range(4):
                        sums[q] = sums[q] + stiff_wide[first + q, b : b + 1, cols] * s
                for q in range(4):
                    c, k = (first + q) // CORNERS, (first + q) % CORNERS
                    col = k * TILE + lane * LANES
                    s = shapes[c * modes : (c + 1) * modes, col : col + LANES]
                    base = k * rows + c * modes
                    mq = jnp.concatenate(
                        [
                            mass_q[g, (first + q) * SUBS : (first + q + 1) * SUBS, cols]
                            for g in range(modes // SUBS)
                        ],
                        axis=0,
                    )
                    power = power + s * mq
                    span = slice(c * modes, (c + 1) * modes)
                    force[span, col : col + LANES] = (direction * sums[q]).astype(bf16)
                    span = slice(rows + c * modes, rows + (c + 1) * modes)
                    force[span, col : col + LANES] = (dir_mass * mq).astype(bf16)
                    resid_ref[base : base + modes, pl.ds(at_lane, LANES)] = weight * (
                        sums[q] - scaled * mq
                    )
            power_ref[:, pl.ds(at_lane, LANES)] = power * mass

        sums_t[...] += dot_nt(hot[...], force[...])

    for i in range((nodes + LANES) // LANES):
        span = slice(i * LANES, (i + 1) * LANES)
        for part in range(2 * rows // LANES):
            node_ref[part * LANES : (part + 1) * LANES, span] = sums_t[
                span, part * LANES : (part + 1) * LANES
            ].T


def gather_modes(refs, c, modes):
    return jnp.concatenate([r[c * modes : (c + 1) * modes, :] for r in refs], axis=0)


def gram_kernel(modes, groups, nodes, node_ref, eig_ref, *refs):
    fields, rims, out_ref = refs[:groups], refs[groups : 2 * groups], refs[2 * groups]
    rows = COMPS * modes
    eig = column_of(eig_ref[...], lax.axis_index("mode") * modes, modes)
    grams = [jnp.zeros((modes, groups * modes), f32) for _ in range(2)]
    for c in range(COMPS):
        for cols, parts in ((slice(0, nodes), fields), (slice(nodes, nodes + LANES), rims)):
            pieces = []
            for kind in range(2):
                base = kind * rows + c * modes
                pieces += three_pieces(node_ref[base : base + modes, cols])
            each = dot_nt(jnp.concatenate(pieces, axis=0), gather_modes(parts, c, modes))
            each = [each[i * modes : (i + 1) * modes] for i in range(6)]
            grams = [grams[k] + (each[3 * k] + (each[3 * k + 1] + each[3 * k + 2])) for k in range(2)]
    stiff_gram, mass_gram = grams
    out_ref[0:modes, :] = stiff_gram - eig * mass_gram
    mask = iota(mass_gram.shape, 0) == iota(mass_gram.shape, 1)
    out_ref[modes : modes + 8, :] = jnp.broadcast_to(
        jnp.sum(jnp.where(mask, mass_gram, 0.0), axis=0, keepdims=True), (8, LANES)
    )


def energy_kernel(modes, groups, nodes, des, elems, gram_ref, eig_ref, weight_ref, *refs):
    fields, rims, refs = refs[:groups], refs[groups : 2 * groups], refs[2 * groups :]
    conn_ref, owner_row, resid_ref, power_ref = refs[:4]
    low_ref, own_ref, high_ref, deriv_ref = refs[4:8]
    deriv, factor, hot, totals = refs[8:]
    rows = COMPS * modes
    rank = lax.axis_index("dom")
    mode_start = lax.axis_index("mode") * modes

    total = gram_ref[0]
    for i in range(1, gram_ref.shape[0]):
        total = total + gram_ref[i]
    gram = total[:modes]
    mass_diag = column_of(total[modes : modes + 1], 0, modes)
    shape = (modes, groups * modes)
    mask = iota(shape, 0) == iota(shape, 1)
    eig_rows = jnp.broadcast_to(eig_ref[...], (8, LANES))
    turned = pltpu.roll(eig_rows, lax.rem(LANES - mode_start, LANES), 1)[0:1]
    spacing = column_of(turned, 0, modes) - turned
    combiner = jnp.where(mask, -0.5 * mass_diag, gram / jnp.where(mask, 1.0, spacing)).astype(bf16)
    diagonal = jnp.where(mask, gram, 0.0)
    deriv_ref[...] = jnp.sum(diagonal, axis=0, keepdims=True)[:, :modes]
    eig_deriv = jnp.sum(diagonal, axis=1, keepdims=True)
    factor[...] = jnp.broadcast_to(eig_deriv * column_of(weight_ref[...], 0, modes), factor.shape)
    for c in range(COMPS):
        span = slice(c * modes, (c + 1) * modes)
        deriv[span, 0:nodes] = dot(combiner, gather_modes(fields, c, modes)).astype(bf16)
        deriv[span, nodes : nodes + LANES] = dot(combiner, gather_modes(rims, c, modes)).astype(bf16)
    totals[...] = jnp.zeros_like(totals)

    @pl.loop(0, elems // TILE)
    def _(t):
        at = pl.multiple_of(t * TILE, TILE)
        fill_one_hot(conn_ref, at, hot, nodes)
        moved = dot(deriv[...], hot[...])
        energies = []
        for lane in range(TILE // LANES):
            cols = pl.ds(pl.multiple_of(at + lane * LANES, LANES), LANES)
            total = -factor[...] * power_ref[:, cols]
            for k in range(CORNERS):
                col = k * TILE + lane * LANES
                for c in range(COMPS):
                    base = k * rows + c * modes
                    total = total + moved[
                        c * modes : (c + 1) * modes, col : col + LANES
                    ] * resid_ref[base : base + modes, cols]
            energies.append(jnp.sum(total, axis=0, keepdims=True))
        energy = jnp.concatenate(energies, axis=1)
        local = owner_row[:, pl.ds(at, TILE)] - (rank - 1) * des
        entries = totals.shape[0]
        here = iota((entries, TILE), 0) == local // LANES
        spread = jnp.concatenate(
            [jnp.where(here, p.astype(f32), 0.0).astype(bf16) for p in three_pieces(energy)], axis=0
        )
        sums = dot_nt(spread, one_hot(LANES, local % LANES))
        totals[...] += sums[:entries] + sums[entries : 2 * entries] + sums[2 * entries :]

    per = des // LANES
    for side, ref in enumerate((low_ref, own_ref, high_ref)):
        for i in range(per):
            at = side * per + i
            ref[:, i * LANES : (i + 1) * LANES] = totals[at : at + 1, :]


def neighbour(value, step):
    count = lax.axis_size("dom")
    pairs = [(i, i + step) for i in range(count) if 0 <= i + step < count]
    return lax.ppermute(value, "dom", pairs)


def shift_in(value, axis, step):
    count = lax.axis_size(axis)
    return lax.ppermute(value, axis, [(i, (i - step) % count) for i in range(count)])


def from_all(value, axis, groups):
    size = len(groups[0])
    copies = jnp.broadcast_to(value[None], (size,) + value.shape)
    return lax.all_to_all(copies, axis, 0, 0, axis_index_groups=groups)


def whole(shape):
    return pl.BlockSpec(shape, lambda t: (0,) * len(shape))


def params(mib):
    return pltpu.CompilerParams(vmem_limit_bytes=mib * MIB)


def cost(flops, bytes_):
    return pl.CostEstimate(flops=flops, bytes_accessed=bytes_, transcendentals=0)


def on_device(
    mode_shapes,
    eigenvalues,
    mode_weights,
    stiff_deriv,
    mass_ref,
    mass_scale,
    connectivity,
    design_owner,
    direction,
):
    modes, _, nodes = mode_shapes.shape
    elems = connectivity.shape[1]
    des = direction.shape[0]
    groups = lax.axis_size("mode")
    count = lax.axis_size("dom")
    total_modes = groups * modes
    rows = COMPS * modes
    big = CORNERS * rows
    tiles = elems // TILE
    wide = CORNERS * TILE
    entries = 16
    shaped = jax.ShapeDtypeStruct
    vmem = pl.BlockSpec(memory_space=pltpu.VMEM)
    hbm = pl.BlockSpec(memory_space=pltpu.HBM)

    field = jnp.transpose(mode_shapes, (1, 0, 2)).reshape(rows, nodes)
    eig_row = eigenvalues.reshape(1, total_modes)
    weight_row = mode_weights.reshape(1, modes)

    up, down = pl.pallas_call(
        functools.partial(pack_kernel, rows, des),
        grid=(1,),
        in_specs=[
            pl.BlockSpec((rows, LANES), lambda t: (0, 0)),
            pl.BlockSpec((rows, LANES), lambda t: (0, nodes // LANES - 1)),
            whole((des,)),
        ],
        out_specs=[whole((rows + EXTRA, LANES))] * 2,
        out_shape=[shaped((rows + EXTRA, LANES), bf16)] * 2,
        name="pack",
    )(field, field, direction)
    low, high = neighbour(up, 1), neighbour(down, -1)
    upper = lax.broadcasted_iota(jnp.int32, (rows, LANES), 1) < LANES // 2
    rim = jnp.where(upper, high[:rows], low[:rows])
    fields = [field] + [shift_in(field, "mode", s) for s in range(1, groups)]
    rims = [rim] + [shift_in(rim, "mode", s) for s in range(1, groups)]

    def pinned(*values):
        return [pltpu.with_memory_space_constraint(v, pltpu.HBM) for v in values]

    resid, power, node, conn, owner_row, eig_copy, weight_copy = pl.pallas_call(
        functools.partial(forces_kernel, modes, nodes, des, elems),
        in_specs=[hbm] * 8 + [vmem] * 3,
        out_specs=[vmem] * 7,
        out_shape=[
            shaped((big, elems), f32),
            shaped((modes, elems), f32),
            shaped((2 * rows, nodes + LANES), f32),
            shaped((CORNERS, elems), jnp.int32),
            shaped((1, elems), jnp.int32),
            shaped((1, total_modes), f32),
            shaped((1, modes), f32),
        ],
        scratch_shapes=[
            pltpu.VMEM((elems,), jnp.int32),
            pltpu.VMEM((elems,), f32),
            pltpu.VMEM((tiles, DOFS, DOFS, TILE), bf16),
            pltpu.VMEM((rows, nodes + LANES), bf16),
            pltpu.VMEM((DOFS, DOFS), bf16),
            pltpu.SemaphoreType.DMA((7,)),
            pltpu.SemaphoreType.DMA((tiles,)),
            pltpu.VMEM((1, elems), f32),
            pltpu.VMEM((1, elems), f32),
            pltpu.VMEM((DOFS * SUBS, DOFS * SUBS), bf16),
            pltpu.VMEM((nodes + LANES, wide), bf16),
            pltpu.VMEM((rows, wide), f32),
            pltpu.VMEM((modes // SUBS, DOFS * SUBS, TILE), f32),
            pltpu.VMEM((DOFS, DOFS, TILE), f32),
            pltpu.VMEM((2 * rows, wide), bf16),
            pltpu.VMEM((nodes + LANES, 2 * rows), f32),
        ],
        compiler_params=params(24),
        cost_estimate=cost(8_000_000_000, 8_000_000),
        name="forces",
    )(
        *pinned(
            connectivity,
            design_owner,
            mass_scale,
            stiff_deriv,
            field,
            mass_ref,
            eig_row,
            weight_row,
        ),
        low,
        up,
        high,
    )

    gram = pl.pallas_call(
        functools.partial(gram_kernel, modes, groups, nodes),
        out_shape=shaped((modes + 8, total_modes), f32),
        compiler_params=params(24),
        name="gram",
    )(node, eig_copy, *fields, *rims)

    gram = gram + lax.ppermute(gram, "dom", [(i, i ^ 1) for i in range(count)])
    grams = from_all(gram, "dom", [list(range(core, count, 2)) for core in range(2)])

    low_sum, own_sum, high_sum, eig_deriv = pl.pallas_call(
        functools.partial(energy_kernel, modes, groups, nodes, des, elems),
        in_specs=[vmem] * (7 + 2 * groups),
        out_specs=[vmem] * 4,
        out_shape=[shaped((1, des), f32)] * 3 + [shaped((1, modes), f32)],
        scratch_shapes=[
            pltpu.VMEM((rows, nodes + LANES), bf16),
            pltpu.VMEM((modes, LANES), f32),
            pltpu.VMEM((nodes + LANES, wide), bf16),
            pltpu.VMEM((entries, LANES), f32),
        ],
        compiler_params=params(24),
        name="energy",
    )(grams, eig_copy, weight_copy, *fields, *rims, conn, owner_row, resid, power)

    owned = own_sum + neighbour(low_sum, -1) + neighbour(high_sum, 1)
    hess_vec = jnp.sum(from_all(owned, "mode", [list(range(groups))]), axis=0)
    return (hess_vec.reshape(des), eig_deriv.reshape(modes))


def solution(mesh):
    return jax.shard_map(
        on_device,
        mesh=mesh,
        in_specs=(
            P("mode", None, "dom"),
            P(),
            P("mode"),
            P(None, None, "dom"),
            P(),
            P("dom"),
            P(None, "dom"),
            P("dom"),
            P("dom"),
        ),
        out_specs=(P("dom"), P("mode")),
        check_vma=False,
    )
```

time: 605 us -> 87.9 us (0.15)
  the two profiles are of different devices: /device:TPU:2 before, /device:TPU:8 now
where the time goes in v3:
time: 87.9 us; the launch traced here: 87.2 us
  Pallas kernels  31.3 us (36%)
  starting transfers between devices  25.7 us (29%)
  blocking collectives  23.4 us (27%)
  waiting for transfers between devices  4.55 us (5%)
    all_to_all x2, blocking collectives, from_all(): return lax.all_to_all(copies, axis, 0, 0, axis_index_groups=groups)  23.4 us
    pallas_call x1, Pallas kernels, on_device(): pl.pallas_call(functools.partial(forces_kernel, modes, nodes, des, elems)...  22.8 us
    ppermute x4, starting transfers between devices, neighbour(): return lax.ppermute(value, 'dom', pairs)  15.3 us
    ppermute x6, starting transfers between devices, shift_in(): lax.ppermute(value, axis, [(i, (i - step) % count) for i in range(count)])  10.3 us
    pallas_call x1, Pallas kernels, on_device(): pl.pallas_call(functools.partial(energy_kernel, modes, groups, nodes, des...  6.08 us
    ppermute x4, waiting for transfers between devices, neighbour(): return lax.ppermute(value, 'dom', pairs)  3.35 us
  transfers between devices with their start and end apart: 11, of which 4 were waited for; matrix products, arithmetic and copies ran while one was open for 0% of the time, Pallas kernels for 26%

profile of v3, /device:TPU:8, one launch (start us, length us, event | category | flops | bytes accessed | tf_op | source)
XLA Modules:
  0.0 87.2 jit_solution(948854508733734240)
XLA Ops:
  0.6 1.5 %pack.1 = (bf16[208,128]{1,0:T(8,128)(2,1)}, bf16[208,128]{1,0:T(8,128)(2,1)}) custom-call(bf16[192,1024]{1,0:T(8,128)(2,1)} %bitcast.6, bf16[192,1024]{1,0:T(8,128)(2,1)} %bitcast.7, f32[640]{0:T(1024)} %dir_ref.1), custom_call_target="tpu_custom_call" | custom-call | tf_op jit(solution)/shard_map/pack/pallas_call | solution.py:397
  2.1 1.9 %collective-permute-start = (bf16[208,128]{1,0:T(8,128)(2,1)}, bf16[208,128]{1,0:T(8,128)(2,1)S(1)}, u32[]{:S(2)}, u32[]{:S(2)}) collective-permute-start(bf16[208,128]{1,0:T(8,128)(2,1)} %get-tuple-element.15.own_ref), channel_id=1, source_target_pairs={{0,4},{4,8},{8,12},{12,16},{16,20},{20,24},{24,28},{28,32},{32,36}... | collective-permute-start | bytes 159752 | tf_op jit(solution)/shard_map/ppermute | solution.py:341
  4.0 5.8 %collective-permute-start.1 = (bf16[208,128]{1,0:T(8,128)(2,1)}, bf16[208,128]{1,0:T(8,128)(2,1)S(1)}, u32[]{:S(2)}, u32[]{:S(2)}) collective-permute-start(bf16[208,128]{1,0:T(8,128)(2,1)} %get-tuple-element.16), channel_id=1, source_target_pairs={{4,0},{8,4},{12,8},{16,12},{20,16},{24,20},{28,24},{32,28},{36,32}... | collective-permute-start | bytes 159752 | tf_op jit(solution)/shard_map/ppermute | solution.py:341
  9.8 0.1 collective-permute-done.low_ref
  9.9 2.0 %collective-permute-done.1.high_ref = bf16[208,128]{1,0:T(8,128)(2,1)S(1)} collective-permute-done((bf16[208,128]{1,0:T(8,128)(2,1)}, bf16[208,128]{1,0:T(8,128)(2,1)S(1)}, u32[]{:S(2)}, u32[]{:S(2)}) %collective-permute-start.1) | collective-permute-done | bytes 53280 | tf_op jit(solution)/shard_map/ppermute | solution.py:341
  11.9 4.1 %collective-permute-start.5 = (bf16[192,128]{1,0:T(8,128)(2,1)S(1)}, bf16[192,128]{1,0:T(8,128)(2,1)S(1)}, u32[]{:S(2)}, u32[]{:S(2)}) collective-permute-start(bf16[192,128]{1,0:T(8,128)(2,1)S(1)} %slice_select_fusion.refs_4_), channel_id=1, source_target_pairs={{0,3},{1,0},{2,1},{3,2},{4,7},{5,4},{6,5},{7,6},{8,11},{9,8},{10,9... | collective-permute-start | bytes 147464 | tf_op jit(solution)/shard_map/ppermute | solution.py:346
  16.0 0.4 collective-permute-start.2
  16.4 0.0 collective-permute-start.3
  16.4 1.6 %collective-permute-start.4 = (bf16[192,1024]{1,0:T(8,128)(2,1)}, bf16[192,1024]{1,0:T(8,128)(2,1)S(1)}, u32[]{:S(2)}, u32[]{:S(2)}) collective-permute-start(bf16[192,1024]{1,0:T(8,128)(2,1)} %bitcast.10), channel_id=1, source_target_pairs={{0,1},{1,2},{2,3},{3,0},{4,5},{5,6},{6,7},{7,4},{8,9},{9,10},{10,1... | collective-permute-start | bytes 1179656 | tf_op jit(solution)/shard_map/ppermute | solution.py:346
  18.0 4.1 %collective-permute-start.6 = (bf16[192,128]{1,0:T(8,128)(2,1)S(1)}, bf16[192,128]{1,0:T(8,128)(2,1)S(1)}, u32[]{:S(2)}, u32[]{:S(2)}) collective-permute-start(bf16[192,128]{1,0:T(8,128)(2,1)S(1)} %slice_select_fusion.refs_4_), channel_id=1, source_target_pairs={{0,2},{1,3},{2,0},{3,1},{4,6},{5,7},{6,4},{7,5},{8,10},{9,11},{10,... | collective-permute-start | bytes 147464 | tf_op jit(solution)/shard_map/ppermute | solution.py:346
  22.2 0.0 collective-permute-done.5.refs_5_
  22.2 0.0 collective-permute-start.7
  22.2 0.0 copy-start.1
  22.2 0.8 copy-done.1
  23.0 22.8 %forces.1 = (f32[768,1536]{1,0:T(8,128)S(1)}, f32[32,1536]{1,0:T(8,128)S(1)}, f32[384,1152]{1,0:T(8,128)S(1)}, s32[4,1536]{1,0:T(4,128)S(1)}, s32[1,1536]{1,0:T(...) custom-call(s32[4,1536]{1,0:T(4,128)} %conn_hbm.1, s32[1536]{0:T(1024)} %owner_hbm.1, f32[1536]{0:T(1024)} %mass_hbm.1, ...), custom_call_target="tpu_custom_call" | custom-call | flops 8000000000 | bytes 8000000 | tf_op jit(solution)/shard_map/forces/pallas_call | solution.py:418
  45.8 0.0 collective-permute-done.6.refs_6_
  45.8 0.0 collective-permute-done.7.refs_7_
  45.9 0.0 collective-permute-done.2.refs_1_
  45.9 0.0 collective-permute-done.3.refs_2_
  45.9 0.0 collective-permute-done.4.refs_3_
  45.9 0.0 copy-done
  45.9 0.9 %gram.1 = f32[40,128]{1,0:T(8,128)S(1)} custom-call(f32[384,1152]{1,0:T(8,128)S(1)} %get-tuple-element.17.node_ref, f32[1,128]{1,0:T(1,128)S(1)} %get-tuple-element.18.eig_ref, bf16[192,1024]{1,0:T(8,128)(2,1)S(1)} %bitcast.12, bf16[192,1024]{1,0:T(8,128)(2,1)S(1)} %collective-permute-done.2.refs_1_, bf16[192,1024]{1,0:T(8,128)(2,1)S(1)} %collective-permute-done.3.refs_2_, ...), custom_call_target="tpu_custom_call" | custom-call | tf_op jit(solution)/shard_map/gram/pallas_call | solution.py:468
  46.8 0.1 collective-permute-start.8
  46.9 1.2 %collective-permute-done.8 = f32[40,128]{1,0:T(8,128)S(1)} collective-permute-done((f32[40,128]{1,0:T(8,128)S(1)}, f32[40,128]{1,0:T(8,128)S(1)}, u32[]{:S(2)}, u32[]{:S(2)}) %collective-permute-start.8) | collective-permute-done | bytes 20512 | tf_op jit(solution)/shard_map/ppermute | solution.py:475
  48.1 14.1 %all_to_all.10.gram_ref = f32[16,40,128]{2,1,0:T(8,128)S(1)} all-to-all(f32[16,40,128]{2,1,0:T(8,128)S(1)} %broadcast_in_dim.6), channel_id=1, replica_groups={{0,8,16,24,32,40,48,56,64,72,80,88,96,104,112,120},{4,12,20,28,36,44,52..., dimensions={0} | all-to-all | bytes 655360 | tf_op jit(solution)/shard_map/all_to_all | solution.py:352
  62.2 6.1 %energy.1 = (f32[1,640]{1,0:T(1,128)S(1)}, f32[1,640]{1,0:T(1,128)S(1)}, f32[1,640]{1,0:T(1,128)S(1)}, f32[1,32]{1,0:T(1,128)}) custom-call(f32[16,40,128]{2,1,0:T(8,128)S(1)} %all_to_all.10.gram_ref, f32[1,128]{1,0:T(1,128)S(1)} %get-tuple-element.18.eig_ref, f32[1,32]{1,0:T(1,128)S(1)} %get-tuple-element.19.weight_ref, bf16[192,1024]{1,0:T(8,128)(2,1)S(1)} %bitcast.13, ...), custom_call_target="tpu_custom_call" | custom-call | tf_op jit(solution)/shard_map/energy/pallas_call | solution.py:478
  68.3 1.9 %collective-permute-start.10 = (f32[1,640]{1,0:T(1,128)S(1)}, f32[1,640]{1,0:T(1,128)S(1)}, u32[]{:S(2)}, u32[]{:S(2)}) collective-permute-start(f32[1,640]{1,0:T(1,128)S(1)} %get-tuple-element.26), channel_id=1, source_target_pairs={{0,4},{4,8},{8,12},{12,16},{16,20},{20,24},{24,28},{28,32},{32,36}... | collective-permute-start | bytes 7688 | tf_op jit(solution)/shard_map/ppermute | solution.py:341
  70.2 5.8 %collective-permute-start.9 = (f32[1,640]{1,0:T(1,128)S(1)}, f32[1,640]{1,0:T(1,128)S(1)}, u32[]{:S(2)}, u32[]{:S(2)}) collective-permute-start(f32[1,640]{1,0:T(1,128)S(1)} %get-tuple-element.25), channel_id=1, source_target_pairs={{4,0},{8,4},{12,8},{16,12},{20,16},{24,20},{28,24},{32,28},{36,32}... | collective-permute-start | bytes 7688 | tf_op jit(solution)/shard_map/ppermute | solution.py:341
  76.0 0.0 collective-permute-done.10
  76.0 1.3 %collective-permute-done.9 = f32[1,640]{1,0:T(1,128)S(1)} collective-permute-done((f32[1,640]{1,0:T(1,128)S(1)}, f32[1,640]{1,0:T(1,128)S(1)}, u32[]{:S(2)}, u32[]{:S(2)}) %collective-permute-start.9) | collective-permute-done | bytes 2592 | tf_op jit(solution)/shard_map/ppermute | solution.py:341
  77.3 9.3 %all_to_all.11 = f32[4,1,640]{2,1,0:T(1,128)S(1)} all-to-all(f32[4,1,640]{2,1,0:T(1,128)S(1)} %broadcast_in_dim.16), channel_id=1, replica_groups={{0,1,2,3},{4,5,6,7},{8,9,10,11},{12,13,14,15},{16,17,18,19},{20,21,22,2..., dimensions={0} | all-to-all | bytes 20480 | tf_op jit(solution)/shard_map/all_to_all | solution.py:352
  86.6 0.6 reduce_sum.9
  (7 shorter events, 0.1 us)
Async XLA Ops:
  2.1 7.8 %collective-permute-start = (bf16[208,128]{1,0:T(8,128)(2,1)}, bf16[208,128]{1,0:T(8,128)(2,1)S(1)}, u32[]{:S(2)}, u32[]{:S(2)}) collective-permute-start(bf16[208,128]{1,0:T(8,128)(2,1)} %get-tuple-element.15.own_ref), channel_id=1, source_target_pairs={{0,4},{4,8},{8,12},{12,16},{16,20},{20,24},{24,28},{28,32},{32,36}... | collective-permute-start | bytes 159752 | tf_op jit(solution)/shard_map/ppermute | solution.py:341
  4.0 7.8 %collective-permute-start.1 = (bf16[208,128]{1,0:T(8,128)(2,1)}, bf16[208,128]{1,0:T(8,128)(2,1)S(1)}, u32[]{:S(2)}, u32[]{:S(2)}) collective-permute-start(bf16[208,128]{1,0:T(8,128)(2,1)} %get-tuple-element.16), channel_id=1, source_target_pairs={{4,0},{8,4},{12,8},{16,12},{20,16},{24,20},{28,24},{32,28},{36,32}... | collective-permute-start | bytes 159752 | tf_op jit(solution)/shard_map/ppermute | solution.py:341
  11.9 10.3 %collective-permute-start.5 = (bf16[192,128]{1,0:T(8,128)(2,1)S(1)}, bf16[192,128]{1,0:T(8,128)(2,1)S(1)}, u32[]{:S(2)}, u32[]{:S(2)}) collective-permute-start(bf16[192,128]{1,0:T(8,128)(2,1)S(1)} %slice_select_fusion.refs_4_), channel_id=1, source_target_pairs={{0,3},{1,0},{2,1},{3,2},{4,7},{5,4},{6,5},{7,6},{8,11},{9,8},{10,9... | collective-permute-start | bytes 147464 | tf_op jit(solution)/shard_map/ppermute | solution.py:346
  16.0 29.9 %collective-permute-start.2 = (bf16[192,1024]{1,0:T(8,128)(2,1)}, bf16[192,1024]{1,0:T(8,128)(2,1)S(1)}, u32[]{:S(2)}, u32[]{:S(2)}) collective-permute-start(bf16[192,1024]{1,0:T(8,128)(2,1)} %bitcast.8), channel_id=1, source_target_pairs={{0,3},{1,0},{2,1},{3,2},{4,7},{5,4},{6,5},{7,6},{8,11},{9,8},{10,9... | collective-permute-start | bytes 1179656 | tf_op jit(solution)/shard_map/ppermute | solution.py:346
  16.4 29.5 %collective-permute-start.3 = (bf16[192,1024]{1,0:T(8,128)(2,1)}, bf16[192,1024]{1,0:T(8,128)(2,1)S(1)}, u32[]{:S(2)}, u32[]{:S(2)}) collective-permute-start(bf16[192,1024]{1,0:T(8,128)(2,1)} %bitcast.9), channel_id=1, source_target_pairs={{0,2},{1,3},{2,0},{3,1},{4,6},{5,7},{6,4},{7,5},{8,10},{9,11},{10,... | collective-permute-start | bytes 1179656 | tf_op jit(solution)/shard_map/ppermute | solution.py:346
  16.4 29.5 %collective-permute-start.4 = (bf16[192,1024]{1,0:T(8,128)(2,1)}, bf16[192,1024]{1,0:T(8,128)(2,1)S(1)}, u32[]{:S(2)}, u32[]{:S(2)}) collective-permute-start(bf16[192,1024]{1,0:T(8,128)(2,1)} %bitcast.10), channel_id=1, source_target_pairs={{0,1},{1,2},{2,3},{3,0},{4,5},{5,6},{6,7},{7,4},{8,9},{9,10},{10,1... | collective-permute-start | bytes 1179656 | tf_op jit(solution)/shard_map/ppermute | solution.py:346
  18.0 27.8 %collective-permute-start.6 = (bf16[192,128]{1,0:T(8,128)(2,1)S(1)}, bf16[192,128]{1,0:T(8,128)(2,1)S(1)}, u32[]{:S(2)}, u32[]{:S(2)}) collective-permute-start(bf16[192,128]{1,0:T(8,128)(2,1)S(1)} %slice_select_fusion.refs_4_), channel_id=1, source_target_pairs={{0,2},{1,3},{2,0},{3,1},{4,6},{5,7},{6,4},{7,5},{8,10},{9,11},{10,... | collective-permute-start | bytes 147464 | tf_op jit(solution)/shard_map/ppermute | solution.py:346
  22.2 23.7 %collective-permute-start.7 = (bf16[192,128]{1,0:T(8,128)(2,1)S(1)}, bf16[192,128]{1,0:T(8,128)(2,1)S(1)}, u32[]{:S(2)}, u32[]{:S(2)}) collective-permute-start(bf16[192,128]{1,0:T(8,128)(2,1)S(1)} %slice_select_fusion.refs_4_), channel_id=1, source_target_pairs={{0,1},{1,2},{2,3},{3,0},{4,5},{5,6},{6,7},{7,4},{8,9},{9,10},{10,1... | collective-permute-start | bytes 147464 | tf_op jit(solution)/shard_map/ppermute | solution.py:346
  22.2 0.8 copy-start.1
  23.0 22.9 %copy-start = (bf16[32,6,1024]{2,0,1:T(8,128)(2,1)S(1)}, bf16[32,6,1024]{2,0,1:T(8,128)(2,1)}, u32[]{:S(2)}) copy-start(bf16[32,6,1024]{2,0,1:T(8,128)(2,1)} %param.9) | copy-start | bytes 1179652
  46.8 1.3 %collective-permute-start.8 = (f32[40,128]{1,0:T(8,128)S(1)}, f32[40,128]{1,0:T(8,128)S(1)}, u32[]{:S(2)}, u32[]{:S(2)}) collective-permute-start(f32[40,128]{1,0:T(8,128)S(1)} %gram.1), channel_id=1, source_target_pairs={{0,4},{4,0},{8,12},{12,8},{16,20},{20,16},{24,28},{28,24},{32,36},... | collective-permute-start | bytes 61448 | tf_op jit(solution)/shard_map/ppermute | solution.py:475
  68.3 7.7 %collective-permute-start.10 = (f32[1,640]{1,0:T(1,128)S(1)}, f32[1,640]{1,0:T(1,128)S(1)}, u32[]{:S(2)}, u32[]{:S(2)}) collective-permute-start(f32[1,640]{1,0:T(1,128)S(1)} %get-tuple-element.26), channel_id=1, source_target_pairs={{0,4},{4,8},{8,12},{12,16},{16,20},{20,24},{24,28},{28,32},{32,36}... | collective-permute-start | bytes 7688 | tf_op jit(solution)/shard_map/ppermute | solution.py:341
  70.2 7.1 %collective-permute-start.9 = (f32[1,640]{1,0:T(1,128)S(1)}, f32[1,640]{1,0:T(1,128)S(1)}, u32[]{:S(2)}, u32[]{:S(2)}) collective-permute-start(f32[1,640]{1,0:T(1,128)S(1)} %get-tuple-element.25), channel_id=1, source_target_pairs={{4,0},{8,4},{12,8},{16,12},{20,16},{24,20},{28,24},{32,28},{36,32}... | collective-permute-start | bytes 7688 | tf_op jit(solution)/shard_map/ppermute | solution.py:341

commit v4 on v3

--- a/solution.py
+++ b/solution.py
@@ -11,7 +11,7 @@
 COMPS = 6
 CORNERS = 4
 DOFS = 24
-TILE = 256
+TILE = 768
 LANES = 128
 EXTRA = 16
 SUBS = 8
@@ -97,8 +97,8 @@
     ref_hbm,
     eig_hbm,
     weight_hbm,
+    own_hbm,
     low_ref,
-    own_ref,
     high_ref,
     resid_ref,
     power_ref,
@@ -112,6 +112,7 @@
     stiff,
     field,
     ref,
+    own,
     sems,
     stiff_sems,
     mass_row,
@@ -140,6 +141,7 @@
                 (mass_hbm, mass_flat),
                 (eig_hbm, eig_row),
                 (weight_hbm, weight_row),
+                (own_hbm.at[pl.ds(rows, EXTRA)], own),
             )
         )
     ]
@@ -153,13 +155,6 @@
     for t in range(tiles):
         stiff_copy(t).start()
 
-    per = des // LANES
-    sides = []
-    for ref_ in (low_ref, own_ref, high_ref):
-        packed = ref_[rows : rows + EXTRA, :].astype(f32)
-        sides.append(packed[:per] + packed[per : 2 * per] + packed[2 * per : 3 * per])
-    sides.append(jnp.zeros((entries - 3 * per, LANES), f32))
-    table = jnp.concatenate(three_pieces(jnp.concatenate(sides, axis=0)), axis=0)
     lower = iota((rows, LANES), 1) >= LANES // 2
     field[:, nodes : nodes + LANES] = jnp.where(
         lower, low_ref[0:rows, :].astype(f32), high_ref[0:rows, :].astype(f32)
@@ -167,6 +162,13 @@
     sums_t[...] = jnp.zeros_like(sums_t)
     for copy in small:
         copy.wait()
+    per = des // LANES
+    sides = []
+    for pieces in (low_ref[rows : rows + EXTRA, :], own[...], high_ref[rows : rows + EXTRA, :]):
+        packed = pieces.astype(f32)
+        sides.append(packed[:per] + packed[per : 2 * per] + packed[2 * per : 3 * per])
+    sides.append(jnp.zeros((entries - 3 * per, LANES), f32))
+    table = jnp.concatenate(three_pieces(jnp.concatenate(sides, axis=0)), axis=0)
     mass_big[...] = expand_mass(ref[...])
     rows_of(owner_flat, owner_row)
     rows_of(mass_flat, mass_row)
@@ -406,10 +408,11 @@
         out_shape=[shaped((rows + EXTRA, LANES), bf16)] * 2,
         name="pack",
     )(field, field, direction)
+    sent, up, down = lax.optimization_barrier((field, up, down))
     low, high = neighbour(up, 1), neighbour(down, -1)
     upper = lax.broadcasted_iota(jnp.int32, (rows, LANES), 1) < LANES // 2
     rim = jnp.where(upper, high[:rows], low[:rows])
-    fields = [field] + [shift_in(field, "mode", s) for s in range(1, groups)]
+    fields = [field] + [shift_in(sent, "mode", s) for s in range(1, groups)]
     rims = [rim] + [shift_in(rim, "mode", s) for s in range(1, groups)]
 
     def pinned(*values):
@@ -417,7 +420,7 @@
 
     resid, power, node, conn, owner_row, eig_copy, weight_copy = pl.pallas_call(
         functools.partial(forces_kernel, modes, nodes, des, elems),
-        in_specs=[hbm] * 8 + [vmem] * 3,
+        in_specs=[hbm] * 9 + [vmem] * 2,
         out_specs=[vmem] * 7,
         out_shape=[
             shaped((big, elems), f32),
@@ -434,7 +437,8 @@
             pltpu.VMEM((tiles, DOFS, DOFS, TILE), bf16),
             pltpu.VMEM((rows, nodes + LANES), bf16),
             pltpu.VMEM((DOFS, DOFS), bf16),
-            pltpu.SemaphoreType.DMA((7,)),
+            pltpu.VMEM((EXTRA, LANES), bf16),
+            pltpu.SemaphoreType.DMA((8,)),
             pltpu.SemaphoreType.DMA((tiles,)),
             pltpu.VMEM((1, elems), f32),
             pltpu.VMEM((1, elems), f32),
@@ -446,8 +450,8 @@
             pltpu.VMEM((2 * rows, wide), bf16),
             pltpu.VMEM((nodes + LANES, 2 * rows), f32),
         ],
-        compiler_params=params(24),
-        cost_estimate=cost(8_000_000_000, 8_000_000),
+        compiler_params=params(44),
+        cost_estimate=cost(1_000_000, 100_000),
         name="forces",
     )(
         *pinned(
@@ -459,9 +463,9 @@
             mass_ref,
             eig_row,
             weight_row,
+            up,
         ),
         low,
-        up,
         high,
     )
 
@@ -486,7 +490,7 @@
             pltpu.VMEM((nodes + LANES, wide), bf16),
             pltpu.VMEM((entries, LANES), f32),
         ],
-        compiler_params=params(24),
+        compiler_params=params(44),
         name="energy",
     )(grams, eig_copy, weight_copy, *fields, *rims, conn, owner_row, resid, power)
 

time: 87.9 us -> 90 us (1.024)
  waiting for transfers between devices: 4.55 us -> 8.26 us
  Pallas kernels: 31.3 us -> 28.1 us
  blocking collectives: 23.4 us -> 25.2 us
    ppermute x6, waiting for transfers between devices: 0.02 us -> 3.73 us  [shift_in(): lax.ppermute(value, axis, [(i, (i - step) % count) for i in range(count)])]
    all_to_all x2, blocking collectives: 23.4 us -> 25.2 us  [from_all(): return lax.all_to_all(copies, axis, 0, 0, axis_index_groups=groups)]
    pallas_call x1, Pallas kernels: 22.8 us -> 21.1 us  [on_device(): pl.pallas_call(functools.partial(forces_kernel, modes, nodes, des, elems)...]
    pallas_call x1, Pallas kernels: 6.08 us -> 4.55 us  [on_device(): pl.pallas_call(functools.partial(energy_kernel, modes, groups, nodes, des...]
  transfers between devices with their start and end apart: 11 -> 11, of which waited for: 4 -> 5; matrix products, arithmetic and copies ran while one was open for 0% -> 0% of each run, Pallas kernels for 26% -> 24%
where the time goes in v4:
time: 90 us; the launch traced here: 89.3 us
  Pallas kernels  28.1 us (31%)
  starting transfers between devices  26.3 us (29%)
  blocking collectives  25.2 us (28%)
  waiting for transfers between devices  8.26 us (9%)
    all_to_all x2, blocking collectives, from_all(): return lax.all_to_all(copies, axis, 0, 0, axis_index_groups=groups)  25.2 us
    pallas_call x1, Pallas kernels, on_device(): pl.pallas_call(functools.partial(forces_kernel, modes, nodes, des, elems)...  21.1 us
    ppermute x4, starting transfers between devices, neighbour(): return lax.ppermute(value, 'dom', pairs)  15.3 us
    ppermute x6, starting transfers between devices, shift_in(): lax.ppermute(value, axis, [(i, (i - step) % count) for i in range(count)])  10.8 us
    pallas_call x1, Pallas kernels, on_device(): pl.pallas_call(functools.partial(energy_kernel, modes, groups, nodes, des...  4.55 us
    ppermute x6, waiting for transfers between devices, shift_in(): lax.ppermute(value, axis, [(i, (i - step) % count) for i in range(count)])  3.73 us
    ppermute x4, waiting for transfers between devices, neighbour(): return lax.ppermute(value, 'dom', pairs)  3.35 us
  transfers between devices with their start and end apart: 11, of which 5 were waited for; matrix products, arithmetic and copies ran while one was open for 0% of the time, Pallas kernels for 24%

profile of v4, /device:TPU:8, one launch (start us, length us, event | category | flops | bytes accessed | tf_op | source)
XLA Modules:
  0.0 89.3 jit_solution(17253617684589864775)
XLA Ops:
  0.6 0.0 copy-start
  0.6 1.5 %pack.1 = (bf16[208,128]{1,0:T(8,128)(2,1)}, bf16[208,128]{1,0:T(8,128)(2,1)}) custom-call(bf16[192,1024]{1,0:T(8,128)(2,1)} %bitcast.6, bf16[192,1024]{1,0:T(8,128)(2,1)} %bitcast.7, f32[640]{0:T(1024)} %dir_ref.1), custom_call_target="tpu_custom_call" | custom-call | tf_op jit(solution)/shard_map/pack/pallas_call | solution.py:399
  2.2 4.0 %collective-permute-start.2 = (bf16[192,1024]{1,0:T(8,128)(2,1)}, bf16[192,1024]{1,0:T(8,128)(2,1)S(1)}, u32[]{:S(2)}, u32[]{:S(2)}) collective-permute-start(bf16[192,1024]{1,0:T(8,128)(2,1)} %bitcast.8), channel_id=1, source_target_pairs={{0,3},{1,0},{2,1},{3,2},{4,7},{5,4},{6,5},{7,6},{8,11},{9,8},{10,9... | collective-permute-start | bytes 1179656 | tf_op jit(solution)/shard_map/ppermute | solution.py:348
  6.2 0.0 collective-permute-start.3
  6.2 1.3 %collective-permute-start.4 = (bf16[192,1024]{1,0:T(8,128)(2,1)}, bf16[192,1024]{1,0:T(8,128)(2,1)S(1)}, u32[]{:S(2)}, u32[]{:S(2)}) collective-permute-start(bf16[192,1024]{1,0:T(8,128)(2,1)} %bitcast.10), channel_id=1, source_target_pairs={{0,1},{1,2},{2,3},{3,0},{4,5},{5,6},{6,7},{7,4},{8,9},{9,10},{10,1... | collective-permute-start | bytes 1179656 | tf_op jit(solution)/shard_map/ppermute | solution.py:348
  7.5 1.9 %collective-permute-start = (bf16[208,128]{1,0:T(8,128)(2,1)}, bf16[208,128]{1,0:T(8,128)(2,1)S(1)}, u32[]{:S(2)}, u32[]{:S(2)}) collective-permute-start(bf16[208,128]{1,0:T(8,128)(2,1)} %get-tuple-element.20.own_hbm), channel_id=1, source_target_pairs={{0,4},{4,8},{8,12},{12,16},{16,20},{20,24},{24,28},{28,32},{32,36}... | collective-permute-start | bytes 159752 | tf_op jit(solution)/shard_map/ppermute | solution.py:343
  9.4 5.8 %collective-permute-start.1 = (bf16[208,128]{1,0:T(8,128)(2,1)}, bf16[208,128]{1,0:T(8,128)(2,1)S(1)}, u32[]{:S(2)}, u32[]{:S(2)}) collective-permute-start(bf16[208,128]{1,0:T(8,128)(2,1)} %get-tuple-element.21), channel_id=1, source_target_pairs={{4,0},{8,4},{12,8},{16,12},{20,16},{24,20},{28,24},{32,28},{36,32}... | collective-permute-start | bytes 159752 | tf_op jit(solution)/shard_map/ppermute | solution.py:343
  15.2 0.1 collective-permute-done.low_ref
  15.2 2.0 %collective-permute-done.1.high_ref = bf16[208,128]{1,0:T(8,128)(2,1)S(1)} collective-permute-done((bf16[208,128]{1,0:T(8,128)(2,1)}, bf16[208,128]{1,0:T(8,128)(2,1)S(1)}, u32[]{:S(2)}, u32[]{:S(2)}) %collective-permute-start.1) | collective-permute-done | bytes 53280 | tf_op jit(solution)/shard_map/ppermute | solution.py:343
  17.3 2.0 %collective-permute-start.5 = (bf16[192,128]{1,0:T(8,128)(2,1)S(1)}, bf16[192,128]{1,0:T(8,128)(2,1)S(1)}, u32[]{:S(2)}, u32[]{:S(2)}) collective-permute-start(bf16[192,128]{1,0:T(8,128)(2,1)S(1)} %slice_select_fusion.refs_4_), channel_id=1, source_target_pairs={{0,3},{1,0},{2,1},{3,2},{4,7},{5,4},{6,5},{7,6},{8,11},{9,8},{10,9... | collective-permute-start | bytes 147464 | tf_op jit(solution)/shard_map/ppermute | solution.py:348
  19.3 2.3 %collective-permute-start.6 = (bf16[192,128]{1,0:T(8,128)(2,1)S(1)}, bf16[192,128]{1,0:T(8,128)(2,1)S(1)}, u32[]{:S(2)}, u32[]{:S(2)}) collective-permute-start(bf16[192,128]{1,0:T(8,128)(2,1)S(1)} %slice_select_fusion.refs_4_), channel_id=1, source_target_pairs={{0,2},{1,3},{2,0},{3,1},{4,6},{5,7},{6,4},{7,5},{8,10},{9,11},{10,... | collective-permute-start | bytes 147464 | tf_op jit(solution)/shard_map/ppermute | solution.py:348
  21.6 3.7 %collective-permute-done.5.refs_5_ = bf16[192,128]{1,0:T(8,128)(2,1)S(1)} collective-permute-done((bf16[192,128]{1,0:T(8,128)(2,1)S(1)}, bf16[192,128]{1,0:T(8,128)(2,1)S(1)}, u32[]{:S(2)}, u32[]{:S(2)}) %collective-permute-start.5) | collective-permute-done | bytes 49184 | tf_op jit(solution)/shard_map/ppermute | solution.py:348
  25.3 1.2 %collective-permute-start.7 = (bf16[192,128]{1,0:T(8,128)(2,1)S(1)}, bf16[192,128]{1,0:T(8,128)(2,1)S(1)}, u32[]{:S(2)}, u32[]{:S(2)}) collective-permute-start(bf16[192,128]{1,0:T(8,128)(2,1)S(1)} %slice_select_fusion.refs_4_), channel_id=1, source_target_pairs={{0,1},{1,2},{2,3},{3,0},{4,5},{5,6},{6,7},{7,4},{8,9},{9,10},{10,1... | collective-permute-start | bytes 147464 | tf_op jit(solution)/shard_map/ppermute | solution.py:348
  26.5 21.1 %forces.1 = (f32[768,1536]{1,0:T(8,128)S(1)}, f32[32,1536]{1,0:T(8,128)S(1)}, f32[384,1152]{1,0:T(8,128)S(1)}, s32[4,1536]{1,0:T(4,128)S(1)}, s32[1,1536]{1,0:T(...) custom-call(s32[4,1536]{1,0:T(4,128)} %conn_hbm.1, s32[1536]{0:T(1024)} %owner_hbm.1, f32[1536]{0:T(1024)} %mass_hbm.1, ...), custom_call_target="tpu_custom_call" | custom-call | flops 1000000 | bytes 100000 | tf_op jit(solution)/shard_map/forces/pallas_call | solution.py:421
  47.7 0.0 collective-permute-done.6.refs_6_
  47.7 0.0 collective-permute-done.7.refs_7_
  47.7 0.0 collective-permute-done.2.refs_1_
  47.7 0.0 collective-permute-done.3.refs_2_
  47.7 0.0 collective-permute-done.4.refs_3_
  47.7 0.0 copy-done
  47.7 0.9 %gram.1 = f32[40,128]{1,0:T(8,128)S(1)} custom-call(f32[384,1152]{1,0:T(8,128)S(1)} %get-tuple-element.22.node_ref, f32[1,128]{1,0:T(1,128)S(1)} %get-tuple-element.23.eig_ref, bf16[192,1024]{1,0:T(8,128)(2,1)S(1)} %bitcast.12, bf16[192,1024]{1,0:T(8,128)(2,1)S(1)} %collective-permute-done.2.refs_1_, bf16[192,1024]{1,0:T(8,128)(2,1)S(1)} %collective-permute-done.3.refs_2_, ...), custom_call_target="tpu_custom_call" | custom-call | tf_op jit(solution)/shard_map/gram/pallas_call | solution.py:472
  48.6 0.1 collective-permute-start.8
  48.7 1.2 %collective-permute-done.8 = f32[40,128]{1,0:T(8,128)S(1)} collective-permute-done((f32[40,128]{1,0:T(8,128)S(1)}, f32[40,128]{1,0:T(8,128)S(1)}, u32[]{:S(2)}, u32[]{:S(2)}) %collective-permute-start.8) | collective-permute-done | bytes 20512 | tf_op jit(solution)/shard_map/ppermute | solution.py:479
  49.9 14.8 %all_to_all.10.gram_ref = f32[16,40,128]{2,1,0:T(8,128)S(1)} all-to-all(f32[16,40,128]{2,1,0:T(8,128)S(1)} %broadcast_in_dim.6), channel_id=1, replica_groups={{0,8,16,24,32,40,48,56,64,72,80,88,96,104,112,120},{4,12,20,28,36,44,52..., dimensions={0} | all-to-all | bytes 655360 | tf_op jit(solution)/shard_map/all_to_all | solution.py:354
  64.8 4.5 %energy.1 = (f32[1,640]{1,0:T(1,128)S(1)}, f32[1,640]{1,0:T(1,128)S(1)}, f32[1,640]{1,0:T(1,128)S(1)}, f32[1,32]{1,0:T(1,128)}) custom-call(f32[16,40,128]{2,1,0:T(8,128)S(1)} %all_to_all.10.gram_ref, f32[1,128]{1,0:T(1,128)S(1)} %get-tuple-element.23.eig_ref, f32[1,32]{1,0:T(1,128)S(1)} %get-tuple-element.25.weight_ref, bf16[192,1024]{1,0:T(8,128)(2,1)S(1)} %bitcast.13, ...), custom_call_target="tpu_custom_call" | custom-call | tf_op jit(solution)/shard_map/energy/pallas_call | solution.py:482
  69.3 1.9 %collective-permute-start.10 = (f32[1,640]{1,0:T(1,128)S(1)}, f32[1,640]{1,0:T(1,128)S(1)}, u32[]{:S(2)}, u32[]{:S(2)}) collective-permute-start(f32[1,640]{1,0:T(1,128)S(1)} %get-tuple-element.32), channel_id=1, source_target_pairs={{0,4},{4,8},{8,12},{12,16},{16,20},{20,24},{24,28},{28,32},{32,36}... | collective-permute-start | bytes 7688 | tf_op jit(solution)/shard_map/ppermute | solution.py:343
  71.2 5.8 %collective-permute-start.9 = (f32[1,640]{1,0:T(1,128)S(1)}, f32[1,640]{1,0:T(1,128)S(1)}, u32[]{:S(2)}, u32[]{:S(2)}) collective-permute-start(f32[1,640]{1,0:T(1,128)S(1)} %get-tuple-element.31), channel_id=1, source_target_pairs={{4,0},{8,4},{12,8},{16,12},{20,16},{24,20},{28,24},{32,28},{36,32}... | collective-permute-start | bytes 7688 | tf_op jit(solution)/shard_map/ppermute | solution.py:343
  77.0 0.0 collective-permute-done.10
  77.0 1.3 %collective-permute-done.9 = f32[1,640]{1,0:T(1,128)S(1)} collective-permute-done((f32[1,640]{1,0:T(1,128)S(1)}, f32[1,640]{1,0:T(1,128)S(1)}, u32[]{:S(2)}, u32[]{:S(2)}) %collective-permute-start.9) | collective-permute-done | bytes 2592 | tf_op jit(solution)/shard_map/ppermute | solution.py:343
  78.3 10.4 %all_to_all.11 = f32[4,1,640]{2,1,0:T(1,128)S(1)} all-to-all(f32[4,1,640]{2,1,0:T(1,128)S(1)} %broadcast_in_dim.16), channel_id=1, replica_groups={{0,1,2,3},{4,5,6,7},{8,9,10,11},{12,13,14,15},{16,17,18,19},{20,21,22,2..., dimensions={0} | all-to-all | bytes 20480 | tf_op jit(solution)/shard_map/all_to_all | solution.py:354
  88.7 0.6 reduce_sum.9
  (6 shorter events, 0.1 us)
Async XLA Ops:
  0.6 47.1 %copy-start = (bf16[32,6,1024]{2,0,1:T(8,128)(2,1)S(1)}, bf16[32,6,1024]{2,0,1:T(8,128)(2,1)}, u32[]{:S(2)}) copy-start(bf16[32,6,1024]{2,0,1:T(8,128)(2,1)} %param.9) | copy-start | bytes 1179652
  2.2 45.5 %collective-permute-start.2 = (bf16[192,1024]{1,0:T(8,128)(2,1)}, bf16[192,1024]{1,0:T(8,128)(2,1)S(1)}, u32[]{:S(2)}, u32[]{:S(2)}) collective-permute-start(bf16[192,1024]{1,0:T(8,128)(2,1)} %bitcast.8), channel_id=1, source_target_pairs={{0,3},{1,0},{2,1},{3,2},{4,7},{5,4},{6,5},{7,6},{8,11},{9,8},{10,9... | collective-permute-start | bytes 1179656 | tf_op jit(solution)/shard_map/ppermute | solution.py:348
  6.2 41.5 %collective-permute-start.3 = (bf16[192,1024]{1,0:T(8,128)(2,1)}, bf16[192,1024]{1,0:T(8,128)(2,1)S(1)}, u32[]{:S(2)}, u32[]{:S(2)}) collective-permute-start(bf16[192,1024]{1,0:T(8,128)(2,1)} %bitcast.9), channel_id=1, source_target_pairs={{0,2},{1,3},{2,0},{3,1},{4,6},{5,7},{6,4},{7,5},{8,10},{9,11},{10,... | collective-permute-start | bytes 1179656 | tf_op jit(solution)/shard_map/ppermute | solution.py:348
  6.2 41.5 %collective-permute-start.4 = (bf16[192,1024]{1,0:T(8,128)(2,1)}, bf16[192,1024]{1,0:T(8,128)(2,1)S(1)}, u32[]{:S(2)}, u32[]{:S(2)}) collective-permute-start(bf16[192,1024]{1,0:T(8,128)(2,1)} %bitcast.10), channel_id=1, source_target_pairs={{0,1},{1,2},{2,3},{3,0},{4,5},{5,6},{6,7},{7,4},{8,9},{9,10},{10,1... | collective-permute-start | bytes 1179656 | tf_op jit(solution)/shard_map/ppermute | solution.py:348
  7.5 7.8 %collective-permute-start = (bf16[208,128]{1,0:T(8,128)(2,1)}, bf16[208,128]{1,0:T(8,128)(2,1)S(1)}, u32[]{:S(2)}, u32[]{:S(2)}) collective-permute-start(bf16[208,128]{1,0:T(8,128)(2,1)} %get-tuple-element.20.own_hbm), channel_id=1, source_target_pairs={{0,4},{4,8},{8,12},{12,16},{16,20},{20,24},{24,28},{28,32},{32,36}... | collective-permute-start | bytes 159752 | tf_op jit(solution)/shard_map/ppermute | solution.py:343
  9.4 7.8 %collective-permute-start.1 = (bf16[208,128]{1,0:T(8,128)(2,1)}, bf16[208,128]{1,0:T(8,128)(2,1)S(1)}, u32[]{:S(2)}, u32[]{:S(2)}) collective-permute-start(bf16[208,128]{1,0:T(8,128)(2,1)} %get-tuple-element.21), channel_id=1, source_target_pairs={{4,0},{8,4},{12,8},{16,12},{20,16},{24,20},{28,24},{32,28},{36,32}... | collective-permute-start | bytes 159752 | tf_op jit(solution)/shard_map/ppermute | solution.py:343
  17.3 8.1 %collective-permute-start.5 = (bf16[192,128]{1,0:T(8,128)(2,1)S(1)}, bf16[192,128]{1,0:T(8,128)(2,1)S(1)}, u32[]{:S(2)}, u32[]{:S(2)}) collective-permute-start(bf16[192,128]{1,0:T(8,128)(2,1)S(1)} %slice_select_fusion.refs_4_), channel_id=1, source_target_pairs={{0,3},{1,0},{2,1},{3,2},{4,7},{5,4},{6,5},{7,6},{8,11},{9,8},{10,9... | collective-permute-start | bytes 147464 | tf_op jit(solution)/shard_map/ppermute | solution.py:348
  19.3 28.4 %collective-permute-start.6 = (bf16[192,128]{1,0:T(8,128)(2,1)S(1)}, bf16[192,128]{1,0:T(8,128)(2,1)S(1)}, u32[]{:S(2)}, u32[]{:S(2)}) collective-permute-start(bf16[192,128]{1,0:T(8,128)(2,1)S(1)} %slice_select_fusion.refs_4_), channel_id=1, source_target_pairs={{0,2},{1,3},{2,0},{3,1},{4,6},{5,7},{6,4},{7,5},{8,10},{9,11},{10,... | collective-permute-start | bytes 147464 | tf_op jit(solution)/shard_map/ppermute | solution.py:348
  25.3 22.3 %collective-permute-start.7 = (bf16[192,128]{1,0:T(8,128)(2,1)S(1)}, bf16[192,128]{1,0:T(8,128)(2,1)S(1)}, u32[]{:S(2)}, u32[]{:S(2)}) collective-permute-start(bf16[192,128]{1,0:T(8,128)(2,1)S(1)} %slice_select_fusion.refs_4_), channel_id=1, source_target_pairs={{0,1},{1,2},{2,3},{3,0},{4,5},{5,6},{6,7},{7,4},{8,9},{9,10},{10,1... | collective-permute-start | bytes 147464 | tf_op jit(solution)/shard_map/ppermute | solution.py:348
  48.6 1.3 %collective-permute-start.8 = (f32[40,128]{1,0:T(8,128)S(1)}, f32[40,128]{1,0:T(8,128)S(1)}, u32[]{:S(2)}, u32[]{:S(2)}) collective-permute-start(f32[40,128]{1,0:T(8,128)S(1)} %gram.1), channel_id=1, source_target_pairs={{0,4},{4,0},{8,12},{12,8},{16,20},{20,16},{24,28},{28,24},{32,36},... | collective-permute-start | bytes 61448 | tf_op jit(solution)/shard_map/ppermute | solution.py:479
  69.3 7.7 %collective-permute-start.10 = (f32[1,640]{1,0:T(1,128)S(1)}, f32[1,640]{1,0:T(1,128)S(1)}, u32[]{:S(2)}, u32[]{:S(2)}) collective-permute-start(f32[1,640]{1,0:T(1,128)S(1)} %get-tuple-element.32), channel_id=1, source_target_pairs={{0,4},{4,8},{8,12},{12,16},{16,20},{20,24},{24,28},{28,32},{32,36}... | collective-permute-start | bytes 7688 | tf_op jit(solution)/shard_map/ppermute | solution.py:343
  71.2 7.1 %collective-permute-start.9 = (f32[1,640]{1,0:T(1,128)S(1)}, f32[1,640]{1,0:T(1,128)S(1)}, u32[]{:S(2)}, u32[]{:S(2)}) collective-permute-start(f32[1,640]{1,0:T(1,128)S(1)} %get-tuple-element.31), channel_id=1, source_target_pairs={{4,0},{8,4},{12,8},{16,12},{20,16},{24,20},{28,24},{32,28},{36,32}... | collective-permute-start | bytes 7688 | tf_op jit(solution)/shard_map/ppermute | solution.py:343

commit v5 on v4

--- a/solution.py
+++ b/solution.py
@@ -93,11 +93,11 @@
     owner_hbm,
     mass_hbm,
     stiff_hbm,
-    field_hbm,
     ref_hbm,
     eig_hbm,
     weight_hbm,
     own_hbm,
+    field,
     low_ref,
     high_ref,
     resid_ref,
@@ -110,7 +110,6 @@
     owner_flat,
     mass_flat,
     stiff,
-    field,
     ref,
     own,
     sems,
@@ -136,7 +135,6 @@
             (
                 (ref_hbm, ref),
                 (conn_hbm, conn),
-                (field_hbm, field.at[:, pl.ds(0, nodes)]),
                 (owner_hbm, owner_flat),
                 (mass_hbm, mass_flat),
                 (eig_hbm, eig_row),
@@ -155,10 +153,6 @@
     for t in range(tiles):
         stiff_copy(t).start()
 
-    lower = iota((rows, LANES), 1) >= LANES // 2
-    field[:, nodes : nodes + LANES] = jnp.where(
-        lower, low_ref[0:rows, :].astype(f32), high_ref[0:rows, :].astype(f32)
-    ).astype(bf16)
     sums_t[...] = jnp.zeros_like(sums_t)
     for copy in small:
         copy.wait()
@@ -251,20 +245,19 @@
     return jnp.concatenate([r[c * modes : (c + 1) * modes, :] for r in refs], axis=0)
 
 
-def gram_kernel(modes, groups, nodes, node_ref, eig_ref, *refs):
-    fields, rims, out_ref = refs[:groups], refs[groups : 2 * groups], refs[2 * groups]
+def gram_kernel(modes, groups, node_ref, eig_ref, *refs):
+    fields, out_ref = refs[:groups], refs[groups]
     rows = COMPS * modes
     eig = column_of(eig_ref[...], lax.axis_index("mode") * modes, modes)
     grams = [jnp.zeros((modes, groups * modes), f32) for _ in range(2)]
     for c in range(COMPS):
-        for cols, parts in ((slice(0, nodes), fields), (slice(nodes, nodes + LANES), rims)):
-            pieces = []
-            for kind in range(2):
-                base = kind * rows + c * modes
-                pieces += three_pieces(node_ref[base : base + modes, cols])
-            each = dot_nt(jnp.concatenate(pieces, axis=0), gather_modes(parts, c, modes))
-            each = [each[i * modes : (i + 1) * modes] for i in range(6)]
-            grams = [grams[k] + (each[3 * k] + (each[3 * k + 1] + each[3 * k + 2])) for k in range(2)]
+        pieces = []
+        for kind in range(2):
+            base = kind * rows + c * modes
+            pieces += three_pieces(node_ref[base : base + modes, :])
+        each = dot_nt(jnp.concatenate(pieces, axis=0), gather_modes(fields, c, modes))
+        each = [each[i * modes : (i + 1) * modes] for i in range(6)]
+        grams = [grams[k] + (each[3 * k] + (each[3 * k + 1] + each[3 * k + 2])) for k in range(2)]
     stiff_gram, mass_gram = grams
     out_ref[0:modes, :] = stiff_gram - eig * mass_gram
     mask = iota(mass_gram.shape, 0) == iota(mass_gram.shape, 1)
@@ -274,7 +267,7 @@
 
 
 def energy_kernel(modes, groups, nodes, des, elems, gram_ref, eig_ref, weight_ref, *refs):
-    fields, rims, refs = refs[:groups], refs[groups : 2 * groups], refs[2 * groups :]
+    fields, refs = refs[:groups], refs[groups:]
     conn_ref, owner_row, resid_ref, power_ref = refs[:4]
     low_ref, own_ref, high_ref, deriv_ref = refs[4:8]
     deriv, factor, hot, totals = refs[8:]
@@ -299,8 +292,7 @@
     factor[...] = jnp.broadcast_to(eig_deriv * column_of(weight_ref[...], 0, modes), factor.shape)
     for c in range(COMPS):
         span = slice(c * modes, (c + 1) * modes)
-        deriv[span, 0:nodes] = dot(combiner, gather_modes(fields, c, modes)).astype(bf16)
-        deriv[span, nodes : nodes + LANES] = dot(combiner, gather_modes(rims, c, modes)).astype(bf16)
+        deriv[span, :] = dot(combiner, gather_modes(fields, c, modes)).astype(bf16)
     totals[...] = jnp.zeros_like(totals)
 
     @pl.loop(0, elems // TILE)
@@ -408,19 +400,17 @@
         out_shape=[shaped((rows + EXTRA, LANES), bf16)] * 2,
         name="pack",
     )(field, field, direction)
-    sent, up, down = lax.optimization_barrier((field, up, down))
     low, high = neighbour(up, 1), neighbour(down, -1)
     upper = lax.broadcasted_iota(jnp.int32, (rows, LANES), 1) < LANES // 2
-    rim = jnp.where(upper, high[:rows], low[:rows])
-    fields = [field] + [shift_in(sent, "mode", s) for s in range(1, groups)]
-    rims = [rim] + [shift_in(rim, "mode", s) for s in range(1, groups)]
+    extended = jnp.concatenate([field, jnp.where(upper, high[:rows], low[:rows])], axis=1)
+    fields = [extended] + [shift_in(extended, "mode", s) for s in range(1, groups)]
 
     def pinned(*values):
         return [pltpu.with_memory_space_constraint(v, pltpu.HBM) for v in values]
 
     resid, power, node, conn, owner_row, eig_copy, weight_copy = pl.pallas_call(
         functools.partial(forces_kernel, modes, nodes, des, elems),
-        in_specs=[hbm] * 9 + [vmem] * 2,
+        in_specs=[hbm] * 8 + [vmem] * 3,
         out_specs=[vmem] * 7,
         out_shape=[
             shaped((big, elems), f32),
@@ -435,10 +425,9 @@
             pltpu.VMEM((elems,), jnp.int32),
             pltpu.VMEM((elems,), f32),
             pltpu.VMEM((tiles, DOFS, DOFS, TILE), bf16),
-            pltpu.VMEM((rows, nodes + LANES), bf16),
             pltpu.VMEM((DOFS, DOFS), bf16),
             pltpu.VMEM((EXTRA, LANES), bf16),
-            pltpu.SemaphoreType.DMA((8,)),
+            pltpu.SemaphoreType.DMA((7,)),
             pltpu.SemaphoreType.DMA((tiles,)),
             pltpu.VMEM((1, elems), f32),
             pltpu.VMEM((1, elems), f32),
@@ -459,29 +448,29 @@
             design_owner,
             mass_scale,
             stiff_deriv,
-            field,
             mass_ref,
             eig_row,
             weight_row,
             up,
         ),
+        extended,
         low,
         high,
     )
 
     gram = pl.pallas_call(
-        functools.partial(gram_kernel, modes, groups, nodes),
+        functools.partial(gram_kernel, modes, groups),
         out_shape=shaped((modes + 8, total_modes), f32),
         compiler_params=params(24),
         name="gram",
-    )(node, eig_copy, *fields, *rims)
+    )(node, eig_copy, *fields)
 
     gram = gram + lax.ppermute(gram, "dom", [(i, i ^ 1) for i in range(count)])
     grams = from_all(gram, "dom", [list(range(core, count, 2)) for core in range(2)])
 
     low_sum, own_sum, high_sum, eig_deriv = pl.pallas_call(
         functools.partial(energy_kernel, modes, groups, nodes, des, elems),
-        in_specs=[vmem] * (7 + 2 * groups),
+        in_specs=[vmem] * (7 + groups),
         out_specs=[vmem] * 4,
         out_shape=[shaped((1, des), f32)] * 3 + [shaped((1, modes), f32)],
         scratch_shapes=[
@@ -492,7 +481,7 @@
         ],
         compiler_params=params(44),
         name="energy",
-    )(grams, eig_copy, weight_copy, *fields, *rims, conn, owner_row, resid, power)
+    )(grams, eig_copy, weight_copy, *fields, conn, owner_row, resid, power)
 
     owned = own_sum + neighbour(low_sum, -1) + neighbour(high_sum, 1)
     hess_vec = jnp.sum(from_all(owned, "mode", [list(range(groups))]), axis=0)

time: 90 us -> 80.4 us (0.89)
  starting transfers between devices: 26.3 us -> 17.5 us
  blocking collectives: 25.2 us -> 23.6 us
  other arithmetic: 0.65 us -> 1.68 us
    ppermute x6 -> x3, starting transfers between devices: 10.8 us -> 5.37 us  [shift_in(): lax.ppermute(value, axis, [(i, (i - step) % count) for i in range(count)])]
    ppermute x4, waiting for transfers between devices: 3.35 us -> 7.15 us  [neighbour(): return lax.ppermute(value, 'dom', pairs)]
    ppermute x6 -> x3, waiting for transfers between devices: 3.73 us -> 0.01 us  [shift_in(): lax.ppermute(value, axis, [(i, (i - step) % count) for i in range(count)])]
    ppermute x4, starting transfers between devices: 15.3 us -> 12 us  [neighbour(): return lax.ppermute(value, 'dom', pairs)]
    all_to_all x2, blocking collectives: 25.2 us -> 23.6 us  [from_all(): return lax.all_to_all(copies, axis, 0, 0, axis_index_groups=groups)]
    concatenate x0 -> x1, other arithmetic: none -> 1.03 us  [on_device(): jnp.concatenate([field, jnp.where(upper, high[:rows], low[:rows])], axis=1)]
  transfers between devices with their start and end apart: 11 -> 8, of which waited for: 5 -> 4; matrix products, arithmetic and copies ran while one was open for 0% -> 0% of each run, Pallas kernels for 24% -> 26%
where the time goes in v5:
time: 80.4 us; the launch traced here: 80 us
  Pallas kernels  28.1 us (35%)
  blocking collectives  23.6 us (29%)
  starting transfers between devices  17.5 us (22%)
  waiting for transfers between devices  8.34 us (10%)
  other arithmetic  1.68 us (2%)
    all_to_all x2, blocking collectives, from_all(): return lax.all_to_all(copies, axis, 0, 0, axis_index_groups=groups)  23.6 us
    pallas_call x1, Pallas kernels, on_device(): pl.pallas_call(functools.partial(forces_kernel, modes, nodes, des, elems)...  21.2 us
    ppermute x4, starting transfers between devices, neighbour(): return lax.ppermute(value, 'dom', pairs)  12 us
    ppermute x4, waiting for transfers between devices, neighbour(): return lax.ppermute(value, 'dom', pairs)  7.15 us
    ppermute x3, starting transfers between devices, shift_in(): lax.ppermute(value, axis, [(i, (i - step) % count) for i in range(count)])  5.37 us
    pallas_call x1, Pallas kernels, on_device(): pl.pallas_call(functools.partial(energy_kernel, modes, groups, nodes, des...  4.55 us
  transfers between devices with their start and end apart: 8, of which 4 were waited for; matrix products, arithmetic and copies ran while one was open for 0% of the time, Pallas kernels for 26%

profile of v5, /device:TPU:8, one launch (start us, length us, event | category | flops | bytes accessed | tf_op | source)
XLA Modules:
  0.0 80.0 jit_solution(6724030715407500217)
XLA Ops:
  0.6 1.5 %pack.1 = (bf16[208,128]{1,0:T(8,128)(2,1)}, bf16[208,128]{1,0:T(8,128)(2,1)}) custom-call(bf16[192,1024]{1,0:T(8,128)(2,1)} %bitcast.6, bf16[192,1024]{1,0:T(8,128)(2,1)} %bitcast.7, f32[640]{0:T(1024)} %dir_ref.1), custom_call_target="tpu_custom_call" | custom-call | tf_op jit(solution)/shard_map/pack/pallas_call | solution.py:391
  2.1 1.9 %collective-permute-start.1 = (bf16[208,128]{1,0:T(8,128)(2,1)}, bf16[208,128]{1,0:T(8,128)(2,1)S(1)}, u32[]{:S(2)}, u32[]{:S(2)}) collective-permute-start(bf16[208,128]{1,0:T(8,128)(2,1)} %get-tuple-element.15.own_hbm), channel_id=1, source_target_pairs={{0,4},{4,8},{8,12},{12,16},{16,20},{20,24},{24,28},{28,32},{32,36}... | collective-permute-start | bytes 159752 | tf_op jit(solution)/shard_map/ppermute | solution.py:335
  4.0 5.8 %collective-permute-start = (bf16[208,128]{1,0:T(8,128)(2,1)}, bf16[208,128]{1,0:T(8,128)(2,1)S(1)}, u32[]{:S(2)}, u32[]{:S(2)}) collective-permute-start(bf16[208,128]{1,0:T(8,128)(2,1)} %get-tuple-element.16), channel_id=1, source_target_pairs={{4,0},{8,4},{12,8},{16,12},{20,16},{24,20},{28,24},{32,28},{36,32}... | collective-permute-start | bytes 159752 | tf_op jit(solution)/shard_map/ppermute | solution.py:335
  9.8 0.1 collective-permute-done.1.low_ref
  9.9 2.0 %collective-permute-done.high_ref = bf16[208,128]{1,0:T(8,128)(2,1)S(1)} collective-permute-done((bf16[208,128]{1,0:T(8,128)(2,1)}, bf16[208,128]{1,0:T(8,128)(2,1)S(1)}, u32[]{:S(2)}, u32[]{:S(2)}) %collective-permute-start) | collective-permute-done | bytes 53280 | tf_op jit(solution)/shard_map/ppermute | solution.py:335
  11.9 1.0 %pad_maximum_fusion.field.refs_0_ = bf16[192,1152]{1,0:T(8,128)(2,1)S(1)} fusion(bf16[192,128]{1,0:T(8,128)(2,1)S(1)} %slice_select_fusion, bf16[192,1024]{1,0:T(8,128)(2,1)} %bitcast.8), kind=kLoop, calls=%fused_computation | loop fusion | flops 884736 | bytes 884736 | tf_op jit(solution)/shard_map/concatenate | solution.py:405
  12.9 4.1 %collective-permute-start.2 = (bf16[192,1152]{1,0:T(8,128)(2,1)S(1)}, bf16[192,1152]{1,0:T(8,128)(2,1)S(1)}, u32[]{:S(2)}, u32[]{:S(2)}) collective-permute-start(bf16[192,1152]{1,0:T(8,128)(2,1)S(1)} %pad_maximum_fusion.field.refs_0_), channel_id=1, source_target_pairs={{0,3},{1,0},{2,1},{3,2},{4,7},{5,4},{6,5},{7,6},{8,11},{9,8},{10,9... | collective-permute-start | bytes 1327112 | tf_op jit(solution)/shard_map/ppermute | solution.py:340
  17.0 0.0 collective-permute-start.3
  17.0 1.3 %collective-permute-start.4 = (bf16[192,1152]{1,0:T(8,128)(2,1)S(1)}, bf16[192,1152]{1,0:T(8,128)(2,1)S(1)}, u32[]{:S(2)}, u32[]{:S(2)}) collective-permute-start(bf16[192,1152]{1,0:T(8,128)(2,1)S(1)} %pad_maximum_fusion.field.refs_0_), channel_id=1, source_target_pairs={{0,1},{1,2},{2,3},{3,0},{4,5},{5,6},{6,7},{7,4},{8,9},{9,10},{10,1... | collective-permute-start | bytes 1327112 | tf_op jit(solution)/shard_map/ppermute | solution.py:340
  18.3 21.2 %forces.1 = (f32[768,1536]{1,0:T(8,128)S(1)}, f32[32,1536]{1,0:T(8,128)S(1)}, f32[384,1152]{1,0:T(8,128)S(1)}, s32[4,1536]{1,0:T(4,128)S(1)}, s32[1,1536]{1,0:T(...) custom-call(s32[4,1536]{1,0:T(4,128)} %conn_hbm.1, s32[1536]{0:T(1024)} %owner_hbm.1, f32[1536]{0:T(1024)} %mass_hbm.1, ...), custom_call_target="tpu_custom_call" | custom-call | flops 1000000 | bytes 100000 | tf_op jit(solution)/shard_map/forces/pallas_call | solution.py:411
  39.5 0.0 collective-permute-done.2.refs_1_
  39.5 0.0 collective-permute-done.3.refs_2_
  39.5 0.0 collective-permute-done.4.refs_3_
  39.5 0.9 %gram.1 = f32[40,128]{1,0:T(8,128)S(1)} custom-call(f32[384,1152]{1,0:T(8,128)S(1)} %get-tuple-element.17.node_ref, f32[1,128]{1,0:T(1,128)S(1)} %get-tuple-element.18.eig_ref, bf16[192,1152]{1,0:T(8,128)(2,1)S(1)} %pad_maximum_fusion.field.refs_0_, bf16[192,1152]{1,0:T(8,128)(2,1)S(1)} %collective-permute-done.2.refs_1_, ...), custom_call_target="tpu_custom_call" | custom-call | tf_op jit(solution)/shard_map/gram/pallas_call | solution.py:461
  40.4 0.1 collective-permute-start.5
  40.5 1.2 %collective-permute-done.5 = f32[40,128]{1,0:T(8,128)S(1)} collective-permute-done((f32[40,128]{1,0:T(8,128)S(1)}, f32[40,128]{1,0:T(8,128)S(1)}, u32[]{:S(2)}, u32[]{:S(2)}) %collective-permute-start.5) | collective-permute-done | bytes 20512 | tf_op jit(solution)/shard_map/ppermute | solution.py:468
  41.7 14.6 %all_to_all.10.gram_ref = f32[16,40,128]{2,1,0:T(8,128)S(1)} all-to-all(f32[16,40,128]{2,1,0:T(8,128)S(1)} %broadcast_in_dim.6), channel_id=1, replica_groups={{0,8,16,24,32,40,48,56,64,72,80,88,96,104,112,120},{4,12,20,28,36,44,52..., dimensions={0} | all-to-all | bytes 655360 | tf_op jit(solution)/shard_map/all_to_all | solution.py:346
  56.4 4.5 %energy.1 = (f32[1,640]{1,0:T(1,128)S(1)}, f32[1,640]{1,0:T(1,128)S(1)}, f32[1,640]{1,0:T(1,128)S(1)}, f32[1,32]{1,0:T(1,128)}) custom-call(f32[16,40,128]{2,1,0:T(8,128)S(1)} %all_to_all.10.gram_ref, f32[1,128]{1,0:T(1,128)S(1)} %get-tuple-element.18.eig_ref, f32[1,32]{1,0:T(1,128)S(1)} %get-tuple-element.19.weight_ref, ...), custom_call_target="tpu_custom_call" | custom-call | tf_op jit(solution)/shard_map/energy/pallas_call | solution.py:471
  60.9 2.5 %collective-permute-start.6 = (f32[1,640]{1,0:T(1,128)S(1)}, f32[1,640]{1,0:T(1,128)S(1)}, u32[]{:S(2)}, u32[]{:S(2)}) collective-permute-start(f32[1,640]{1,0:T(1,128)S(1)} %get-tuple-element.25), channel_id=1, source_target_pairs={{4,0},{8,4},{12,8},{16,12},{20,16},{24,20},{28,24},{32,28},{36,32}... | collective-permute-start | bytes 7688 | tf_op jit(solution)/shard_map/ppermute | solution.py:335
  63.4 1.9 %collective-permute-start.7 = (f32[1,640]{1,0:T(1,128)S(1)}, f32[1,640]{1,0:T(1,128)S(1)}, u32[]{:S(2)}, u32[]{:S(2)}) collective-permute-start(f32[1,640]{1,0:T(1,128)S(1)} %get-tuple-element.26), channel_id=1, source_target_pairs={{0,4},{4,8},{8,12},{12,16},{16,20},{20,24},{24,28},{28,32},{32,36}... | collective-permute-start | bytes 7688 | tf_op jit(solution)/shard_map/ppermute | solution.py:335
  65.3 0.0 collective-permute-done.6
  65.3 5.1 %collective-permute-done.7 = f32[1,640]{1,0:T(1,128)S(1)} collective-permute-done((f32[1,640]{1,0:T(1,128)S(1)}, f32[1,640]{1,0:T(1,128)S(1)}, u32[]{:S(2)}, u32[]{:S(2)}) %collective-permute-start.7) | collective-permute-done | bytes 2592 | tf_op jit(solution)/shard_map/ppermute | solution.py:335
  70.4 8.9 %all_to_all.11 = f32[4,1,640]{2,1,0:T(1,128)S(1)} all-to-all(f32[4,1,640]{2,1,0:T(1,128)S(1)} %broadcast_in_dim.16), channel_id=1, replica_groups={{0,1,2,3},{4,5,6,7},{8,9,10,11},{12,13,14,15},{16,17,18,19},{20,21,22,2..., dimensions={0} | all-to-all | bytes 20480 | tf_op jit(solution)/shard_map/all_to_all | solution.py:346
  79.4 0.6 reduce_sum.9
  (6 shorter events, 0.1 us)
Async XLA Ops:
  2.1 7.8 %collective-permute-start.1 = (bf16[208,128]{1,0:T(8,128)(2,1)}, bf16[208,128]{1,0:T(8,128)(2,1)S(1)}, u32[]{:S(2)}, u32[]{:S(2)}) collective-permute-start(bf16[208,128]{1,0:T(8,128)(2,1)} %get-tuple-element.15.own_hbm), channel_id=1, source_target_pairs={{0,4},{4,8},{8,12},{12,16},{16,20},{20,24},{24,28},{28,32},{32,36}... | collective-permute-start | bytes 159752 | tf_op jit(solution)/shard_map/ppermute | solution.py:335
  4.0 7.8 %collective-permute-start = (bf16[208,128]{1,0:T(8,128)(2,1)}, bf16[208,128]{1,0:T(8,128)(2,1)S(1)}, u32[]{:S(2)}, u32[]{:S(2)}) collective-permute-start(bf16[208,128]{1,0:T(8,128)(2,1)} %get-tuple-element.16), channel_id=1, source_target_pairs={{4,0},{8,4},{12,8},{16,12},{20,16},{24,20},{28,24},{32,28},{36,32}... | collective-permute-start | bytes 159752 | tf_op jit(solution)/shard_map/ppermute | solution.py:335
  12.9 26.5 %collective-permute-start.2 = (bf16[192,1152]{1,0:T(8,128)(2,1)S(1)}, bf16[192,1152]{1,0:T(8,128)(2,1)S(1)}, u32[]{:S(2)}, u32[]{:S(2)}) collective-permute-start(bf16[192,1152]{1,0:T(8,128)(2,1)S(1)} %pad_maximum_fusion.field.refs_0_), channel_id=1, source_target_pairs={{0,3},{1,0},{2,1},{3,2},{4,7},{5,4},{6,5},{7,6},{8,11},{9,8},{10,9... | collective-permute-start | bytes 1327112 | tf_op jit(solution)/shard_map/ppermute | solution.py:340
  17.0 22.4 %collective-permute-start.3 = (bf16[192,1152]{1,0:T(8,128)(2,1)S(1)}, bf16[192,1152]{1,0:T(8,128)(2,1)S(1)}, u32[]{:S(2)}, u32[]{:S(2)}) collective-permute-start(bf16[192,1152]{1,0:T(8,128)(2,1)S(1)} %pad_maximum_fusion.field.refs_0_), channel_id=1, source_target_pairs={{0,2},{1,3},{2,0},{3,1},{4,6},{5,7},{6,4},{7,5},{8,10},{9,11},{10,... | collective-permute-start | bytes 1327112 | tf_op jit(solution)/shard_map/ppermute | solution.py:340
  17.0 22.4 %collective-permute-start.4 = (bf16[192,1152]{1,0:T(8,128)(2,1)S(1)}, bf16[192,1152]{1,0:T(8,128)(2,1)S(1)}, u32[]{:S(2)}, u32[]{:S(2)}) collective-permute-start(bf16[192,1152]{1,0:T(8,128)(2,1)S(1)} %pad_maximum_fusion.field.refs_0_), channel_id=1, source_target_pairs={{0,1},{1,2},{2,3},{3,0},{4,5},{5,6},{6,7},{7,4},{8,9},{9,10},{10,1... | collective-permute-start | bytes 1327112 | tf_op jit(solution)/shard_map/ppermute | solution.py:340
  40.4 1.3 %collective-permute-start.5 = (f32[40,128]{1,0:T(8,128)S(1)}, f32[40,128]{1,0:T(8,128)S(1)}, u32[]{:S(2)}, u32[]{:S(2)}) collective-permute-start(f32[40,128]{1,0:T(8,128)S(1)} %gram.1), channel_id=1, source_target_pairs={{0,4},{4,0},{8,12},{12,8},{16,20},{20,16},{24,28},{28,24},{32,36},... | collective-permute-start | bytes 61448 | tf_op jit(solution)/shard_map/ppermute | solution.py:468
  60.9 4.4 %collective-permute-start.6 = (f32[1,640]{1,0:T(1,128)S(1)}, f32[1,640]{1,0:T(1,128)S(1)}, u32[]{:S(2)}, u32[]{:S(2)}) collective-permute-start(f32[1,640]{1,0:T(1,128)S(1)} %get-tuple-element.25), channel_id=1, source_target_pairs={{4,0},{8,4},{12,8},{16,12},{20,16},{24,20},{28,24},{32,28},{36,32}... | collective-permute-start | bytes 7688 | tf_op jit(solution)/shard_map/ppermute | solution.py:335
  63.4 7.0 %collective-permute-start.7 = (f32[1,640]{1,0:T(1,128)S(1)}, f32[1,640]{1,0:T(1,128)S(1)}, u32[]{:S(2)}, u32[]{:S(2)}) collective-permute-start(f32[1,640]{1,0:T(1,128)S(1)} %get-tuple-element.26), channel_id=1, source_target_pairs={{0,4},{4,8},{8,12},{12,16},{16,20},{20,24},{24,28},{28,32},{32,36}... | collective-permute-start | bytes 7688 | tf_op jit(solution)/shard_map/ppermute | solution.py:335

commit v6 on v5

--- a/solution.py
+++ b/solution.py
@@ -145,7 +145,7 @@
     ]
 
     def stiff_copy(t):
-        cols = pl.ds(pl.multiple_of(t * TILE, TILE), TILE)
+        cols = pl.ds(t * TILE, TILE)
         return pltpu.make_async_copy(stiff_hbm.at[:, :, cols], stiff.at[t], stiff_sems.at[t])
 
     for copy in small:
@@ -174,9 +174,8 @@
     here = iota((entries, elems), 0) == local // LANES
     dir_row[...] = jnp.sum(jnp.where(here, looked, 0.0), axis=0, keepdims=True)
 
-    @pl.loop(0, tiles)
-    def _(t):
-        at = pl.multiple_of(t * TILE, TILE)
+    for t in range(tiles):
+        at = t * TILE
         elem_dir = dir_row[:, pl.ds(at, TILE)]
         elem_mass = mass_row[:, pl.ds(at, TILE)]
         fill_one_hot(conn, at, hot, nodes)
@@ -195,7 +194,7 @@
 
         for lane in range(TILE // LANES):
             cols = slice(lane * LANES, (lane + 1) * LANES)
-            at_lane = pl.multiple_of(at + lane * LANES, LANES)
+            at_lane = at + lane * LANES
             direction = elem_dir[:, cols]
             mass = elem_mass[:, cols]
             scaled = eig * mass
@@ -295,14 +294,13 @@
         deriv[span, :] = dot(combiner, gather_modes(fields, c, modes)).astype(bf16)
     totals[...] = jnp.zeros_like(totals)
 
-    @pl.loop(0, elems // TILE)
-    def _(t):
-        at = pl.multiple_of(t * TILE, TILE)
+    for t in range(elems // TILE):
+        at = t * TILE
         fill_one_hot(conn_ref, at, hot, nodes)
         moved = dot(deriv[...], hot[...])
         energies = []
         for lane in range(TILE // LANES):
-            cols = pl.ds(pl.multiple_of(at + lane * LANES, LANES), LANES)
+            cols = pl.ds(at + lane * LANES, LANES)
             total = -factor[...] * power_ref[:, cols]
             for k in range(CORNERS):
                 col = k * TILE + lane * LANES

time: 80.4 us -> 78.2 us (0.973)
  Pallas kernels: 28.1 us -> 25.3 us
  waiting for transfers between devices: 8.34 us -> 10.4 us
  blocking collectives: 23.6 us -> 22.3 us
    pallas_call x1, Pallas kernels: 21.2 us -> 18.2 us  [on_device(): pl.pallas_call(functools.partial(forces_kernel, modes, nodes, des, elems)...]
    ppermute x3, waiting for transfers between devices: 0.01 us -> 2.4 us  [shift_in(): lax.ppermute(value, axis, [(i, (i - step) % count) for i in range(count)])]
    all_to_all x2, blocking collectives: 23.6 us -> 22.3 us  [from_all(): return lax.all_to_all(copies, axis, 0, 0, axis_index_groups=groups)]
  transfers between devices with their start and end apart: 8 -> 8, of which waited for: 4 -> 5; matrix products, arithmetic and copies ran while one was open for 0% -> 0% of each run, Pallas kernels for 26% -> 23%
where the time goes in v6:
time: 78.2 us; the launch traced here: 77.9 us
  Pallas kernels  25.3 us (32%)
  blocking collectives  22.3 us (29%)
  starting transfers between devices  17.4 us (22%)
  waiting for transfers between devices  10.4 us (13%)
  other arithmetic  1.68 us (2%)
    all_to_all x2, blocking collectives, from_all(): return lax.all_to_all(copies, axis, 0, 0, axis_index_groups=groups)  22.3 us
    pallas_call x1, Pallas kernels, on_device(): pl.pallas_call(functools.partial(forces_kernel, modes, nodes, des, elems)...  18.2 us
    ppermute x4, starting transfers between devices, neighbour(): return lax.ppermute(value, 'dom', pairs)  12 us
    ppermute x4, waiting for transfers between devices, neighbour(): return lax.ppermute(value, 'dom', pairs)  6.84 us
    ppermute x3, starting transfers between devices, shift_in(): lax.ppermute(value, axis, [(i, (i - step) % count) for i in range(count)])  5.37 us
    pallas_call x1, Pallas kernels, on_device(): pl.pallas_call(functools.partial(energy_kernel, modes, groups, nodes, des...  4.7 us
    ppermute x3, waiting for transfers between devices, shift_in(): lax.ppermute(value, axis, [(i, (i - step) % count) for i in range(count)])  2.4 us
  transfers between devices with their start and end apart: 8, of which 5 were waited for; matrix products, arithmetic and copies ran while one was open for 0% of the time, Pallas kernels for 23%

profile of v6, /device:TPU:8, one launch (start us, length us, event | category | flops | bytes accessed | tf_op | source)
XLA Modules:
  0.0 77.9 jit_solution(1268647895979524449)
XLA Ops:
  0.6 1.5 %pack.1 = (bf16[208,128]{1,0:T(8,128)(2,1)}, bf16[208,128]{1,0:T(8,128)(2,1)}) custom-call(bf16[192,1024]{1,0:T(8,128)(2,1)} %bitcast.6, bf16[192,1024]{1,0:T(8,128)(2,1)} %bitcast.7, f32[640]{0:T(1024)} %dir_ref.1), custom_call_target="tpu_custom_call" | custom-call | tf_op jit(solution)/shard_map/pack/pallas_call | solution.py:389
  2.1 1.9 %collective-permute-start.1 = (bf16[208,128]{1,0:T(8,128)(2,1)}, bf16[208,128]{1,0:T(8,128)(2,1)S(1)}, u32[]{:S(2)}, u32[]{:S(2)}) collective-permute-start(bf16[208,128]{1,0:T(8,128)(2,1)} %get-tuple-element.15.own_hbm), channel_id=1, source_target_pairs={{0,4},{4,8},{8,12},{12,16},{16,20},{20,24},{24,28},{28,32},{32,36}... | collective-permute-start | bytes 159752 | tf_op jit(solution)/shard_map/ppermute | solution.py:333
  4.0 5.8 %collective-permute-start = (bf16[208,128]{1,0:T(8,128)(2,1)}, bf16[208,128]{1,0:T(8,128)(2,1)S(1)}, u32[]{:S(2)}, u32[]{:S(2)}) collective-permute-start(bf16[208,128]{1,0:T(8,128)(2,1)} %get-tuple-element.16), channel_id=1, source_target_pairs={{4,0},{8,4},{12,8},{16,12},{20,16},{24,20},{28,24},{32,28},{36,32}... | collective-permute-start | bytes 159752 | tf_op jit(solution)/shard_map/ppermute | solution.py:333
  9.8 0.1 collective-permute-done.1.low_ref
  9.9 2.0 %collective-permute-done.high_ref = bf16[208,128]{1,0:T(8,128)(2,1)S(1)} collective-permute-done((bf16[208,128]{1,0:T(8,128)(2,1)}, bf16[208,128]{1,0:T(8,128)(2,1)S(1)}, u32[]{:S(2)}, u32[]{:S(2)}) %collective-permute-start) | collective-permute-done | bytes 53280 | tf_op jit(solution)/shard_map/ppermute | solution.py:333
  11.9 1.0 %pad_maximum_fusion.field.refs_0_ = bf16[192,1152]{1,0:T(8,128)(2,1)S(1)} fusion(bf16[192,128]{1,0:T(8,128)(2,1)S(1)} %slice_select_fusion, bf16[192,1024]{1,0:T(8,128)(2,1)} %bitcast.8), kind=kLoop, calls=%fused_computation | loop fusion | flops 884736 | bytes 884736 | tf_op jit(solution)/shard_map/concatenate | solution.py:403
  12.9 4.1 %collective-permute-start.2 = (bf16[192,1152]{1,0:T(8,128)(2,1)S(1)}, bf16[192,1152]{1,0:T(8,128)(2,1)S(1)}, u32[]{:S(2)}, u32[]{:S(2)}) collective-permute-start(bf16[192,1152]{1,0:T(8,128)(2,1)S(1)} %pad_maximum_fusion.field.refs_0_), channel_id=1, source_target_pairs={{0,3},{1,0},{2,1},{3,2},{4,7},{5,4},{6,5},{7,6},{8,11},{9,8},{10,9... | collective-permute-start | bytes 1327112 | tf_op jit(solution)/shard_map/ppermute | solution.py:338
  17.0 0.0 collective-permute-start.3
  17.0 1.3 %collective-permute-start.4 = (bf16[192,1152]{1,0:T(8,128)(2,1)S(1)}, bf16[192,1152]{1,0:T(8,128)(2,1)S(1)}, u32[]{:S(2)}, u32[]{:S(2)}) collective-permute-start(bf16[192,1152]{1,0:T(8,128)(2,1)S(1)} %pad_maximum_fusion.field.refs_0_), channel_id=1, source_target_pairs={{0,1},{1,2},{2,3},{3,0},{4,5},{5,6},{6,7},{7,4},{8,9},{9,10},{10,1... | collective-permute-start | bytes 1327112 | tf_op jit(solution)/shard_map/ppermute | solution.py:338
  18.3 18.2 %forces.1 = (f32[768,1536]{1,0:T(8,128)S(1)}, f32[32,1536]{1,0:T(8,128)S(1)}, f32[384,1152]{1,0:T(8,128)S(1)}, s32[4,1536]{1,0:T(4,128)S(1)}, s32[1,1536]{1,0:T(...) custom-call(s32[4,1536]{1,0:T(4,128)} %conn_hbm.1, s32[1536]{0:T(1024)} %owner_hbm.1, f32[1536]{0:T(1024)} %mass_hbm.1, ...), custom_call_target="tpu_custom_call" | custom-call | flops 1000000 | bytes 100000 | tf_op jit(solution)/shard_map/forces/pallas_call | solution.py:409
  36.5 0.0 collective-permute-done.2.refs_1_
  36.5 0.0 collective-permute-done.3.refs_2_
  36.5 2.4 %collective-permute-done.4.refs_3_ = bf16[192,1152]{1,0:T(8,128)(2,1)S(1)} collective-permute-done((bf16[192,1152]{1,0:T(8,128)(2,1)S(1)}, bf16[192,1152]{1,0:T(8,128)(2,1)S(1)}, u32[]{:S(2)}, u32[]{:S(2)}) %collective-permute-start.4) | collective-permute-done | bytes 442400 | tf_op jit(solution)/shard_map/ppermute | solution.py:338
  38.9 0.9 %gram.1 = f32[40,128]{1,0:T(8,128)S(1)} custom-call(f32[384,1152]{1,0:T(8,128)S(1)} %get-tuple-element.17.node_ref, f32[1,128]{1,0:T(1,128)S(1)} %get-tuple-element.18.eig_ref, bf16[192,1152]{1,0:T(8,128)(2,1)S(1)} %pad_maximum_fusion.field.refs_0_, bf16[192,1152]{1,0:T(8,128)(2,1)S(1)} %collective-permute-done.2.refs_1_, ...), custom_call_target="tpu_custom_call" | custom-call | tf_op jit(solution)/shard_map/gram/pallas_call | solution.py:459
  39.9 0.1 collective-permute-start.5
  39.9 1.2 %collective-permute-done.5 = f32[40,128]{1,0:T(8,128)S(1)} collective-permute-done((f32[40,128]{1,0:T(8,128)S(1)}, f32[40,128]{1,0:T(8,128)S(1)}, u32[]{:S(2)}, u32[]{:S(2)}) %collective-permute-start.5) | collective-permute-done | bytes 20512 | tf_op jit(solution)/shard_map/ppermute | solution.py:466
  41.2 14.6 %all_to_all.10.gram_ref = f32[16,40,128]{2,1,0:T(8,128)S(1)} all-to-all(f32[16,40,128]{2,1,0:T(8,128)S(1)} %broadcast_in_dim.6), channel_id=1, replica_groups={{0,8,16,24,32,40,48,56,64,72,80,88,96,104,112,120},{4,12,20,28,36,44,52..., dimensions={0} | all-to-all | bytes 655360 | tf_op jit(solution)/shard_map/all_to_all | solution.py:344
  55.7 4.7 %energy.1 = (f32[1,640]{1,0:T(1,128)S(1)}, f32[1,640]{1,0:T(1,128)S(1)}, f32[1,640]{1,0:T(1,128)S(1)}, f32[1,32]{1,0:T(1,128)}) custom-call(f32[16,40,128]{2,1,0:T(8,128)S(1)} %all_to_all.10.gram_ref, f32[1,128]{1,0:T(1,128)S(1)} %get-tuple-element.18.eig_ref, f32[1,32]{1,0:T(1,128)S(1)} %get-tuple-element.19.weight_ref, ...), custom_call_target="tpu_custom_call" | custom-call | tf_op jit(solution)/shard_map/energy/pallas_call | solution.py:469
  60.4 2.1 %collective-permute-start.6 = (f32[1,640]{1,0:T(1,128)S(1)}, f32[1,640]{1,0:T(1,128)S(1)}, u32[]{:S(2)}, u32[]{:S(2)}) collective-permute-start(f32[1,640]{1,0:T(1,128)S(1)} %get-tuple-element.25), channel_id=1, source_target_pairs={{4,0},{8,4},{12,8},{16,12},{20,16},{24,20},{28,24},{32,28},{36,32}... | collective-permute-start | bytes 7688 | tf_op jit(solution)/shard_map/ppermute | solution.py:333
  62.5 2.2 %collective-permute-start.7 = (f32[1,640]{1,0:T(1,128)S(1)}, f32[1,640]{1,0:T(1,128)S(1)}, u32[]{:S(2)}, u32[]{:S(2)}) collective-permute-start(f32[1,640]{1,0:T(1,128)S(1)} %get-tuple-element.26), channel_id=1, source_target_pairs={{0,4},{4,8},{8,12},{12,16},{16,20},{20,24},{24,28},{28,32},{32,36}... | collective-permute-start | bytes 7688 | tf_op jit(solution)/shard_map/ppermute | solution.py:333
  64.8 0.0 collective-permute-done.6
  64.8 4.8 %collective-permute-done.7 = f32[1,640]{1,0:T(1,128)S(1)} collective-permute-done((f32[1,640]{1,0:T(1,128)S(1)}, f32[1,640]{1,0:T(1,128)S(1)}, u32[]{:S(2)}, u32[]{:S(2)}) %collective-permute-start.7) | collective-permute-done | bytes 2592 | tf_op jit(solution)/shard_map/ppermute | solution.py:333
  69.6 7.7 %all_to_all.11 = f32[4,1,640]{2,1,0:T(1,128)S(1)} all-to-all(f32[4,1,640]{2,1,0:T(1,128)S(1)} %broadcast_in_dim.16), channel_id=1, replica_groups={{0,1,2,3},{4,5,6,7},{8,9,10,11},{12,13,14,15},{16,17,18,19},{20,21,22,2..., dimensions={0} | all-to-all | bytes 20480 | tf_op jit(solution)/shard_map/all_to_all | solution.py:344
  77.3 0.6 reduce_sum.9
  (6 shorter events, 0.1 us)
Async XLA Ops:
  2.1 7.8 %collective-permute-start.1 = (bf16[208,128]{1,0:T(8,128)(2,1)}, bf16[208,128]{1,0:T(8,128)(2,1)S(1)}, u32[]{:S(2)}, u32[]{:S(2)}) collective-permute-start(bf16[208,128]{1,0:T(8,128)(2,1)} %get-tuple-element.15.own_hbm), channel_id=1, source_target_pairs={{0,4},{4,8},{8,12},{12,16},{16,20},{20,24},{24,28},{28,32},{32,36}... | collective-permute-start | bytes 159752 | tf_op jit(solution)/shard_map/ppermute | solution.py:333
  4.0 7.8 %collective-permute-start = (bf16[208,128]{1,0:T(8,128)(2,1)}, bf16[208,128]{1,0:T(8,128)(2,1)S(1)}, u32[]{:S(2)}, u32[]{:S(2)}) collective-permute-start(bf16[208,128]{1,0:T(8,128)(2,1)} %get-tuple-element.16), channel_id=1, source_target_pairs={{4,0},{8,4},{12,8},{16,12},{20,16},{24,20},{28,24},{32,28},{36,32}... | collective-permute-start | bytes 159752 | tf_op jit(solution)/shard_map/ppermute | solution.py:333
  12.9 23.6 %collective-permute-start.2 = (bf16[192,1152]{1,0:T(8,128)(2,1)S(1)}, bf16[192,1152]{1,0:T(8,128)(2,1)S(1)}, u32[]{:S(2)}, u32[]{:S(2)}) collective-permute-start(bf16[192,1152]{1,0:T(8,128)(2,1)S(1)} %pad_maximum_fusion.field.refs_0_), channel_id=1, source_target_pairs={{0,3},{1,0},{2,1},{3,2},{4,7},{5,4},{6,5},{7,6},{8,11},{9,8},{10,9... | collective-permute-start | bytes 1327112 | tf_op jit(solution)/shard_map/ppermute | solution.py:338
  17.0 19.5 %collective-permute-start.3 = (bf16[192,1152]{1,0:T(8,128)(2,1)S(1)}, bf16[192,1152]{1,0:T(8,128)(2,1)S(1)}, u32[]{:S(2)}, u32[]{:S(2)}) collective-permute-start(bf16[192,1152]{1,0:T(8,128)(2,1)S(1)} %pad_maximum_fusion.field.refs_0_), channel_id=1, source_target_pairs={{0,2},{1,3},{2,0},{3,1},{4,6},{5,7},{6,4},{7,5},{8,10},{9,11},{10,... | collective-permute-start | bytes 1327112 | tf_op jit(solution)/shard_map/ppermute | solution.py:338
  17.0 21.9 %collective-permute-start.4 = (bf16[192,1152]{1,0:T(8,128)(2,1)S(1)}, bf16[192,1152]{1,0:T(8,128)(2,1)S(1)}, u32[]{:S(2)}, u32[]{:S(2)}) collective-permute-start(bf16[192,1152]{1,0:T(8,128)(2,1)S(1)} %pad_maximum_fusion.field.refs_0_), channel_id=1, source_target_pairs={{0,1},{1,2},{2,3},{3,0},{4,5},{5,6},{6,7},{7,4},{8,9},{9,10},{10,1... | collective-permute-start | bytes 1327112 | tf_op jit(solution)/shard_map/ppermute | solution.py:338
  39.9 1.3 %collective-permute-start.5 = (f32[40,128]{1,0:T(8,128)S(1)}, f32[40,128]{1,0:T(8,128)S(1)}, u32[]{:S(2)}, u32[]{:S(2)}) collective-permute-start(f32[40,128]{1,0:T(8,128)S(1)} %gram.1), channel_id=1, source_target_pairs={{0,4},{4,0},{8,12},{12,8},{16,20},{20,16},{24,28},{28,24},{32,36},... | collective-permute-start | bytes 61448 | tf_op jit(solution)/shard_map/ppermute | solution.py:466
  60.4 4.3 %collective-permute-start.6 = (f32[1,640]{1,0:T(1,128)S(1)}, f32[1,640]{1,0:T(1,128)S(1)}, u32[]{:S(2)}, u32[]{:S(2)}) collective-permute-start(f32[1,640]{1,0:T(1,128)S(1)} %get-tuple-element.25), channel_id=1, source_target_pairs={{4,0},{8,4},{12,8},{16,12},{20,16},{24,20},{28,24},{32,28},{36,32}... | collective-permute-start | bytes 7688 | tf_op jit(solution)/shard_map/ppermute | solution.py:333
  62.5 7.0 %collective-permute-start.7 = (f32[1,640]{1,0:T(1,128)S(1)}, f32[1,640]{1,0:T(1,128)S(1)}, u32[]{:S(2)}, u32[]{:S(2)}) collective-permute-start(f32[1,640]{1,0:T(1,128)S(1)} %get-tuple-element.26), channel_id=1, source_target_pairs={{0,4},{4,8},{8,12},{12,16},{16,20},{20,24},{24,28},{28,32},{32,36}... | collective-permute-start | bytes 7688 | tf_op jit(solution)/shard_map/ppermute | solution.py:333
